TPU v7x, 512 devices: a whole 4x8x8 slice. The times are simulated.
512 devices in a mesh: owner: 128 (over z, y, core), rep: 4 (over x).
Axes of the slice: x: 4, y: 8, z: 8, core: 2. Of those that a mesh axis runs over, the one named last changes fastest.
Arguments:
- features: bfloat16 [32768, 768], P('owner'), may hold values from -6 to 6
- hidden_weight: bfloat16 [1024, 768], P('owner'), may hold values from -0.21875 to 0.21875
- class_weight: bfloat16 [153, 1024], replicated, may hold values from -210 to 210
- request_ids: int32 [65536, 4], P(('owner', 'rep')), may hold values from 0 to 255
- request_counts: int32 [65536, 2], P(('owner', 'rep')), may hold values from 1 to 2, as said below
- outer_tiles: int32 [1024, 2], P(('owner', 'rep')), may hold values from 0 to 3
- outer_masks: int32 [1024, 2, 128, 128], P(('owner', 'rep')), may hold values 0 or 1
- inner_tiles: int32 [512, 2], P(('owner', 'rep')), may hold values from 0 to 1
- inner_masks: int32 [512, 2, 128, 128], P(('owner', 'rep')), may hold values 0 or 1
- labels: int32 [65536], P(('owner', 'rep')), may hold values from 0 to 152
Outputs:
- hidden_grad: float32 [1024, 768], P('owner')
- class_grad: float32 [153, 1024], replicated
- node_grad: bfloat16 [32768, 1024], P('owner', 'rep')
Inputs may be any that keep to these rules, and one draw needn't show every extreme that they name: `request_counts`: column 0 counts live hop-one slots, column 1 live hop-two slots, each of the 2 slots of its part; the rest are padding. Some owners are requested more than others. `outer_tiles`: column block numbers may repeat within a row block; repeated tiles add. `inner_tiles`: column block numbers may repeat within a row block; repeated tiles add.
All inputs are finite; a program needn't handle non-finite values. No bound on the sum of `outer_masks` or of `inner_masks` on one device may be relied on, other than what follows from the above.
Results may differ from a plain program's by a relative error of at most 0.012.
The roundings to bfloat16 on the way count: a program that leaves them out, or rounds other values in their place, can miss the bound.
Values may be sent and summed in bfloat16 or wider, within the bound.
A program may use at most 64 MiB of HBM per device.

v0:
```python
import jax
import jax.numpy as jnp
from jax import lax
from jax.sharding import PartitionSpec as P


def tile_product(tile_weights, tile_cols, row_blocks):
    picked = row_blocks[tile_cols]
    return jnp.einsum("bkij,bkjw->biw", tile_weights, picked, preferred_element_type=jnp.float32)


def slot_validity(counts_part, slot_count):
    half_slots = slot_count // 2
    position = jnp.arange(slot_count, dtype=jnp.int32)[None, :]
    first_ok = position < counts_part[:, 0:1]
    second_ok = position - half_slots < counts_part[:, 1:2]
    return jnp.where(position < half_slots, first_ok, second_ok).astype(jnp.float32)


def on_device(
    features,
    hidden_weight,
    class_weight,
    request_ids,
    request_counts,
    outer_tiles,
    outer_masks,
    inner_tiles,
    inner_masks,
    labels,
):
    n_owner = lax.axis_size("owner")
    slot_count = request_ids.shape[1]
    half_slots = slot_count // 2
    width = features.shape[1]
    tile_rows = outer_masks.shape[2]
    hop_rows = n_owner * half_slots
    front_rows = 2 * hop_rows
    seed_count = labels.shape[0]
    hidden_width = class_weight.shape[1]
    class_count = class_weight.shape[0]
    wanted_ids = lax.all_to_all(request_ids, "owner", split_axis=0, concat_axis=0, tiled=True)
    picked = jnp.take(features, wanted_ids, axis=0)
    returned = lax.all_to_all(picked, "owner", split_axis=0, concat_axis=0, tiled=True)
    validity = slot_validity(request_counts, slot_count)
    frontier = returned.reshape(front_rows, width)
    own_rows = returned[:, :half_slots].reshape(hop_rows, width).astype(jnp.float32)
    valid_blocks = validity.reshape(front_rows // tile_rows, tile_rows)
    outer_weights = outer_masks.astype(jnp.float32) * valid_blocks[outer_tiles][:, :, None, :]
    outer_degree = jnp.sum(outer_weights, axis=(1, 3)).reshape(hop_rows, 1)
    gathered = tile_product(
        outer_weights.astype(jnp.bfloat16),
        outer_tiles,
        frontier.reshape(front_rows // tile_rows, tile_rows, width),
    )
    agg_one = ((own_rows + gathered.reshape(hop_rows, width)) / (1.0 + outer_degree)).astype(
        jnp.bfloat16
    )
    pre_act = lax.dot_general(
        agg_one,
        lax.all_gather(hidden_weight, "owner", axis=0, tiled=True),
        (((1,), (1,)), ((), ())),
        preferred_element_type=jnp.float32,
    )
    hidden = jnp.maximum(pre_act, 0.0).astype(jnp.bfloat16)
    hop_valid = validity[:, :half_slots].reshape(hop_rows // tile_rows, tile_rows)
    inner_weights = inner_masks.astype(jnp.float32) * hop_valid[inner_tiles][:, :, None, :]
    inner_degree = jnp.maximum(jnp.sum(inner_weights, axis=(1, 3)).reshape(seed_count, 1), 1.0)
    summed = tile_product(
        inner_weights.astype(jnp.bfloat16),
        inner_tiles,
        hidden.reshape(hop_rows // tile_rows, tile_rows, hidden_width),
    )
    agg_two = (summed.reshape(seed_count, hidden_width) / inner_degree).astype(jnp.bfloat16)
    logits = jnp.dot(agg_two, class_weight.T, preferred_element_type=jnp.float32)
    shifted = logits - jnp.max(logits, axis=1, keepdims=True)
    exponent = jnp.exp(shifted)
    softmax_out = exponent / jnp.sum(exponent, axis=1, keepdims=True)
    one_hot = (labels[:, None] == jnp.arange(class_count, dtype=jnp.int32)[None, :]).astype(
        jnp.float32
    )
    logit_grad = ((softmax_out - one_hot) / seed_count).astype(jnp.bfloat16)
    class_term = lax.dot_general(
        logit_grad, agg_two, (((0,), (0,)), ((), ())), preferred_element_type=jnp.float32
    )
    agg_grad = jnp.dot(logit_grad, class_weight, preferred_element_type=jnp.float32) / inner_degree
    spread = jnp.einsum(
        "bkij,biw->bkjw",
        inner_weights,
        agg_grad.reshape(seed_count // tile_rows, tile_rows, hidden_width),
        precision=lax.Precision.HIGHEST,
    )
    block_count = hop_rows // tile_rows
    selector = (
        inner_tiles.reshape(-1)[:, None] == jnp.arange(block_count, dtype=jnp.int32)[None, :]
    ).astype(jnp.float32)
    hidden_diff = jnp.einsum(
        "sn,sjw->njw",
        selector,
        spread.reshape(-1, tile_rows, hidden_width),
        precision=lax.Precision.HIGHEST,
    ).reshape(hop_rows, hidden_width)
    pre_grad = jnp.where(pre_act > 0.0, hidden_diff, 0.0).astype(jnp.bfloat16)
    arrived = lax.all_to_all(
        hidden_diff.reshape(n_owner, half_slots, hidden_width).astype(jnp.bfloat16),
        "owner",
        split_axis=0,
        concat_axis=0,
        tiled=True,
    ).astype(jnp.float32)
    targets = wanted_ids[:, :half_slots].reshape(-1)
    node_acc = (
        jnp.zeros((features.shape[0], hidden_width), jnp.float32)
        .at[targets]
        .add(arrived.reshape(-1, hidden_width))
    )
    node_grad = lax.psum_scatter(
        node_acc.astype(jnp.bfloat16), "rep", scatter_dimension=1, tiled=True
    )
    share_rows = hidden_weight.shape[0]
    hidden_term = lax.dot_general(
        pre_grad, agg_one, (((0,), (0,)), ((), ())), preferred_element_type=jnp.float32
    )
    hidden_total, class_grad = lax.psum((hidden_term, class_term), ("owner", "rep"))
    hidden_grad = lax.dynamic_slice_in_dim(
        hidden_total, lax.axis_index("owner") * share_rows, share_rows, 0
    )
    return (hidden_grad, class_grad, node_grad)


def solution(mesh):
    placed = (
        P("owner", None),
        P("owner", None),
        P(),
        P(("owner", "rep"), None),
        P(("owner", "rep"), None),
        P(("owner", "rep"), None),
        P(("owner", "rep"), None, None, None),
        P(("owner", "rep"), None),
        P(("owner", "rep"), None, None, None),
        P(("owner", "rep")),
    )
    return jax.shard_map(
        on_device,
        mesh=mesh,
        in_specs=placed,
        out_specs=(P("owner", None), P(), P("owner", "rep")),
        check_vma=False,
    )
```

profile of v0, /device:TPU:1, one launch (start us, length us, event | category | flops | bytes accessed | tf_op | source)
XLA Modules:
  0.0 442.7 jit_solution(16807419640073765535)
XLA Ops:
  7.2 0.7 all-gather.2.cloned.1.call-update
  7.9 1.4 copy.20
  9.3 18.4 %all-to-all-start = ((s32[128,1,4]{2,1,0:T(1,128)}), s32[128,1,4]{2,1,0:T(1,128)S(1)}, u32[]{:S(2)}, u32[]{:S(2)}) async-start(s32[128,1,4]{2,1,0:T(1,128)} %bitcast), calls=%async_computation | async-start | bytes 131072 | tf_op jit(solution)/shard_map/all_to_all | solution.py:42
  27.8 0.7 compare_select_fusion.3
  28.5 0.8 slice_reduce_fusion.1
  29.5 0.1 broadcast_in_dim.46
  29.9 0.1 lt.132
  30.1 0.1 lt.125
  30.2 8.9 %all-to-all-done = s32[128,1,4]{2,1,0:T(1,128)S(1)} async-done(((s32[128,1,4]{2,1,0:T(1,128)}), s32[128,1,4]{2,1,0:T(1,128)S(1)}, u32[]{:S(2)}, u32[]{:S(2)}) %all-to-all-start) | async-done | bytes 2080 | tf_op jit(solution)/shard_map/all_to_all | solution.py:42
  39.3 2.0 gather_fusion
  41.4 0.2 reshape.179
  41.6 1.4 broadcast_select_fusion
  43.0 5.8 %all-to-all-start.1 = ((bf16[128,4,768]{2,1,0:T(4,128)(2,1)}), bf16[128,4,768]{2,1,0:T(4,128)(2,1)S(1)}, u32[]{:S(2)}, u32[]{:S(2)}) async-start(bf16[128,4,768]{2,1,0:T(4,128)(2,1)} %broadcast_select_fusion), calls=%async_computation.1 | async-start | bytes 1572864 | tf_op jit(solution)/shard_map/all_to_all | solution.py:44
  48.7 0.2 all-reduce.3.cloned.1.call-start
  49.1 0.1 reshape.175
  49.2 0.6 gather_fusion.1
  49.8 0.6 gather_fusion.3
  50.5 0.1 fusion.10
  50.6 0.5 broadcast_maximum_fusion
  51.2 23.7 %all-to-all-done.1 = bf16[128,4,768]{2,1,0:T(4,128)(2,1)S(1)} async-done(((bf16[128,4,768]{2,1,0:T(4,128)(2,1)}), bf16[128,4,768]{2,1,0:T(4,128)(2,1)S(1)}, u32[]{:S(2)}, u32[]{:S(2)}) %all-to-all-start.1) | async-done | bytes 786464 | tf_op jit(solution)/shard_map/all_to_all | solution.py:44
  74.8 0.2 reshape_reshape.4
  75.0 0.6 gather_fusion.2
  75.6 0.2 slice_convert_fusion
  75.8 0.5 reshape.173
  76.4 1.2 fusion.12
  77.6 0.1 fusion.7
  77.8 30.3 %all-gather.2.cloned.1.call-done = bf16[1024,768]{1,0:T(8,128)(2,1)} async-done(((bf16[8,768]{1,0:T(8,128)(2,1)}), bf16[1024,768]{1,0:T(8,128)(2,1)}) %all-gather.2.cloned.1.call-update) | async-done | bytes 1572880 | tf_op jit(solution)/shard_map/all_gather | solution.py:61
  108.1 2.0 maximum_convert_fusion
  110.1 0.6 gather_fusion.4
  110.7 0.2 fusion.5
  111.0 0.3 fusion.33
  111.3 1.1 fusion.31
  112.4 0.3 fusion
  112.6 1.0 fusion.14
  113.7 2.6 fusion.2
  116.4 0.2 fusion.1
  116.6 2.3 fusion.34
  118.9 1.0 convert_element_type.65
  119.9 9.5 %all-to-all-start.2 = ((bf16[128,2,1024]{2,1,0:T(2,128)(2,1)}), bf16[128,2,1024]{2,1,0:T(2,128)(2,1)S(1)}, u32[]{:S(2)}, u32[]{:S(2)}) async-start(bf16[128,2,1024]{2,1,0:T(2,128)(2,1)} %convert_element_type.65), calls=%async_computation.2 | async-start | bytes 1048576 | tf_op jit(solution)/shard_map/all_to_all | solution.py:104
  129.5 0.1 reshape.170
  129.6 20.7 %all-to-all-done.2 = bf16[128,2,1024]{2,1,0:T(2,128)(2,1)S(1)} async-done(((bf16[128,2,1024]{2,1,0:T(2,128)(2,1)}), bf16[128,2,1024]{2,1,0:T(2,128)(2,1)S(1)}, u32[]{:S(2)}, u32[]{:S(2)}) %all-to-all-start.2) | async-done | bytes 524320 | tf_op jit(solution)/shard_map/all_to_all | solution.py:104
  150.3 0.1 reshape.222
  150.5 2.9 scatter_custom_fusion
  153.3 0.9 convert_element_type.66
  154.2 254.5 %all-reduce.3.cloned.1.call-done = (f32[1024,768]{1,0:T(8,128)}, f32[153,1024]{1,0:T(8,128)}) async-done(((f32[1024,768]{1,0:T(8,128)}, f32[153,1024]{1,0:T(8,128)}), (f32[1024,768]{1,0:T(8,128)}, f32[153,1024]{1,0:T(8,128)})) %all-reduce.3.cloned.1.call-update) | async-done | bytes 3772432 | tf_op jit(solution)/shard_map/psum | solution.py:124
  408.8 1.3 constant_dynamic-slice_fusion
  410.1 24.1 %reduce-scatter.2.cloned.1.call-done = bf16[256,256]{1,0:T(8,128)(2,1)} async-done(((bf16[256,1024]{1,0:T(8,128)(2,1)}), bf16[256,256]{1,0:T(8,128)(2,1)}) %reduce-scatter.2.cloned.1.call-update) | async-done | bytes 131088 | tf_op jit(solution)/shard_map/reduce_scatter | solution.py:117
  434.2 2.0 copy.34
  (52 shorter events, 1.3 us)
Async XLA Ops:
  7.2 32.1 %copy-start = (bf16[256,768]{1,0:T(8,128)(2,1)S(1)}, bf16[256,768]{1,0:T(8,128)(2,1)}, u32[]{:S(2)}) copy-start(bf16[256,768]{1,0:T(8,128)(2,1)} %param.10) | copy-start | bytes 1179652
  7.2 100.9 %all-gather.2.cloned.1.call-start = ((), (), s32[]{:S(2)}) async-start(), calls=%async_computation.4 | async-start | bytes 1585152 | tf_op jit(solution)/shard_map/all_gather | solution.py:61
  9.3 29.8 %all-to-all-start = ((s32[128,1,4]{2,1,0:T(1,128)}), s32[128,1,4]{2,1,0:T(1,128)S(1)}, u32[]{:S(2)}, u32[]{:S(2)}) async-start(s32[128,1,4]{2,1,0:T(1,128)} %bitcast), calls=%async_computation | async-start | bytes 131072 | tf_op jit(solution)/shard_map/all_to_all | solution.py:42
  39.1 2.4 copy-start.1
  41.3 8.5 %copy-start.8 = (s32[1,2]{1,0:T(1,128)S(1)}, s32[1,2]{1,0:T(1,128)}, u32[]{:S(2)}) copy-start(s32[1,2]{1,0:T(1,128)} %param.17) | copy-start | bytes 28
  41.3 9.1 %copy-start.4 = (s32[1,2,128,128]{3,2,1,0:T(8,128)S(1)}, s32[1,2,128,128]{3,2,1,0:T(8,128)}, u32[]{:S(2)}) copy-start(s32[1,2,128,128]{3,2,1,0:T(8,128)} %param.18) | copy-start | bytes 393220
  41.3 9.2 %copy-start.3 = (s32[2,2,128,128]{3,2,1,0:T(8,128)S(1)}, s32[2,2,128,128]{3,2,1,0:T(8,128)}, u32[]{:S(2)}) copy-start(s32[2,2,128,128]{3,2,1,0:T(8,128)} %param.16) | copy-start | bytes 786436
  43.0 31.9 %all-to-all-start.1 = ((bf16[128,4,768]{2,1,0:T(4,128)(2,1)}), bf16[128,4,768]{2,1,0:T(4,128)(2,1)S(1)}, u32[]{:S(2)}, u32[]{:S(2)}) async-start(bf16[128,4,768]{2,1,0:T(4,128)(2,1)} %broadcast_select_fusion), calls=%async_computation.1 | async-start | bytes 1572864 | tf_op jit(solution)/shard_map/all_to_all | solution.py:44
  48.7 360.0 %all-reduce.3.cloned.1.call-start = ((), (), s32[]{:S(2)}) async-start(), calls=%async_computation.6 | async-start | bytes 7602176 | tf_op jit(solution)/shard_map/psum | solution.py:124
  77.6 33.1 %copy-start.5 = (s32[1,2,128,128]{3,2,1,0:T(8,128)S(1)}, s32[1,2,128,128]{3,2,1,0:T(8,128)}, u32[]{:S(2)}) copy-start(s32[1,2,128,128]{3,2,1,0:T(8,128)} %param.18) | copy-start | bytes 393220
  77.6 33.1 %copy-start.10 = (f32[128]{0:T(128)S(1)}, f32[128]{0:T(128)}, u32[]{:S(2)}) copy-start(f32[128]{0:T(128)} %broadcast_maximum_fusion) | copy-start | bytes 1540
  77.8 33.2 %copy-start.6 = (bf16[153,1024]{1,0:T(8,128)(2,1)S(1)}, bf16[153,1024]{1,0:T(8,128)(2,1)}, u32[]{:S(2)}) copy-start(bf16[153,1024]{1,0:T(8,128)(2,1)} %param.12) | copy-start | bytes 940036
  77.8 33.5 %copy-start.7 = (s32[128]{0:T(128)S(1)}, s32[128]{0:T(128)}, u32[]{:S(2)}) copy-start(s32[128]{0:T(128)} %param.19) | copy-start | bytes 1540
  111.0 2.7 copy-start.9
  118.9 10.6 %copy-start.2 = (s32[128,1,4]{2,1,0:T(1,128)S(1)}, s32[128,1,4]{2,1,0:T(1,128)}, u32[]{:S(2)}) copy-start(s32[128,1,4]{2,1,0:T(1,128)} %copy-done.1) | copy-start | bytes 6148
  119.9 30.4 %all-to-all-start.2 = ((bf16[128,2,1024]{2,1,0:T(2,128)(2,1)}), bf16[128,2,1024]{2,1,0:T(2,128)(2,1)S(1)}, u32[]{:S(2)}, u32[]{:S(2)}) async-start(bf16[128,2,1024]{2,1,0:T(2,128)(2,1)} %convert_element_type.65), calls=%async_computation.2 | async-start | bytes 1048576 | tf_op jit(solution)/shard_map/all_to_all | solution.py:104
  129.4 304.8 %reduce-scatter.2.cloned.1.call-start = ((), (), s32[]{:S(2)}) async-start(), calls=%async_computation.5 | async-start | bytes 655360 | tf_op jit(solution)/shard_map/reduce_scatter | solution.py:117
Sparse Core Ops, SparseCore 0:
  11.2 96.8 all-gather.1
  119.0 289.6 all-reduce.2
  412.4 21.7 reduce-scatter.1
where the time goes:
time: 444 us; the launch traced here: 443 us
  waiting for transfers between devices  363 us (82%)
  starting transfers between devices  34 us (8%)
  between operations  14.2 us (3%)
  local copies, waits for them, and re-layouts  13.4 us (3%)
  matrix products  11 us (2%)
  other arithmetic  7.31 us (2%)
    psum x1, waiting for transfers between devices, on_device(): lax.psum((hidden_term, class_term), ('owner', 'rep'))  255 us
    all_gather x1, waiting for transfers between devices, on_device(): lax.all_gather(hidden_weight, 'owner', axis=0, tiled=True)  30.3 us
    reduce_scatter x1, waiting for transfers between devices, on_device(): lax.psum_scatter(node_acc.astype(jnp.bfloat16), 'rep', scatter_dimension=...  24.1 us
    all_to_all x1, waiting for transfers between devices, on_device(): lax.all_to_all(picked, 'owner', split_axis=0, concat_axis=0, tiled=True)  23.7 us
    all_to_all x1, waiting for transfers between devices, on_device(): lax.all_to_all(hidden_diff.reshape(n_owner, half_slots, hidden_width).ast...  20.7 us
    all_to_all x1, starting transfers between devices, on_device(): lax.all_to_all(request_ids, 'owner', split_axis=0, concat_axis=0, tiled=T...  18.4 us
    all_to_all x1, starting transfers between devices, on_device(): lax.all_to_all(hidden_diff.reshape(n_owner, half_slots, hidden_width).ast...  9.49 us
    all_to_all x1, waiting for transfers between devices, on_device(): lax.all_to_all(request_ids, 'owner', split_axis=0, concat_axis=0, tiled=T...  8.91 us
  transfers between devices with their start and end apart: 6, of which 6 were waited for; matrix products, arithmetic and copies ran while one was open for 4% of the time, Pallas kernels for 0%

commit v1 on v0

v1 whole, which is shorter than its diff:
```python
import functools

import jax
import jax.numpy as jnp
from jax import lax
from jax.experimental import pallas as pl
from jax.experimental.pallas import tpu as pltpu
from jax.sharding import PartitionSpec as P

MESH = pl.DeviceIdType.MESH
F32 = jnp.float32
BF16 = jnp.bfloat16

GRIDS = {(128, 4): (8, 8, 2, 4), (16, 2): (2, 4, 2, 2)}


def iota(shape, dim):
    return lax.broadcasted_iota(jnp.int32, shape, dim)


def quo(a, n):
    return lax.shift_right_logical(a, jnp.full_like(a, n.bit_length() - 1))


def rem(a, n):
    return lax.bitwise_and(a, jnp.full_like(a, n - 1))


def flag(cond, dtype=BF16):
    return jnp.where(cond, 1.0, 0.0).astype(F32).astype(dtype)


def dot(a, b, ca=1, cb=0):
    return lax.dot_general(a, b, (((ca,), (cb,)), ((), ())), preferred_element_type=F32)


def regroup(outer, middle, inner, transpose=False):
    n = outer * middle * inner
    o, i = iota((n, n), 0), iota((n, n), 1)
    if transpose:
        o, i = i, o
    m, rest = quo(o, outer * inner), rem(o, outer * inner)
    a, b = quo(rest, inner), rem(rest, inner)
    return flag(i == a * (middle * inner) + m * inner + b)


def kernel(
    dims,
    feat_hbm, weight_ref, cls_ref, ids_ref, counts_ref, otile_ref, omask_hbm, itile_ref, imask_hbm, labels_ref,
    hidden_out, class_out, node_out,
    feat, omask, imask,
    i1s, i1r, i2s, i2r,
    ws, wr, w_all,
    fa1s, fa1r, fa2s, fa2r, fb1s, fb1r, fb2s, fb2r,
    agg, pre,
    na1s, na1r, na2s, na2r, nb1s, nb1r, nb2s, nb2r, xs, xr,
    gmine, gs0, gr0, gs1, gr1, gs2, gr2, gs3, gr3, gs4, gr4,
    cmine, cs0, cr0, cs1, cr1, cs2, cr2, cs3, cr3, cfin, ca4, ca5, ca6,
    local_sem,
    i1_ss, i1_rs, i2_ss, i2_rs,
    w1_ss, w1_rs, w2_ss, w2_rs, w3_ss, w3_rs, w4_ss, w4_rs,
    fa1_ss, fa1_rs, fa2_ss, fa2_rs, fb1_ss, fb1_rs, fb2_ss, fb2_rs,
    na1_ss, na1_rs, na2_ss, na2_rs, nb1_ss, nb1_rs, nb2_ss, nb2_rs, x_ss, x_rs,
    g0_ss, g0_rs, g1_ss, g1_rs, g2_ss, g2_rs, g3_ss, g3_rs, g4_ss, g4_rs,
    c0_ss, c0_rs, c1_ss, c1_rs, c2_ss, c2_rs, c3_ss, c3_rs, c4_ss, c4_rs, c5_ss, c5_rs, c6_ss, c6_rs,
):
    Z, Y, C, X, cap, tile, rows, classes = dims
    Q = Y * C
    NO = Z * Q
    half = cap // 2
    hop, front = NO * half, NO * cap
    D, HID = agg.shape[1], pre.shape[1]
    DH, HH = D // 2, HID // 2
    YL = Y // X
    nb, cb, cw = cs2.shape
    CP = nb * cb
    seeds = labels_ref.shape[1]
    row_blocks, col_blocks, K = hop // tile, front // tile, otile_ref.shape[1]
    LW = i2s.shape[2]
    S8 = 8

    me_o = lax.axis_index("owner")
    x = lax.axis_index("rep")
    z = me_o // Q
    q = me_o % Q
    y = q // C
    c = q % C
    sib = C - 1 - c

    def copy(src, dst, ss, rs, zz, qq, xx):
        return pltpu.make_async_remote_copy(
            src_ref=src, dst_ref=dst, send_sem=ss, recv_sem=rs,
            device_id=(zz * Q + qq, xx), device_id_type=MESH,
        )

    def each(n, body):
        def step(i, carry):
            body(i)
            return carry
        lax.fori_loop(1, n, step, 0)

    class Exchange:
        def __init__(self, n, me, at, src, dst, ss, rs):
            self.n, self.me, self.at, self.src, self.dst, self.ss, self.rs = n, me, at, src, dst, ss, rs

        def out(self, d):
            to = (self.me + d) % self.n
            return copy(self.src(to), self.dst(self.me), self.ss.at[d], self.rs.at[self.me], *self.at(to))

        def inn(self, d):
            frm = (self.me + d) % self.n
            return copy(self.src(frm), self.dst(frm), self.ss.at[d], self.rs.at[frm], *self.at(frm))

        def start(self):
            each(self.n, lambda d: self.out(d).start())

        def recv(self):
            each(self.n, lambda d: self.inn(d).wait_recv())

        def sent(self):
            each(self.n, lambda d: self.out(d).wait_send())

    def along_z(src, dst, ss, rs):
        return Exchange(Z, z, lambda t: (t, q, x), src, dst, ss, rs)

    def along_q(src, dst, ss, rs):
        return Exchange(Q, q, lambda t: (z, t, x), src, dst, ss, rs)

    def along_y(src, dst, ss, rs):
        return Exchange(Y, y, lambda t: (z, t * C + c, x), src, dst, ss, rs)

    def along_x(src, dst, ss, rs):
        return Exchange(X, x, lambda t: (z, q, t), src, dst, ss, rs)

    def to_sibling(src, dst, ss, rs):
        return copy(src, dst, ss, rs, z, y * C + sib, x)

    loads = [
        pltpu.make_async_copy(feat_hbm, feat, local_sem.at[0]),
        pltpu.make_async_copy(omask_hbm, omask, local_sem.at[1]),
        pltpu.make_async_copy(imask_hbm, imask, local_sem.at[2]),
    ]
    for load in loads:
        load.start()

    barrier = pltpu.get_barrier_semaphore()

    def greet(zz, qq, xx):
        pl.semaphore_signal(barrier, inc=1, device_id=(zz * Q + qq, xx), device_id_type=MESH)

    each(Z, lambda d: greet((z + d) % Z, q, x))
    each(Q, lambda d: greet(z, (q + d) % Q, x))
    for core in range(C):
        each(X, lambda d: greet(z, y * C + core, (x + d) % X))

    i1s[...] = jnp.zeros_like(i1s)
    i1s[0:cap, :] = ids_ref[...].astype(F32)
    w32 = weight_ref[...].astype(F32)
    ws[...] = jnp.concatenate([w32[:, :DH], w32[:, DH:]], axis=0).astype(BF16)

    pl.semaphore_wait(barrier, (Z - 1) + (Q - 1) + C * (X - 1))

    ex_i1 = along_z(lambda t: i1s, lambda f: i1r.at[f], i1_ss, i1_rs)
    ex_i1.start()
    i1r[z] = i1s[...]

    w_core = y % C

    def w1_copy(t):
        return copy(ws, wr.at[c], w1_ss.at[t], w1_rs.at[c], z, t * C + w_core, x)

    def w1_each(act):
        def step(t, carry):
            @pl.when((y // C == x) & jnp.logical_not((t == y) & (w_core == c)))
            def _():
                act(t)
            return carry
        lax.fori_loop(0, Y, step, 0)

    w1_each(lambda t: w1_copy(t).start())
    y_mine = x * C + c

    ex_i1.recv()
    marks = flag(iota((Q, NO), 1) == z * Q + iota((Q, NO), 0))
    asked = i1r[...].reshape(Z * S8, NO).astype(BF16)
    if LW > Z * S8:
        asked = jnp.concatenate([asked] * (LW // (Z * S8)), axis=0)
    for_q = dot(marks, asked, 1, 1)
    for k in range(Q):
        i2s[k] = jnp.broadcast_to(for_q[k:k + 1, :], (8, LW))
    ex_i2 = along_q(lambda t: i2s.at[t], lambda f: i2r.at[f], i2_ss, i2_rs)
    ex_i2.start()
    i2r[q] = i2s[q]

    for c0 in range(C):
        own = (y == y_mine) & (c == c0)

        @pl.when(own)
        def _():
            wr[c0] = ws[...]

        @pl.when(jnp.logical_not(own))
        def _():
            copy(ws, wr.at[c0], w1_ss.at[0], w1_rs.at[c0], z, y_mine * C + c0, x).wait_recv()
    for hcol in range(2):
        cols = slice(hcol * DH, (hcol + 1) * DH)
        w_all[z, x, c, :, cols] = jnp.concatenate(
            [wr[c0, hcol * 8:(hcol + 1) * 8, :].astype(F32) for c0 in range(C)], axis=0
        ).astype(BF16)
    ex_w2 = along_z(lambda t: w_all.at[z, x, c], lambda f: w_all.at[f, x, c], w2_ss, w2_rs)
    ex_w2.start()

    for load in loads[:1]:
        load.wait()
    lane_q = iota((front, Q * 8), 1)

    ex_i2.recv()
    wanted = i2r[...].reshape(Q * 8, LW).astype(BF16)

    def picked(col_of, q_of):
        spread = dot(flag(iota((front, LW), 1) == col_of), wanted, 1, 1)
        ids = jnp.sum(jnp.where(lane_q == q_of * 8, spread, 0.0), axis=1, keepdims=True)
        return flag(ids == iota((front, rows), 1).astype(F32))

    r = iota((front, 1), 0)
    pick_a = picked(quo(r, cap * Q) * S8 + quo(rem(r, cap * Q), Q), rem(r, Q))
    fa1s[...] = dot(pick_a, feat[:, :DH]).astype(BF16).reshape(fa1s.shape)
    ex_fa1 = along_z(lambda t: fa1s.at[t], lambda f: fa1r.at[f], fa1_ss, fa1_rs)
    ex_fa1.start()
    fa1r[z] = fa1s[z]
    pick_b = picked(rem(r, Z) * S8 + quo(rem(r, cap * Z), Z), quo(r, cap * Z))
    fb1s[...] = dot(pick_b, feat[:, DH:]).astype(BF16).reshape(fb1s.shape)
    ex_fb1 = along_q(lambda t: fb1s.at[t], lambda f: fb1r.at[f], fb1_ss, fb1_rs)
    ex_fb1.start()
    fb1r[q] = fb1s[q]

    ex_w2.recv()
    ex_w3 = along_x(lambda t: w_all.at[:, x, c], lambda f: w_all.at[:, f, c], w3_ss, w3_rs)
    ex_w3.start()

    for load in loads[1:]:
        load.wait()
    counts = counts_ref[...].astype(F32)
    counts8 = jnp.concatenate([counts, jnp.zeros((6, NO), F32)], axis=0).astype(BF16)

    def validity(slots):
        n = NO * slots
        at = iota((NO, n), 1)
        per = dot(counts8, flag(iota((NO, n), 0) == quo(at, slots)))
        j = rem(iota((1, n), 1), slots).astype(F32)
        first = flag(j < per[0:1, :], F32)
        second = flag(j - half < per[1:2, :], F32)
        return jnp.where(j < half, first, second)

    valid = validity(cap)
    outer_rows = []
    for b in range(row_blocks):
        blocks = []
        for cbk in range(col_blocks):
            m = jnp.zeros((tile, tile), jnp.int32)
            for k in range(K):
                m = m + omask[b, k] * (otile_ref[b, k] == cbk).astype(jnp.int32)
            blocks.append(m.astype(F32) * valid[:, cbk * tile:(cbk + 1) * tile])
        outer_rows.append(jnp.concatenate(blocks, axis=1))
    outer = jnp.concatenate(outer_rows, axis=0)
    outer_scale = 1.0 + jnp.sum(outer, axis=1, keepdims=True)
    oi, oc = iota((hop, front), 0), iota((hop, front), 1)
    self_col = quo(oi, half) * cap + rem(oi, half)
    outer_self = (outer + flag(oc == self_col, F32)).astype(BF16)
    outer_a = dot(outer_self, regroup(Z, Q, cap, transpose=True)).astype(BF16)

    hop_valid = validity(half)
    blocks = []
    for cbk in range(row_blocks):
        m = jnp.zeros((tile, tile), jnp.int32)
        for k in range(K):
            m = m + imask[0, k] * (itile_ref[0, k] == cbk).astype(jnp.int32)
        blocks.append(m.astype(F32) * hop_valid[:, cbk * tile:(cbk + 1) * tile])
    inner32 = jnp.concatenate(blocks, axis=1)
    inner_degree = jnp.maximum(jnp.sum(inner32, axis=1, keepdims=True), 1.0)
    inner = inner32.astype(BF16)

    label_row = labels_ref[...]
    label_col = jnp.sum(
        jnp.where(iota((seeds, seeds), 0) == iota((seeds, seeds), 1), label_row, 0), axis=1, keepdims=True
    )
    one_hot = flag(label_col == iota((seeds, classes), 1), F32)

    ex_fa1.recv()
    move_a = regroup(Z * cap, Q, 1)
    fa2s[...] = dot(move_a, fa1r[...].reshape(front, DH)).astype(BF16).reshape(fa2s.shape)
    ex_fa2 = along_q(lambda t: fa2s.at[t], lambda f: fa2r.at[f], fa2_ss, fa2_rs)
    ex_fa2.start()
    fa2r[q] = fa2s[q]
    ex_fb1.recv()
    move_b = regroup(Q * cap, Z, 1)
    fb2s[...] = dot(move_b, fb1r[...].reshape(front, DH)).astype(BF16).reshape(fb2s.shape)
    ex_fb2 = along_z(lambda t: fb2s.at[t], lambda f: fb2r.at[f], fb2_ss, fb2_rs)
    ex_fb2.start()
    fb2r[z] = fb2s[z]

    ex_w3.recv()
    w4 = to_sibling(w_all.at[:, :, c], w_all.at[:, :, c], w4_ss, w4_rs)
    w4_in = to_sibling(w_all.at[:, :, sib], w_all.at[:, :, sib], w4_ss, w4_rs)
    w4.start()

    ex_fa2.recv()
    agg[:, :DH] = (dot(outer_a, fa2r[...].reshape(front, DH)) / outer_scale).astype(BF16)
    ex_fb2.recv()
    agg[:, DH:] = (dot(outer_self, fb2r[...].reshape(front, DH)) / outer_scale).astype(BF16)

    w4_in.wait_recv()
    pre[...] = dot(agg[...], w_all[...].reshape(HID, D), 1, 1)
    hidden = jnp.maximum(pre[...], 0.0).astype(BF16)
    agg_two = (dot(inner, hidden) / inner_degree).astype(BF16)
    logits = dot(agg_two, cls_ref[...], 1, 1)
    exponent = jnp.exp(logits - jnp.max(logits, axis=1, keepdims=True))
    softmax = exponent / jnp.sum(exponent, axis=1, keepdims=True)
    logit_grad = ((softmax - one_hot) / seeds).astype(BF16)
    agg_grad = dot(logit_grad, cls_ref[...]) / inner_degree
    high = agg_grad.astype(BF16)
    low = (agg_grad - high.astype(F32)).astype(BF16)
    hidden_diff = dot(inner, high, 0, 0) + dot(inner, low, 0, 0)

    diff16 = hidden_diff.astype(BF16)
    na1s[...] = diff16[:, :HH].reshape(na1s.shape)
    ex_na1 = along_z(lambda t: na1s.at[t], lambda f: na1r.at[f], na1_ss, na1_rs)
    ex_na1.start()
    na1r[z] = na1s[z]
    swap_a = regroup(Z, Q, half)
    nb1s[...] = dot(swap_a, diff16[:, HH:]).astype(BF16).reshape(nb1s.shape)
    ex_nb1 = along_q(lambda t: nb1s.at[t], lambda f: nb1r.at[f], nb1_ss, nb1_rs)
    ex_nb1.start()
    nb1r[q] = nb1s[q]

    pre_grad = jnp.where(pre[...] > 0.0, hidden_diff, 0.0).astype(BF16)
    theirs = pl.ds(pl.multiple_of(sib * DH, DH), DH)
    ours = pl.ds(pl.multiple_of(c * DH, DH), DH)
    gs0[...] = dot(pre_grad, agg[:, theirs], 0, 0).astype(BF16).reshape(gs0.shape)
    g0 = to_sibling(gs0, gr0, g0_ss, g0_rs)
    g0.start()
    gmine[...] = dot(pre_grad, agg[:, ours], 0, 0).reshape(gmine.shape)

    widen = flag(iota((classes, CP), 0) == iota((classes, CP), 1))
    class_rows = dot(dot(logit_grad, widen).astype(BF16), agg_two, 0, 0)
    left, right = class_rows[:, :HH], class_rows[:, HH:]
    cs0[...] = jnp.where(c == 0, right, left).astype(BF16)
    cmine[...] = jnp.where(c == 0, left, right)
    c0 = to_sibling(cs0, cr0, c0_ss, c0_rs)
    c0.start()

    g0.wait_recv()
    gmine[...] = gmine[...] + gr0[...].astype(F32)
    gs1[...] = gmine[...].astype(BF16)
    ex_g1 = along_x(lambda t: gs1.at[:, t], lambda f: gr1.at[f], g1_ss, g1_rs)
    ex_g1.start()
    gr1[x] = gs1[:, x]

    c0.wait_recv()
    cmine[...] = cmine[...] + cr0[...].astype(F32)
    for t in range(X):
        cs1[t] = cmine[:, t * cw:(t + 1) * cw].astype(BF16)
    ex_c1 = along_x(lambda t: cs1.at[t], lambda f: cr1.at[f], c1_ss, c1_rs)
    ex_c1.start()
    cr1[x] = cs1[x]

    ex_na1.recv()
    na2s[...] = dot(swap_a, na1r[...].reshape(hop, HH)).astype(BF16).reshape(na2s.shape)
    ex_na2 = along_q(lambda t: na2s.at[t], lambda f: na2r.at[f], na2_ss, na2_rs)
    ex_na2.start()
    na2r[q] = na2s[q]
    ex_nb1.recv()
    swap_b = regroup(Q, Z, half)
    nb2s[...] = dot(swap_b, nb1r[...].reshape(hop, HH)).astype(BF16).reshape(nb2s.shape)
    ex_nb2 = along_z(lambda t: nb2s.at[t], lambda f: nb2r.at[f], nb2_ss, nb2_rs)
    ex_nb2.start()
    nb2r[z] = nb2s[z]

    def total(ref, n):
        acc = ref[0].astype(F32)
        for k in range(1, n):
            acc = acc + ref[k].astype(F32)
        return acc

    ex_g1.recv()
    gs2[...] = total(gr1, X).astype(BF16)
    ex_g2 = along_z(lambda t: gs2.at[t], lambda f: gr2.at[f], g2_ss, g2_rs)
    ex_g2.start()
    gr2[z] = gs2[z]

    ex_c1.recv()
    cs2[...] = total(cr1, X).astype(BF16).reshape(cs2.shape)

    def c2_copy(to, frm):
        return copy(cs2.at[to], cr2.at[frm], c2_ss.at[to], c2_rs.at[frm], to, q, x)

    def to_blocks(act):
        def step(t, carry):
            @pl.when(t != z)
            def _():
                act(t)
            return carry
        lax.fori_loop(0, nb, step, 0)

    to_blocks(lambda t: c2_copy(t, z).start())
    summing = z < nb

    ex_c2_in = Exchange(Z, z, lambda t: (t, q, x), lambda t: cs2.at[0], lambda f: cr2.at[f], c2_ss, c2_rs)
    ex_c3 = along_y(lambda t: cs3, lambda f: cr3.at[f], c3_ss, c3_rs)

    @pl.when(summing)
    def _():
        cr2[z] = cs2[z]
        ex_c2_in.recv()
        cs3[...] = total(cr2, Z).astype(BF16)
        ex_c3.start()
        cr3[y] = cs3[...]

    ex_g2.recv()
    gs3[...] = total(gr2, Z).astype(BF16).reshape(gs3.shape)

    def g3_copy(yl, to, frm):
        return copy(gs3.at[yl], gr3.at[frm], g3_ss.at[yl], g3_rs.at[frm], z, to * C + c, x)

    for yl in range(YL):
        @pl.when(x * YL + yl != y)
        def _():
            g3_copy(yl, x * YL + yl, y).start()
    owning = y // YL == x
    ex_g3_in = Exchange(Y, y, lambda t: (z, t * C + c, x), lambda t: gs3.at[0], lambda f: gr3.at[f], g4_ss, g3_rs)

    def scatter(j_of, z_of, q_of, arrived):
        spread = dot(wanted, flag(iota((LW, hop), 0) == z_of * S8 + j_of))
        ids = jnp.sum(jnp.where(iota((Q * 8, hop), 0) == q_of * 8, spread, 0.0), axis=0, keepdims=True)
        return dot(flag(iota((rows, hop), 0).astype(F32) == ids), arrived)

    s = iota((1, hop), 1)
    ex_na2.recv()
    node_a = scatter(rem(s, half), rem(quo(s, half), Z), quo(s, half * Z), na2r[...].reshape(hop, HH)).astype(BF16)
    xw = HID // X
    for t in range(X // 2):
        xs[t] = node_a[:, t * xw:(t + 1) * xw]
    ex_nb2.recv()
    node_b = scatter(rem(s, half), quo(s, half * Q), rem(quo(s, half), Q), nb2r[...].reshape(hop, HH)).astype(BF16)
    for t in range(X // 2):
        xs[X // 2 + t] = node_b[:, t * xw:(t + 1) * xw]
    ex_x = along_x(lambda t: xs.at[t], lambda f: xr.at[f], x_ss, x_rs)
    ex_x.start()
    xr[x] = xs[x]

    def g4_copy(xx, cc):
        return copy(gs4.at[cc], gr4.at[c], g4_ss.at[xx * C + cc], g4_rs.at[c], z, y * C + cc, xx)

    def g4_each(act):
        for xx in range(X):
            for cc in range(C):
                @pl.when(owning & jnp.logical_not((x == xx) & (c == cc)))
                def _():
                    act(xx, cc)

    @pl.when(owning)
    def _():
        gr3[y] = gs3[y % YL]
        ex_g3_in.recv()
        gs4[...] = total(gr3, Y).reshape(gs4.shape)
        gr4[c] = gs4[c]

    g4_each(lambda xx, cc: g4_copy(xx, cc).start())

    ca4_copy = lambda to, frm: copy(cfin, ca4.at[frm], c4_ss.at[to], c4_rs.at[frm], to, q, x)

    @pl.when(summing)
    def _():
        ex_c3.recv()
        cfin[...] = total(cr3, Y).astype(BF16)
        each(Z, lambda d: ca4_copy((z + d) % Z, z).start())
        ca4[z] = cfin[...]

    to_blocks(lambda t: ca4_copy(t, t).wait_recv())
    ex_c5 = along_x(lambda t: ca4, lambda f: ca5.at[f], c5_ss, c5_rs)
    ex_c5.start()
    ca5[x] = ca4[...]
    ex_c5.recv()
    c6 = to_sibling(ca5, ca6, c6_ss, c6_rs)
    c6.start()

    for cc in range(C):
        @pl.when(jnp.logical_not(owning & (c == cc)))
        def _():
            copy(gs4.at[0], gr4.at[cc], g4_ss.at[0], g4_rs.at[cc], z, y * C + cc, y // YL).wait_recv()
        hidden_out[:, cc * DH:(cc + 1) * DH] = gr4[cc]

    ex_x.recv()
    node_out[...] = total(xr, X).astype(BF16)

    c6.wait_recv()
    mine5, theirs6 = ca5[...], ca6[...]
    for t in range(X):
        m, o = mine5[t].reshape(CP, cw), theirs6[t].reshape(CP, cw)
        for cc in range(C):
            class_out[:, cc * HH + t * cw:cc * HH + (t + 1) * cw] = jnp.where(c == cc, m, o)

    for ex in (ex_i1, ex_i2, ex_w2, ex_w3, ex_fa1, ex_fb1, ex_fa2, ex_fb2, ex_na1, ex_nb1, ex_na2, ex_nb2,
               ex_g1, ex_g2, ex_c1, ex_c5, ex_x):
        ex.sent()
    w1_each(lambda t: w1_copy(t).wait_send())
    for one in (w4, g0, c0, c6):
        one.wait_send()
    to_blocks(lambda t: c2_copy(t, z).wait_send())

    @pl.when(summing)
    def _():
        ex_c3.sent()
        each(Z, lambda d: ca4_copy((z + d) % Z, z).wait_send())

    for yl in range(YL):
        @pl.when(x * YL + yl != y)
        def _():
            g3_copy(yl, x * YL + yl, y).wait_send()
    g4_each(lambda xx, cc: g4_copy(xx, cc).wait_send())


def on_device(
    grid, features, hidden_weight, class_weight, request_ids, request_counts,
    outer_tiles, outer_masks, inner_tiles, inner_masks, labels,
):
    Z, Y, C, X = grid
    Q = Y * C
    NO = Z * Q
    cap = request_ids.shape[1]
    half = cap // 2
    rows, D = features.shape
    classes, HID = class_weight.shape
    tile = outer_masks.shape[2]
    hop = NO * half
    DH, HH, YL = D // 2, HID // 2, Y // X
    cb = 32 if classes > 32 else 8
    nb = -(-classes // cb)
    CP, cw = nb * cb, HID // (C * X)
    LW = max(Z * 8, 128)
    dims = (Z, Y, C, X, cap, tile, rows, classes)
    vm, dma = pltpu.VMEM, pltpu.SemaphoreType.DMA
    scratch = [
        vm(features.shape, BF16), vm(outer_masks.shape, jnp.int32), vm(inner_masks.shape, jnp.int32),
        vm((8, NO), F32), vm((Z, 8, NO), F32), vm((Q, 8, LW), F32), vm((Q, 8, LW), F32),
        vm((16, DH), BF16), vm((C, 16, DH), BF16), vm((Z, X, C, 16, D), BF16),
        vm((Z, cap * Q, DH), BF16), vm((Z, cap * Q, DH), BF16), vm((Q, cap * Z, DH), BF16), vm((Q, cap * Z, DH), BF16),
        vm((Q, cap * Z, DH), BF16), vm((Q, cap * Z, DH), BF16), vm((Z, cap * Q, DH), BF16), vm((Z, cap * Q, DH), BF16),
        vm((hop, D), BF16), vm((hop, HID), F32),
        vm((Z, Q * half, HH), BF16), vm((Z, Q * half, HH), BF16), vm((Q, Z * half, HH), BF16), vm((Q, Z * half, HH), BF16),
        vm((Q, Z * half, HH), BF16), vm((Q, Z * half, HH), BF16), vm((Z, Q * half, HH), BF16), vm((Z, Q * half, HH), BF16),
        vm((X, rows, HID // X), BF16), vm((X, rows, HID // X), BF16),
        vm((Z, X, YL * 16, DH), F32), vm((Z, X, YL * 16, DH), BF16), vm((Z, X, YL * 16, DH), BF16),
        vm((Z, X, YL * 16, DH), BF16), vm((X, Z, YL * 16, DH), BF16),
        vm((Z, YL * 16, DH), BF16), vm((Z, YL * 16, DH), BF16),
        vm((YL, 16, DH), BF16), vm((Y, 16, DH), BF16), vm((C, 8, DH), F32), vm((C, 8, DH), F32),
        vm((CP, HH), F32), vm((CP, HH), BF16), vm((CP, HH), BF16),
        vm((X, CP, cw), BF16), vm((X, CP, cw), BF16), vm((nb, cb, cw), BF16), vm((Z, cb, cw), BF16),
        vm((cb, cw), BF16), vm((Y, cb, cw), BF16), vm((cb, cw), BF16), vm((nb, cb, cw), BF16),
        vm((X, nb, cb, cw), BF16), vm((X, nb, cb, cw), BF16),
        dma((3,)),
        dma((Z,)), dma((Z,)), dma((Q,)), dma((Q,)),
        dma((Y,)), dma((C,)), dma((Z,)), dma((Z,)), dma((X,)), dma((X,)), dma, dma,
        dma((Z,)), dma((Z,)), dma((Q,)), dma((Q,)), dma((Q,)), dma((Q,)), dma((Z,)), dma((Z,)),
        dma((Z,)), dma((Z,)), dma((Q,)), dma((Q,)), dma((Q,)), dma((Q,)), dma((Z,)), dma((Z,)), dma((X,)), dma((X,)),
        dma, dma, dma((X,)), dma((X,)), dma((Z,)), dma((Z,)), dma((YL,)), dma((Y,)), dma((X * C,)), dma((C,)),
        dma, dma, dma((X,)), dma((X,)), dma((Z,)), dma((Z,)), dma((Y,)), dma((Y,)), dma((Z,)), dma((Z,)),
        dma((X,)), dma((X,)), dma, dma,
    ]
    hbm = pl.BlockSpec(memory_space=pl.ANY)
    vmem = pl.BlockSpec(memory_space=pltpu.VMEM)
    smem = pl.BlockSpec(memory_space=pltpu.SMEM)
    hidden_grad, class_grad, node_grad = pl.pallas_call(
        functools.partial(kernel, dims),
        out_shape=(
            jax.ShapeDtypeStruct(hidden_weight.shape, F32),
            jax.ShapeDtypeStruct((CP, HID), BF16),
            jax.ShapeDtypeStruct((rows, HID // X), BF16),
        ),
        in_specs=[hbm, vmem, vmem, vmem, vmem, smem, hbm, smem, hbm, vmem],
        out_specs=(vmem, vmem, vmem),
        scratch_shapes=scratch,
        compiler_params=pltpu.CompilerParams(
            collective_id=0, has_side_effects=True, vmem_limit_bytes=56 * 1024 * 1024
        ),
        cost_estimate=pl.CostEstimate(flops=2_000_000_000, bytes_accessed=3_000_000, transcendentals=20_000),
    )(
        features, hidden_weight, class_weight, request_ids.T, request_counts.T,
        outer_tiles, outer_masks, inner_tiles, inner_masks, labels.reshape(1, -1),
    )
    return hidden_grad, class_grad[:classes].astype(F32), node_grad


def solution(mesh):
    grid = GRIDS[(mesh.shape["owner"], mesh.shape["rep"])]
    placed = (
        P("owner", None),
        P("owner", None),
        P(),
        P(("owner", "rep"), None),
        P(("owner", "rep"), None),
        P(("owner", "rep"), None),
        P(("owner", "rep"), None, None, None),
        P(("owner", "rep"), None),
        P(("owner", "rep"), None, None, None),
        P(("owner", "rep")),
    )
    return jax.shard_map(
        functools.partial(on_device, grid),
        mesh=mesh,
        in_specs=placed,
        out_specs=(P("owner", None), P(), P("owner", "rep")),
        check_vma=False,
    )
```

time: 444 us -> 103 us (0.23)
  waiting for transfers between devices: 363 us -> 0 us
  Pallas kernels: 0 us -> 98.8 us
  starting transfers between devices: 34 us -> 0 us
  between operations: 14.2 us -> 0.66 us
  local copies, waits for them, and re-layouts: 13.4 us -> 1.27 us
  matrix products: 11 us -> 0 us
  other arithmetic: 7.31 us -> 1.91 us
    psum x1 -> x0, waiting for transfers between devices: 255 us -> none  [on_device(): lax.psum((hidden_term, class_term), ('owner', 'rep'))]
    pallas_call x0 -> x1, Pallas kernels: none -> 98.8 us  [on_device(): pl.pallas_call(functools.partial(kernel, dims), out_shape=(jax.ShapeDtype...]
    all_to_all x3 -> x0, waiting for transfers between devices: 53.2 us -> none  [the longest x1 23.7 us: on_device(): lax.all_to_all(picked, 'owner', split_axis=0, concat_axis=0, tiled=True)]
    all_to_all x3 -> x0, starting transfers between devices: 33.7 us -> none  [the longest x1 18.4 us: on_device(): lax.all_to_all(request_ids, 'owner', split_axis=0, concat_axis=0, tiled=T...]
    all_gather x1 -> x0, waiting for transfers between devices: 30.3 us -> none  [on_device(): lax.all_gather(hidden_weight, 'owner', axis=0, tiled=True)]
    reduce_scatter x1 -> x0, waiting for transfers between devices: 24.1 us -> none  [on_device(): lax.psum_scatter(node_acc.astype(jnp.bfloat16), 'rep', scatter_dimension=...]
    dot_general x9 -> x0, matrix products: 11 us -> none  [the longest x1 2.6 us: on_device(): jnp.einsum('sn,sjw->njw', selector, spread.reshape(-1, tile_rows, hidden_...]
    gather x6 -> x0, local copies, waits for them, and re-layouts: 4.5 us -> none  [the longest x2 2.21 us: on_device(): picked = jnp.take(features, wanted_ids, axis=0)]
  transfers between devices with their start and end apart: 6 -> 0, of which waited for: 6 -> 0; matrix products, arithmetic and copies ran while one was open for 4% -> 0% of each run, Pallas kernels for 0% -> 0%
where the time goes in v1:
time: 103 us
  Pallas kernels  98.8 us (96%)
  other arithmetic  1.91 us (2%)
  local copies, waits for them, and re-layouts  1.27 us (1%)
    pallas_call x1, Pallas kernels, on_device(): pl.pallas_call(functools.partial(kernel, dims), out_shape=(jax.ShapeDtype...  98.8 us

profile of v1, /device:TPU:1, one launch (start us, length us, event | category | flops | bytes accessed | tf_op | source)
XLA Modules:
  0.0 102.7 jit_solution(306993519702373951)
XLA Ops:
  0.6 98.8 %shard_map.121 = (f32[8,768]{1,0:T(8,128)}, bf16[160,1024]{1,0:T(8,128)(2,1)}, bf16[256,256]{1,0:T(8,128)(2,1)}) custom-call(bf16[256,768]{1,0:T(8,128)(2,1)} %feat_hbm.1, bf16[8,768]{1,0:T(8,128)(2,1)} %weight_ref.1, bf16[153,1024]{1,0:T(8,128)(2,1)} %cls_ref.1, s32[4,128]{1,0:T(4,128)} %bitcast.3, s32[2,128]{1,0:T(2,128)} %bitcast.4, s32[2,2]{1,0:T(2,128)} %otile_ref.1, ...), custom_call_target="tpu_custom_call" | custom-call | flops 2000000000 | bytes 3000000 | tf_op jit(solution)/shard_map/pallas_call | solution.py:573
  99.5 0.0 copy-start.1
  99.5 0.0 copy-start
  99.5 1.9 %slice_convert_fusion = f32[153,1024]{1,0:T(8,128)} fusion(bf16[160,1024]{1,0:T(8,128)(2,1)} %get-tuple-element.7), kind=kLoop, calls=%fused_computation | loop fusion | flops 156672 | bytes 940032 | tf_op jit(solution)/shard_map/convert_element_type | solution.py:591
  101.4 0.0 copy-done.1
  101.4 0.6 copy.15
  102.0 0.0 copy-done
  102.0 0.7 copy.16
Async XLA Ops:
  99.5 1.9 %copy-start.1 = (f32[8,768]{1,0:T(8,128)S(1)}, f32[8,768]{1,0:T(8,128)}, u32[]{:S(2)}) copy-start(f32[8,768]{1,0:T(8,128)} %get-tuple-element.12) | copy-start | bytes 73732
  99.5 2.5 %copy-start = (bf16[256,256]{1,0:T(8,128)(2,1)S(1)}, bf16[256,256]{1,0:T(8,128)(2,1)}, u32[]{:S(2)}) copy-start(bf16[256,256]{1,0:T(8,128)(2,1)} %get-tuple-element.14) | copy-start | bytes 393220

commit v2 on v1

v2 whole, which is shorter than its diff:
```python
import functools

import jax
import jax.numpy as jnp
from jax import lax
from jax.experimental import pallas as pl
from jax.experimental.pallas import tpu as pltpu
from jax.sharding import PartitionSpec as P

MESH = pl.DeviceIdType.MESH
F32 = jnp.float32
BF16 = jnp.bfloat16

GRIDS = {(128, 4): (8, 8, 2, 4), (16, 2): (2, 4, 2, 2)}


def iota(shape, dim):
    return lax.broadcasted_iota(jnp.int32, shape, dim)


def quo(a, n):
    return lax.shift_right_logical(a, jnp.full_like(a, n.bit_length() - 1))


def rem(a, n):
    return lax.bitwise_and(a, jnp.full_like(a, n - 1))


def flag(cond, dtype=BF16):
    return jnp.where(cond, 1.0, 0.0).astype(F32).astype(dtype)


def dot(a, b, ca=1, cb=0):
    return lax.dot_general(a, b, (((ca,), (cb,)), ((), ())), preferred_element_type=F32)


def regroup(outer, middle, inner, transpose=False):
    n = outer * middle * inner
    o, i = iota((n, n), 0), iota((n, n), 1)
    if transpose:
        o, i = i, o
    m, rest = quo(o, outer * inner), rem(o, outer * inner)
    a, b = quo(rest, inner), rem(rest, inner)
    return flag(i == a * (middle * inner) + m * inner + b)


def kernel(
    dims,
    feat_hbm, weight_ref, cls_hbm, ids_ref, counts_ref, otile_ref, omask_hbm, itile_ref, imask_hbm, labels_ref,
    hidden_out, class_out, node_out,
    feat, omask, imask, cls,
    i1s, i1r, i2s, i2r, wx, place_a, place_b,
    ws, wr, w_all,
    fa1s, fa1r, fa2s, fa2r, fb1s, fb1r, fb2s, fb2r, move_a, move_b, swap_a, swap_b,
    agg, agr, pre, pg, pgr,
    na1s, na1r, na2s, na2r, nb1s, nb1r, nb2s, nb2r,
    gs1, gr1, gs2, gr2, gs3, gr3, gs4, gr4,
    cmine, cs0, cr0, cs1, cr1, cs2, cr2, cs3, cr3, cfin, ca4, ca5,
    local_sem,
    i1_ss, i1_rs, i2_ss, i2_rs, wx_ss, wx_rs,
    w1_ss, w1_rs, w2_ss, w2_rs, w3_ss, w3_rs, w4_ss, w4_rs,
    fa1_ss, fa1_rs, fa2_ss, fa2_rs, fb1_ss, fb1_rs, fb2_ss, fb2_rs,
    na1_ss, na1_rs, na2_ss, na2_rs, nb1_ss, nb1_rs, nb2_ss, nb2_rs,
    ga_ss, ga_rs, g0_ss, g0_rs, g1_ss, g1_rs, g2_ss, g2_rs, g3_ss, g3_rs, g4_ss, g4_rs,
    c0_ss, c0_rs, c1_ss, c1_rs, c2_ss, c2_rs, c3_ss, c3_rs, c4_ss, c4_rs, c5_ss, c5_rs,
):
    Z, Y, C, X, cap, tile, rows, classes = dims
    Q = Y * C
    NO = Z * Q
    half = cap // 2
    hop, front = NO * half, NO * cap
    D, HID = feat.shape[1], pre.shape[1]
    DH, HH = D // 2, HID // 2
    YL = Y // X
    nb, cb, cw = cs2.shape
    CP = nb * cb
    seeds = labels_ref.shape[1]
    row_blocks, col_blocks, K = hop // tile, front // tile, otile_ref.shape[1]
    LW = i2s.shape[2]
    S8 = 8

    me_o = lax.axis_index("owner")
    x = lax.axis_index("rep")
    z = me_o // Q
    q = me_o % Q
    y = q // C
    c = q % C
    sib = C - 1 - c

    def copy(src, dst, ss, rs, zz, qq, xx):
        return pltpu.make_async_remote_copy(
            src_ref=src, dst_ref=dst, send_sem=ss, recv_sem=rs,
            device_id=(zz * Q + qq, xx), device_id_type=MESH,
        )

    def each(n, body):
        def step(i, carry):
            body(i)
            return carry
        lax.fori_loop(1, n, step, 0)

    class Exchange:
        def __init__(self, n, me, at, src, dst, bulk, ss, rs):
            self.n, self.me, self.at, self.src, self.dst, self.bulk, self.ss, self.rs = n, me, at, src, dst, bulk, ss, rs

        def start(self):
            def send(d):
                to = lax.bitwise_and(self.me + d, self.n - 1)
                copy(self.src(to), self.dst(self.me), self.ss, self.rs, *self.at(to)).start()
            each(self.n, send)

        def all(self):
            return copy(self.bulk, self.bulk, self.ss, self.rs, *self.at(lax.bitwise_and(self.me + 1, self.n - 1)))

        def recv(self):
            self.all().wait_recv()

        def sent(self):
            self.all().wait_send()

    def along_z(*rest):
        return Exchange(Z, z, lambda t: (t, q, x), *rest)

    def along_q(*rest):
        return Exchange(Q, q, lambda t: (z, t, x), *rest)

    def along_y(*rest):
        return Exchange(Y, y, lambda t: (z, t * C + c, x), *rest)

    def along_x(*rest):
        return Exchange(X, x, lambda t: (z, q, t), *rest)

    def along_xz(*rest):
        return Exchange(X * Z, x * Z + z, lambda t: (lax.bitwise_and(t, Z - 1), q, t // Z), *rest)

    def along_xc(*rest):
        return Exchange(X * C, x * C + c, lambda t: (z, y * C + lax.bitwise_and(t, C - 1), t // C), *rest)

    def blocks(ref, n):
        return ref.at[pl.ds(0, n - 1)]

    def to_sibling(src, dst, ss, rs):
        return copy(src, dst, ss, rs, z, y * C + sib, x)

    loads = [
        pltpu.make_async_copy(feat_hbm, feat, local_sem.at[0]),
        pltpu.make_async_copy(omask_hbm, omask, local_sem.at[1]),
        pltpu.make_async_copy(imask_hbm, imask, local_sem.at[2]),
        pltpu.make_async_copy(cls_hbm, cls, local_sem.at[3]),
    ]
    for load in loads:
        load.start()

    barrier = pltpu.get_barrier_semaphore()

    def greet(zz, qq, xx):
        pl.semaphore_signal(barrier, inc=1, device_id=(zz * Q + qq, xx), device_id_type=MESH)

    def greet_xz(d):
        t = lax.bitwise_and(x * Z + z + d, X * Z - 1)
        greet(lax.bitwise_and(t, Z - 1), q, t // Z)

    each(Q, lambda d: greet(z, lax.bitwise_and(q + d, Q - 1), x))
    each(X * Z, greet_xz)
    each(X, lambda d: greet(z, y * C + sib, lax.bitwise_and(x + d, X - 1)))

    i1s[...] = jnp.zeros_like(i1s)
    i1s[0:cap, :] = ids_ref[...].astype(F32)
    w32 = weight_ref[...].astype(F32)
    ws[...] = jnp.concatenate([w32[:, :DH], w32[:, DH:]], axis=0).astype(BF16)

    pl.semaphore_wait(barrier, (Q - 1) + (X * Z - 1) + (X - 1))

    ex_i1 = along_z(lambda t: i1s, lambda f: i1r.at[f], blocks(i1r, Z), i1_ss, i1_rs)
    ex_i1.start()
    i1r[z] = i1s[...]

    w_core = y % C

    def w1_copy(t):
        return copy(ws, wr.at[c], w1_ss.at[t], w1_rs.at[c], z, t * C + w_core, x)

    def w1_each(act):
        def step(t, carry):
            @pl.when((y // C == x) & jnp.logical_not((t == y) & (w_core == c)))
            def _():
                act(t)
            return carry
        lax.fori_loop(0, Y, step, 0)

    w1_each(lambda t: w1_copy(t).start())
    y_mine = x * C + c

    ex_i1.recv()
    marks = flag(iota((Q, NO), 1) == z * Q + iota((Q, NO), 0))
    asked = i1r[...].reshape(Z * S8, NO).astype(BF16)
    if LW > Z * S8:
        asked = jnp.concatenate([asked] * (LW // (Z * S8)), axis=0)
    for_q = dot(marks, asked, 1, 1)
    for k in range(Q):
        i2s[k] = jnp.broadcast_to(for_q[k:k + 1, :], (8, LW))
    ex_i2 = along_q(lambda t: i2s.at[t], lambda f: i2r.at[f], blocks(i2r, Q), i2_ss, i2_rs)
    ex_i2.start()
    i2r[q] = i2s[q]

    for c0 in range(C):
        own = (y == y_mine) & (c == c0)

        @pl.when(own)
        def _():
            wr[c0] = ws[...]

        @pl.when(jnp.logical_not(own))
        def _():
            copy(ws, wr.at[c0], w1_ss.at[0], w1_rs.at[c0], z, y_mine * C + c0, x).wait_recv()
    for hcol in range(2):
        cols = slice(hcol * DH, (hcol + 1) * DH)
        w_all[z, x, c, :, cols] = jnp.concatenate(
            [wr[c0, hcol * 8:(hcol + 1) * 8, :].astype(F32) for c0 in range(C)], axis=0
        ).astype(BF16)
    ex_w2 = along_z(
        lambda t: w_all.at[z, x, c], lambda f: w_all.at[f, x, c], w_all.at[pl.ds(0, Z - 1), x, c], w2_ss, w2_rs
    )
    ex_w2.start()

    for load in loads[:1]:
        load.wait()
    lane_q = iota((front, Q * 8), 1)

    ex_i2.recv()
    wanted = i2r[...].reshape(Q * 8, LW).astype(BF16)

    wx[x] = wanted
    ex_wx = along_x(lambda t: wx.at[x], lambda f: wx.at[f], blocks(wx, X), wx_ss, wx_rs)

    def picked(col_of, q_of):
        spread = dot(flag(iota((front, LW), 1) == col_of), wanted, 1, 1)
        ids = jnp.sum(jnp.where(lane_q == q_of * 8, spread, 0.0), axis=1, keepdims=True)
        return flag(ids == iota((front, rows), 1).astype(F32))

    r = iota((front, 1), 0)
    pick_a = picked(quo(r, cap * Q) * S8 + quo(rem(r, cap * Q), Q), rem(r, Q))
    fa1s[...] = dot(pick_a, feat[:, :DH]).astype(BF16).reshape(fa1s.shape)
    ex_fa1 = along_z(lambda t: fa1s.at[t], lambda f: fa1r.at[f], blocks(fa1r, Z), fa1_ss, fa1_rs)
    ex_fa1.start()
    fa1r[z] = fa1s[z]
    pick_b = picked(rem(r, Z) * S8 + quo(rem(r, cap * Z), Z), quo(r, cap * Z))
    fb1s[...] = dot(pick_b, feat[:, DH:]).astype(BF16).reshape(fb1s.shape)
    ex_fb1 = along_q(lambda t: fb1s.at[t], lambda f: fb1r.at[f], blocks(fb1r, Q), fb1_ss, fb1_rs)
    ex_fb1.start()
    fb1r[q] = fb1s[q]
    ex_wx.start()
    move_a[...] = regroup(Z * cap, Q, 1)
    move_b[...] = regroup(Q * cap, Z, 1)

    ex_w2.recv()
    ex_w3 = along_x(
        lambda t: w_all.at[:, x, c], lambda f: w_all.at[:, f, c], w_all.at[:, pl.ds(0, X - 1), c], w3_ss, w3_rs
    )
    ex_w3.start()

    for load in loads[1:]:
        load.wait()
    counts = counts_ref[...].astype(F32)
    counts8 = jnp.concatenate([counts, jnp.zeros((6, NO), F32)], axis=0).astype(BF16)

    def validity(slots):
        n = NO * slots
        at = iota((NO, n), 1)
        per = dot(counts8, flag(iota((NO, n), 0) == quo(at, slots)))
        j = rem(iota((1, n), 1), slots).astype(F32)
        first = flag(j < per[0:1, :], F32)
        second = flag(j - half < per[1:2, :], F32)
        return jnp.where(j < half, first, second)

    valid = validity(cap)
    outer_rows = []
    for b in range(row_blocks):
        tiles = []
        for cbk in range(col_blocks):
            m = jnp.zeros((tile, tile), jnp.int32)
            for k in range(K):
                m = m + omask[b, k] * (otile_ref[b, k] == cbk).astype(jnp.int32)
            tiles.append(m.astype(F32) * valid[:, cbk * tile:(cbk + 1) * tile])
        outer_rows.append(jnp.concatenate(tiles, axis=1))
    outer = jnp.concatenate(outer_rows, axis=0)
    outer_scale = 1.0 + jnp.sum(outer, axis=1, keepdims=True)
    oi, oc = iota((hop, front), 0), iota((hop, front), 1)
    self_col = quo(oi, half) * cap + rem(oi, half)
    outer_self = (outer + flag(oc == self_col, F32)).astype(BF16)
    outer_a = dot(outer_self, regroup(Z, Q, cap, transpose=True)).astype(BF16)

    hop_valid = validity(half)
    tiles = []
    for cbk in range(row_blocks):
        m = jnp.zeros((tile, tile), jnp.int32)
        for k in range(K):
            m = m + imask[0, k] * (itile_ref[0, k] == cbk).astype(jnp.int32)
        tiles.append(m.astype(F32) * hop_valid[:, cbk * tile:(cbk + 1) * tile])
    inner32 = jnp.concatenate(tiles, axis=1)
    inner_degree = jnp.maximum(jnp.sum(inner32, axis=1, keepdims=True), 1.0)
    inner = inner32.astype(BF16)

    label_row = labels_ref[...]
    label_col = jnp.sum(
        jnp.where(iota((seeds, seeds), 0) == iota((seeds, seeds), 1), label_row, 0), axis=1, keepdims=True
    )
    one_hot = flag(label_col == iota((seeds, classes), 1), F32)

    ex_fa1.recv()
    fa2s[...] = dot(move_a[...], fa1r[...].reshape(front, DH)).astype(BF16).reshape(fa2s.shape)
    ex_fa2 = along_q(lambda t: fa2s.at[t], lambda f: fa2r.at[f], blocks(fa2r, Q), fa2_ss, fa2_rs)
    ex_fa2.start()
    fa2r[q] = fa2s[q]
    ex_fb1.recv()
    fb2s[...] = dot(move_b[...], fb1r[...].reshape(front, DH)).astype(BF16).reshape(fb2s.shape)
    ex_fb2 = along_z(lambda t: fb2s.at[t], lambda f: fb2r.at[f], blocks(fb2r, Z), fb2_ss, fb2_rs)
    ex_fb2.start()
    fb2r[z] = fb2s[z]

    ex_w3.recv()
    w4 = to_sibling(w_all.at[:, :, c], w_all.at[:, :, c], w4_ss, w4_rs)
    w4_in = to_sibling(w_all.at[:, :, sib], w_all.at[:, :, sib], w4_ss, w4_rs)
    w4.start()

    swap_a[...] = regroup(Z, Q, half)
    swap_b[...] = regroup(Q, Z, half)
    ex_wx.recv()

    def places(x_of, j_of, z_of, q_of):
        n = X * hop
        pick = flag(iota((LW, n), 0) == z_of * S8 + j_of)
        ids = jnp.zeros((1, n), F32)
        for k in range(X):
            here = (iota((Q * 8, n), 0) == q_of * 8) & (x_of == k)
            ids = ids + jnp.sum(jnp.where(here, dot(wx[k], pick), 0.0), axis=0, keepdims=True)
        return flag(iota((rows, n), 0).astype(F32) == ids)

    s = iota((1, X * hop), 1)
    place_a[...] = places(
        rem(quo(s, half * Z), X), rem(s, half), rem(quo(s, half), Z), quo(s, half * Z * X)
    )
    place_b[...] = places(
        quo(s, half * Q * Z), rem(s, half), rem(quo(s, half * Q), Z), rem(quo(s, half), Q)
    )

    ex_fa2.recv()
    agg[0] = (dot(outer_a, fa2r[...].reshape(front, DH)) / outer_scale).astype(BF16)
    w4_in.wait_recv()
    pre[...] = dot(agg[0], w_all[:, :, :, :, :DH].reshape(HID, DH), 1, 1)
    ex_fb2.recv()
    agg[1] = (dot(outer_self, fb2r[...].reshape(front, DH)) / outer_scale).astype(BF16)
    ga = to_sibling(agg.at[sib], agr, ga_ss, ga_rs)
    ga.start()

    pre[...] = pre[...] + dot(agg[1], w_all[:, :, :, :, DH:].reshape(HID, DH), 1, 1)
    hidden = jnp.maximum(pre[...], 0.0).astype(BF16)
    agg_two = (dot(inner, hidden) / inner_degree).astype(BF16)
    logits = dot(agg_two, cls[...], 1, 1)
    exponent = jnp.exp(logits - jnp.max(logits, axis=1, keepdims=True))
    softmax = exponent / jnp.sum(exponent, axis=1, keepdims=True)
    logit_grad = ((softmax - one_hot) / seeds).astype(BF16)
    agg_grad = dot(logit_grad, cls[...]) / inner_degree
    high = agg_grad.astype(BF16)
    low = (agg_grad - high.astype(F32)).astype(BF16)
    hidden_diff = dot(inner, high, 0, 0) + dot(inner, low, 0, 0)

    pg[...] = jnp.where(pre[...] > 0.0, hidden_diff, 0.0).astype(BF16)
    g0 = to_sibling(pg, pgr, g0_ss, g0_rs)
    g0.start()

    diff16 = hidden_diff.astype(BF16)
    xw = HID // X
    xh = xw // 2
    for t in range(X):
        na1s[t * Z:(t + 1) * Z] = diff16[:, t * xw:t * xw + xh].reshape(Z, Q * half, xh)
    ex_na1 = along_xz(lambda t: na1s.at[t], lambda f: na1r.at[f], blocks(na1r, X * Z), na1_ss, na1_rs)
    ex_na1.start()
    me_xz = x * Z + z
    na1r[me_xz] = na1s[me_xz]
    second = jnp.concatenate([diff16[:, t * xw + xh:(t + 1) * xw] for t in range(X)], axis=1)
    nb1s[...] = dot(swap_a[...], second).astype(BF16).reshape(nb1s.shape)
    ex_nb1 = along_q(lambda t: nb1s.at[t], lambda f: nb1r.at[f], blocks(nb1r, Q), nb1_ss, nb1_rs)
    ex_nb1.start()
    nb1r[q] = nb1s[q]

    widen = flag(iota((classes, CP), 0) == iota((classes, CP), 1))
    class_rows = dot(dot(logit_grad, widen).astype(BF16), agg_two, 0, 0)
    left, right = class_rows[:, :HH], class_rows[:, HH:]
    cs0[...] = jnp.where(c == 0, right, left).astype(BF16)
    cmine[...] = jnp.where(c == 0, left, right)
    c0 = to_sibling(cs0, cr0, c0_ss, c0_rs)
    c0.start()

    gmine = dot(pg[...], agg[c], 0, 0)
    ga.wait_recv()
    g0.wait_recv()
    gmine = gmine + dot(pgr[...], agr[...], 0, 0)
    gs1[...] = gmine.astype(BF16).reshape(gs1.shape)
    ex_g1 = along_x(lambda t: gs1.at[:, t], lambda f: gr1.at[f], blocks(gr1, X), g1_ss, g1_rs)
    ex_g1.start()
    gr1[x] = gs1[:, x]

    c0.wait_recv()
    cmine[...] = cmine[...] + cr0[...].astype(F32)
    for t in range(X):
        cs1[t] = cmine[:, t * cw:(t + 1) * cw].astype(BF16)
    ex_c1 = along_x(lambda t: cs1.at[t], lambda f: cr1.at[f], blocks(cr1, X), c1_ss, c1_rs)
    ex_c1.start()
    cr1[x] = cs1[x]

    ex_na1.recv()
    came = jnp.concatenate([na1r[t * Z:(t + 1) * Z].reshape(hop, xh) for t in range(X)], axis=1)
    came = dot(swap_a[...], came).astype(BF16)
    for t in range(X):
        na2s[:, t] = came[:, t * xh:(t + 1) * xh].reshape(Q, Z * half, xh)
    ex_na2 = along_q(lambda t: na2s.at[t], lambda f: na2r.at[f], blocks(na2r, Q), na2_ss, na2_rs)
    ex_na2.start()
    na2r[q] = na2s[q]
    ex_nb1.recv()
    came = dot(swap_b[...], nb1r[...].reshape(hop, X * xh)).astype(BF16)
    for t in range(X):
        nb2s[t * Z:(t + 1) * Z] = came[:, t * xh:(t + 1) * xh].reshape(Z, Q * half, xh)
    ex_nb2 = along_xz(lambda t: nb2s.at[t], lambda f: nb2r.at[f], blocks(nb2r, X * Z), nb2_ss, nb2_rs)
    ex_nb2.start()
    nb2r[me_xz] = nb2s[me_xz]

    def total(ref, n):
        acc = ref[0].astype(F32)
        for k in range(1, n):
            acc = acc + ref[k].astype(F32)
        return acc

    ex_g1.recv()
    gs2[...] = total(gr1, X).astype(BF16)
    ex_g2 = along_z(lambda t: gs2.at[t], lambda f: gr2.at[f], blocks(gr2, Z), g2_ss, g2_rs)
    ex_g2.start()
    gr2[z] = gs2[z]

    ex_c1.recv()
    cs2[...] = total(cr1, X).astype(BF16).reshape(cs2.shape)

    def to_blocks(act):
        def step(t, carry):
            @pl.when(t != z)
            def _():
                act(t)
            return carry
        lax.fori_loop(0, nb, step, 0)

    to_blocks(lambda t: copy(cs2.at[t], cr2.at[z], c2_ss, c2_rs, t, q, x).start())
    summing = z < nb

    ex_c2 = along_z(None, None, blocks(cr2, Z), c2_ss, c2_rs)
    ex_c3 = along_y(lambda t: cs3, lambda f: cr3.at[f], blocks(cr3, Y), c3_ss, c3_rs)
    ex_c4 = along_z(lambda t: cfin, lambda f: ca4.at[f], blocks(cr2, Z), c4_ss, c4_rs)

    @pl.when(summing)
    def _():
        cr2[z] = cs2[z]
        ex_c2.recv()
        cs3[...] = total(cr2, Z).astype(BF16)
        ex_c3.start()
        cr3[y] = cs3[...]

    ex_g2.recv()
    gs3[...] = total(gr2, Z).astype(BF16).reshape(gs3.shape)

    def g3_copy(yl):
        return copy(gs3.at[yl], gr3.at[y], g3_ss.at[yl], g3_rs, z, (x * YL + yl) * C + c, x)

    for yl in range(YL):
        @pl.when(x * YL + yl != y)
        def _():
            g3_copy(yl).start()
    owning = y // YL == x

    @pl.when(summing)
    def _():
        ex_c3.recv()
        cfin[...] = total(cr3, Y).astype(BF16)
        ex_c4.start()
        ca4[z] = cfin[...]

    ex_na2.recv()
    node_out[:, :xh] = dot(place_a[...], na2r[...].reshape(X * hop, xh)).astype(BF16)
    ex_nb2.recv()
    node_out[:, xh:] = dot(place_b[...], nb2r[...].reshape(X * hop, xh)).astype(BF16)

    def g4_copy(xx, cc):
        return copy(gs4.at[cc], gr4.at[c], g4_ss.at[xx * C + cc], g4_rs.at[c], z, y * C + cc, xx)

    def g4_each(act):
        for xx in range(X):
            for cc in range(C):
                @pl.when(owning & jnp.logical_not((x == xx) & (c == cc)))
                def _():
                    act(xx, cc)

    @pl.when(owning)
    def _():
        gr3[y] = gs3[y % YL]
        copy(blocks(gr3, Y), blocks(gr3, Y), g3_ss.at[0], g3_rs, z, q, x).wait_recv()
        gs4[...] = total(gr3, Y).reshape(gs4.shape)
        gr4[c] = gs4[c]

    g4_each(lambda xx, cc: g4_copy(xx, cc).start())

    @pl.when(summing)
    def _():
        some = ca4.at[pl.ds(0, nb - 1)]
        copy(some, some, c4_ss, c4_rs, z, q, x).wait_recv()

    @pl.when(jnp.logical_not(summing))
    def _():
        copy(ca4, ca4, c4_ss, c4_rs, z, q, x).wait_recv()

    me_xc = x * C + c
    ex_c5 = along_xc(lambda t: ca4, lambda f: ca5.at[f], blocks(ca5, X * C), c5_ss, c5_rs)
    ex_c5.start()
    ca5[me_xc] = ca4[...]

    for cc in range(C):
        @pl.when(jnp.logical_not(owning & (c == cc)))
        def _():
            copy(gs4.at[0], gr4.at[cc], g4_ss.at[0], g4_rs.at[cc], z, y * C + cc, y // YL).wait_recv()
        hidden_out[:, cc * DH:(cc + 1) * DH] = gr4[cc]

    ex_c5.recv()
    for t in range(X):
        for cc in range(C):
            class_out[:, cc * HH + t * cw:cc * HH + (t + 1) * cw] = ca5[t * C + cc].reshape(CP, cw)

    for ex in (ex_i1, ex_i2, ex_wx, ex_w2, ex_w3, ex_fa1, ex_fb1, ex_fa2, ex_fb2, ex_na1, ex_nb1, ex_na2, ex_nb2,
               ex_g1, ex_g2, ex_c1, ex_c5):
        ex.sent()
    w1_each(lambda t: w1_copy(t).wait_send())
    for one in (w4, ga, g0, c0):
        one.wait_send()

    @pl.when(summing)
    def _():
        some = cs2.at[pl.ds(0, nb - 1)]
        copy(some, some, c2_ss, c2_rs, z, q, x).wait_send()
        ex_c3.sent()
        ex_c4.sent()

    @pl.when(jnp.logical_not(summing))
    def _():
        copy(cs2, cs2, c2_ss, c2_rs, z, q, x).wait_send()

    for yl in range(YL):
        @pl.when(x * YL + yl != y)
        def _():
            g3_copy(yl).wait_send()
    g4_each(lambda xx, cc: g4_copy(xx, cc).wait_send())


def on_device(
    grid, features, hidden_weight, class_weight, request_ids, request_counts,
    outer_tiles, outer_masks, inner_tiles, inner_masks, labels,
):
    Z, Y, C, X = grid
    Q = Y * C
    NO = Z * Q
    cap = request_ids.shape[1]
    half = cap // 2
    rows, D = features.shape
    classes, HID = class_weight.shape
    tile = outer_masks.shape[2]
    hop = NO * half
    DH, HH, YL = D // 2, HID // 2, Y // X
    cb = 32 if classes > 32 else 8
    nb = -(-classes // cb)
    CP, cw = nb * cb, HID // (C * X)
    LW = max(Z * 8, 128)
    dims = (Z, Y, C, X, cap, tile, rows, classes)
    vm, dma = pltpu.VMEM, pltpu.SemaphoreType.DMA
    xh = HID // X // 2
    scratch = [
        vm(features.shape, BF16), vm(outer_masks.shape, jnp.int32), vm(inner_masks.shape, jnp.int32),
        vm(class_weight.shape, BF16),
        vm((8, NO), F32), vm((Z, 8, NO), F32), vm((Q, 8, LW), F32), vm((Q, 8, LW), F32),
        vm((X, Q * 8, LW), BF16), vm((rows, X * hop), BF16), vm((rows, X * hop), BF16),
        vm((16, DH), BF16), vm((C, 16, DH), BF16), vm((Z, X, C, 16, D), BF16),
        vm((Z, cap * Q, DH), BF16), vm((Z, cap * Q, DH), BF16), vm((Q, cap * Z, DH), BF16), vm((Q, cap * Z, DH), BF16),
        vm((Q, cap * Z, DH), BF16), vm((Q, cap * Z, DH), BF16), vm((Z, cap * Q, DH), BF16), vm((Z, cap * Q, DH), BF16),
        vm((cap * NO, cap * NO), BF16), vm((cap * NO, cap * NO), BF16), vm((hop, hop), BF16), vm((hop, hop), BF16),
        vm((2, hop, DH), BF16), vm((hop, DH), BF16), vm((hop, HID), F32), vm((hop, HID), BF16), vm((hop, HID), BF16),
        vm((X * Z, Q * half, xh), BF16), vm((X * Z, Q * half, xh), BF16),
        vm((Q, X, Z * half, xh), BF16), vm((Q, X, Z * half, xh), BF16),
        vm((Q, Z * half, HH), BF16), vm((Q, Z * half, HH), BF16),
        vm((X * Z, Q * half, xh), BF16), vm((X * Z, Q * half, xh), BF16),
        vm((Z, X, YL * 16, DH), BF16), vm((X, Z, YL * 16, DH), BF16),
        vm((Z, YL * 16, DH), BF16), vm((Z, YL * 16, DH), BF16),
        vm((YL, 16, DH), BF16), vm((Y, 16, DH), BF16), vm((C, 8, DH), F32), vm((C, 8, DH), F32),
        vm((CP, HH), F32), vm((CP, HH), BF16), vm((CP, HH), BF16),
        vm((X, CP, cw), BF16), vm((X, CP, cw), BF16), vm((nb, cb, cw), BF16), vm((Z, cb, cw), BF16),
        vm((cb, cw), BF16), vm((Y, cb, cw), BF16), vm((cb, cw), BF16), vm((nb, cb, cw), BF16),
        vm((X * C, nb, cb, cw), BF16),
        dma((4,)),
        *[dma] * 6,
        dma((Y,)), dma((C,)), *[dma] * 6,
        *[dma] * 16,
        *[dma] * 8, dma((YL,)), dma, dma((X * C,)), dma((C,)),
        *[dma] * 12,
    ]
    hbm = pl.BlockSpec(memory_space=pl.ANY)
    vmem = pl.BlockSpec(memory_space=pltpu.VMEM)
    smem = pl.BlockSpec(memory_space=pltpu.SMEM)
    hidden_grad, class_grad, node_grad = pl.pallas_call(
        functools.partial(kernel, dims),
        out_shape=(
            jax.ShapeDtypeStruct(hidden_weight.shape, F32),
            jax.ShapeDtypeStruct((CP, HID), BF16),
            jax.ShapeDtypeStruct((rows, HID // X), BF16),
        ),
        in_specs=[hbm, vmem, hbm, vmem, vmem, smem, hbm, smem, hbm, vmem],
        out_specs=(vmem, vmem, vmem),
        scratch_shapes=scratch,
        compiler_params=pltpu.CompilerParams(
            collective_id=0, has_side_effects=True, vmem_limit_bytes=56 * 1024 * 1024
        ),
        cost_estimate=pl.CostEstimate(flops=2_000_000_000, bytes_accessed=3_000_000, transcendentals=20_000),
    )(
        features, hidden_weight, class_weight, request_ids.T, request_counts.T,
        outer_tiles, outer_masks, inner_tiles, inner_masks, labels.reshape(1, -1),
    )
    return hidden_grad, class_grad[:classes].astype(F32), node_grad


def solution(mesh):
    grid = GRIDS[(mesh.shape["owner"], mesh.shape["rep"])]
    placed = (
        P("owner", None),
        P("owner", None),
        P(),
        P(("owner", "rep"), None),
        P(("owner", "rep"), None),
        P(("owner", "rep"), None),
        P(("owner", "rep"), None, None, None),
        P(("owner", "rep"), None),
        P(("owner", "rep"), None, None, None),
        P(("owner", "rep")),
    )
    return jax.shard_map(
        functools.partial(on_device, grid),
        mesh=mesh,
        in_specs=placed,
        out_specs=(P("owner", None), P(), P("owner", "rep")),
        check_vma=False,
    )
```

time: 103 us -> 99.7 us (0.968)
  Pallas kernels: 98.8 us -> 95.7 us
    pallas_call x1, Pallas kernels: 98.8 us -> 95.7 us  [on_device(): pl.pallas_call(functools.partial(kernel, dims), out_shape=(jax.ShapeDtype...]
where the time goes in v2:
time: 99.7 us; the launch traced here: 99.5 us
  Pallas kernels  95.7 us (96%)
  other arithmetic  1.91 us (2%)
  local copies, waits for them, and re-layouts  1.27 us (1%)
    pallas_call x1, Pallas kernels, on_device(): pl.pallas_call(functools.partial(kernel, dims), out_shape=(jax.ShapeDtype...  95.7 us

profile of v2, /device:TPU:1, one launch (start us, length us, event | category | flops | bytes accessed | tf_op | source)
XLA Modules:
  0.0 99.5 jit_solution(10337429241676037401)
XLA Ops:
  0.6 95.7 %shard_map.121 = (f32[8,768]{1,0:T(8,128)}, bf16[160,1024]{1,0:T(8,128)(2,1)}, bf16[256,256]{1,0:T(8,128)(2,1)}) custom-call(bf16[256,768]{1,0:T(8,128)(2,1)} %feat_hbm.1, bf16[8,768]{1,0:T(8,128)(2,1)} %weight_ref.1, bf16[153,1024]{1,0:T(8,128)(2,1)} %cls_hbm.1, s32[4,128]{1,0:T(4,128)} %bitcast.3, s32[2,128]{1,0:T(2,128)} %bitcast.4, s32[2,2]{1,0:T(2,128)} %otile_ref.1, ...), custom_call_target="tpu_custom_call" | custom-call | flops 2000000000 | bytes 3000000 | tf_op jit(solution)/shard_map/pallas_call | solution.py:611
  96.3 0.0 copy-start.1
  96.3 0.0 copy-start
  96.3 1.9 %slice_convert_fusion = f32[153,1024]{1,0:T(8,128)} fusion(bf16[160,1024]{1,0:T(8,128)(2,1)} %get-tuple-element.7), kind=kLoop, calls=%fused_computation | loop fusion | flops 156672 | bytes 940032 | tf_op jit(solution)/shard_map/convert_element_type | solution.py:629
  98.2 0.0 copy-done.1
  98.2 0.6 copy.15
  98.8 0.0 copy-done
  98.8 0.7 copy.16
Async XLA Ops:
  96.3 1.9 %copy-start.1 = (f32[8,768]{1,0:T(8,128)S(1)}, f32[8,768]{1,0:T(8,128)}, u32[]{:S(2)}) copy-start(f32[8,768]{1,0:T(8,128)} %get-tuple-element.12) | copy-start | bytes 73732
  96.3 2.5 %copy-start = (bf16[256,256]{1,0:T(8,128)(2,1)S(1)}, bf16[256,256]{1,0:T(8,128)(2,1)}, u32[]{:S(2)}) copy-start(bf16[256,256]{1,0:T(8,128)(2,1)} %get-tuple-element.14) | copy-start | bytes 393220

commit v3 on v2

--- a/solution.py
+++ b/solution.py
@@ -11,7 +11,7 @@
 F32 = jnp.float32
 BF16 = jnp.bfloat16
 
-GRIDS = {(128, 4): (8, 8, 2, 4), (16, 2): (2, 4, 2, 2)}
+GRIDS = {(128, 4): (8, 8, 2, 4), (32, 4): (2, 8, 2, 4)}
 
 
 def iota(shape, dim):
@@ -54,15 +54,15 @@
     fa1s, fa1r, fa2s, fa2r, fb1s, fb1r, fb2s, fb2r, move_a, move_b, swap_a, swap_b,
     agg, agr, pre, pg, pgr,
     na1s, na1r, na2s, na2r, nb1s, nb1r, nb2s, nb2r,
-    gs1, gr1, gs2, gr2, gs3, gr3, gs4, gr4,
-    cmine, cs0, cr0, cs1, cr1, cs2, cr2, cs3, cr3, cfin, ca4, ca5,
+    gs1, gra, grb, gsa, gsb, grl, grr, gs2, gr2, gs3, gr3, gs4, gr4,
+    cs1, cr1, cs2, cr2, cs3, cr3, cfin, ca4, ca5,
     local_sem,
     i1_ss, i1_rs, i2_ss, i2_rs, wx_ss, wx_rs,
     w1_ss, w1_rs, w2_ss, w2_rs, w3_ss, w3_rs, w4_ss, w4_rs,
     fa1_ss, fa1_rs, fa2_ss, fa2_rs, fb1_ss, fb1_rs, fb2_ss, fb2_rs,
     na1_ss, na1_rs, na2_ss, na2_rs, nb1_ss, nb1_rs, nb2_ss, nb2_rs,
     ga_ss, ga_rs, g0_ss, g0_rs, g1_ss, g1_rs, g2_ss, g2_rs, g3_ss, g3_rs, g4_ss, g4_rs,
-    c0_ss, c0_rs, c1_ss, c1_rs, c2_ss, c2_rs, c3_ss, c3_rs, c4_ss, c4_rs, c5_ss, c5_rs,
+    c1_ss, c1_rs, c2_ss, c2_rs, c3_ss, c3_rs, c4_ss, c4_rs, c5_ss, c5_rs,
 ):
     Z, Y, C, X, cap, tile, rows, classes = dims
     Q = Y * C
@@ -238,17 +238,35 @@
         ids = jnp.sum(jnp.where(lane_q == q_of * 8, spread, 0.0), axis=1, keepdims=True)
         return flag(ids == iota((front, rows), 1).astype(F32))
 
+    chunks, wide = fa1s.shape[0], fa1s.shape[3]
     r = iota((front, 1), 0)
     pick_a = picked(quo(r, cap * Q) * S8 + quo(rem(r, cap * Q), Q), rem(r, Q))
-    fa1s[...] = dot(pick_a, feat[:, :DH]).astype(BF16).reshape(fa1s.shape)
-    ex_fa1 = along_z(lambda t: fa1s.at[t], lambda f: fa1r.at[f], blocks(fa1r, Z), fa1_ss, fa1_rs)
-    ex_fa1.start()
-    fa1r[z] = fa1s[z]
+    rows_a = dot(pick_a, feat[:, :DH]).astype(BF16)
+    ex_fa1, ex_fb1, ex_fa2, ex_fb2 = [], [], [], []
+    for k in range(chunks):
+        at = slice(k * wide, (k + 1) * wide)
+        fa1s[k] = rows_a[:, at].reshape(fa1s.shape[1:])
+        ex_fa1.append(along_z(
+            lambda t, k=k: fa1s.at[k, t], lambda f, k=k: fa1r.at[k, f], blocks(fa1r.at[k], Z), fa1_ss.at[k], fa1_rs.at[k]))
+        ex_fb1.append(along_q(
+            lambda t, k=k: fb1s.at[k, t], lambda f, k=k: fb1r.at[k, f], blocks(fb1r.at[k], Q), fb1_ss.at[k], fb1_rs.at[k]))
+        ex_fa2.append(along_q(
+            lambda t, k=k: fa2s.at[k, t], lambda f, k=k: fa2r.at[k, f], blocks(fa2r.at[k], Q), fa2_ss.at[k], fa2_rs.at[k]))
+        ex_fb2.append(along_z(
+            lambda t, k=k: fb2s.at[k, t], lambda f, k=k: fb2r.at[k, f], blocks(fb2r.at[k], Z), fb2_ss.at[k], fb2_rs.at[k]))
+    ex_fa1[0].start()
     pick_b = picked(rem(r, Z) * S8 + quo(rem(r, cap * Z), Z), quo(r, cap * Z))
-    fb1s[...] = dot(pick_b, feat[:, DH:]).astype(BF16).reshape(fb1s.shape)
-    ex_fb1 = along_q(lambda t: fb1s.at[t], lambda f: fb1r.at[f], blocks(fb1r, Q), fb1_ss, fb1_rs)
-    ex_fb1.start()
-    fb1r[q] = fb1s[q]
+    rows_b = dot(pick_b, feat[:, DH:]).astype(BF16)
+    for k in range(chunks):
+        at = slice(k * wide, (k + 1) * wide)
+        fb1s[k] = rows_b[:, at].reshape(fb1s.shape[1:])
+    ex_fb1[0].start()
+    for k in range(1, chunks):
+        ex_fa1[k].start()
+        ex_fb1[k].start()
+    for k in range(chunks):
+        fa1r[k, z] = fa1s[k, z]
+        fb1r[k, q] = fb1s[k, q]
     ex_wx.start()
     move_a[...] = regroup(Z * cap, Q, 1)
     move_b[...] = regroup(Q * cap, Z, 1)
@@ -307,16 +325,15 @@
     )
     one_hot = flag(label_col == iota((seeds, classes), 1), F32)
 
-    ex_fa1.recv()
-    fa2s[...] = dot(move_a[...], fa1r[...].reshape(front, DH)).astype(BF16).reshape(fa2s.shape)
-    ex_fa2 = along_q(lambda t: fa2s.at[t], lambda f: fa2r.at[f], blocks(fa2r, Q), fa2_ss, fa2_rs)
-    ex_fa2.start()
-    fa2r[q] = fa2s[q]
-    ex_fb1.recv()
-    fb2s[...] = dot(move_b[...], fb1r[...].reshape(front, DH)).astype(BF16).reshape(fb2s.shape)
-    ex_fb2 = along_z(lambda t: fb2s.at[t], lambda f: fb2r.at[f], blocks(fb2r, Z), fb2_ss, fb2_rs)
-    ex_fb2.start()
-    fb2r[z] = fb2s[z]
+    for k in range(chunks):
+        ex_fa1[k].recv()
+        fa2s[k] = dot(move_a[...], fa1r[k].reshape(front, wide)).astype(BF16).reshape(fa2s.shape[1:])
+        ex_fa2[k].start()
+        fa2r[k, q] = fa2s[k, q]
+        ex_fb1[k].recv()
+        fb2s[k] = dot(move_b[...], fb1r[k].reshape(front, wide)).astype(BF16).reshape(fb2s.shape[1:])
+        ex_fb2[k].start()
+        fb2r[k, z] = fb2s[k, z]
 
     ex_w3.recv()
     w4 = to_sibling(w_all.at[:, :, c], w_all.at[:, :, c], w4_ss, w4_rs)
@@ -344,12 +361,17 @@
         quo(s, half * Q * Z), rem(s, half), rem(quo(s, half * Q), Z), rem(quo(s, half), Q)
     )
 
-    ex_fa2.recv()
-    agg[0] = (dot(outer_a, fa2r[...].reshape(front, DH)) / outer_scale).astype(BF16)
+    for k in range(chunks):
+        at = slice(k * wide, (k + 1) * wide)
+        ex_fa2[k].recv()
+        agg[0, :, at] = (dot(outer_a, fa2r[k].reshape(front, wide)) / outer_scale).astype(BF16)
+        if k < chunks - 1:
+            ex_fb2[k].recv()
+            agg[1, :, at] = (dot(outer_self, fb2r[k].reshape(front, wide)) / outer_scale).astype(BF16)
     w4_in.wait_recv()
     pre[...] = dot(agg[0], w_all[:, :, :, :, :DH].reshape(HID, DH), 1, 1)
-    ex_fb2.recv()
-    agg[1] = (dot(outer_self, fb2r[...].reshape(front, DH)) / outer_scale).astype(BF16)
+    ex_fb2[-1].recv()
+    agg[1, :, DH - wide:] = (dot(outer_self, fb2r[chunks - 1].reshape(front, wide)) / outer_scale).astype(BF16)
     ga = to_sibling(agg.at[sib], agr, ga_ss, ga_rs)
     ga.start()
 
@@ -360,6 +382,16 @@
     exponent = jnp.exp(logits - jnp.max(logits, axis=1, keepdims=True))
     softmax = exponent / jnp.sum(exponent, axis=1, keepdims=True)
     logit_grad = ((softmax - one_hot) / seeds).astype(BF16)
+    widen = flag(iota((classes, CP), 0) == iota((classes, CP), 1))
+    class_rows = dot(dot(logit_grad, widen).astype(BF16), agg_two, 0, 0).astype(BF16)
+    for t in range(X):
+        for cc in range(C):
+            cs1[t * C + cc] = class_rows[:, cc * HH + t * cw:cc * HH + (t + 1) * cw]
+    me_xc = x * C + c
+    ex_c1 = along_xc(lambda t: cs1.at[t], lambda f: cr1.at[f], blocks(cr1, X * C), c1_ss, c1_rs)
+    ex_c1.start()
+    cr1[me_xc] = cs1[me_xc]
+
     agg_grad = dot(logit_grad, cls[...]) / inner_degree
     high = agg_grad.astype(BF16)
     low = (agg_grad - high.astype(F32)).astype(BF16)
@@ -384,30 +416,53 @@
     ex_nb1.start()
     nb1r[q] = nb1s[q]
 
-    widen = flag(iota((classes, CP), 0) == iota((classes, CP), 1))
-    class_rows = dot(dot(logit_grad, widen).astype(BF16), agg_two, 0, 0)
-    left, right = class_rows[:, :HH], class_rows[:, HH:]
-    cs0[...] = jnp.where(c == 0, right, left).astype(BF16)
-    cmine[...] = jnp.where(c == 0, left, right)
-    c0 = to_sibling(cs0, cr0, c0_ss, c0_rs)
-    c0.start()
+    def total(ref, n):
+        acc = ref[0].astype(F32)
+        for k in range(1, n):
+            acc = acc + ref[k].astype(F32)
+        return acc
 
     gmine = dot(pg[...], agg[c], 0, 0)
     ga.wait_recv()
     g0.wait_recv()
-    gmine = gmine + dot(pgr[...], agr[...], 0, 0)
-    gs1[...] = gmine.astype(BF16).reshape(gs1.shape)
-    ex_g1 = along_x(lambda t: gs1.at[:, t], lambda f: gr1.at[f], blocks(gr1, X), g1_ss, g1_rs)
-    ex_g1.start()
-    gr1[x] = gs1[:, x]
-
-    c0.wait_recv()
-    cmine[...] = cmine[...] + cr0[...].astype(F32)
+    gmine = (gmine + dot(pgr[...], agr[...], 0, 0)).astype(BF16).reshape(Z, X, YL * 16, DH)
     for t in range(X):
-        cs1[t] = cmine[:, t * cw:(t + 1) * cw].astype(BF16)
-    ex_c1 = along_x(lambda t: cs1.at[t], lambda f: cr1.at[f], blocks(cr1, X), c1_ss, c1_rs)
-    ex_c1.start()
-    cr1[x] = cs1[x]
+        gs1[t] = gmine[:, t]
+    right, left, across = (lax.bitwise_and(x + d, X - 1) for d in (1, X - 1, 2))
+    lower, upper = pl.ds(0, Z // 2), pl.ds(Z // 2, Z // 2)
+
+    def g1(k, src, dst, to):
+        return copy(src, dst, g1_ss.at[k], g1_rs.at[k], z, q, to)
+
+    r1, l1 = g1(0, gs1.at[across, lower], gra, right), g1(1, gs1.at[across, upper], grb, left)
+    r2, l2 = g1(2, gs1.at[right, upper], grl.at[upper], right), g1(3, gs1.at[left, lower], grr.at[lower], left)
+    r3, l3 = g1(4, gsa, grl.at[lower], right), g1(5, gsb, grr.at[upper], left)
+    for one in (r1, l1, r2, l2):
+        one.start()
+
+    ex_c1.recv()
+    cs2[...] = total(cr1, X * C).astype(BF16).reshape(cs2.shape)
+
+    def to_blocks(act):
+        def step(t, carry):
+            @pl.when(t != z)
+            def _():
+                act(t)
+            return carry
+        lax.fori_loop(0, nb, step, 0)
+
+    to_blocks(lambda t: copy(cs2.at[t], cr2.at[z], c2_ss, c2_rs, t, q, x).start())
+    summing = z < nb
+    ex_c2 = along_z(None, None, blocks(cr2, Z), c2_ss, c2_rs)
+    ex_c3 = along_y(lambda t: cs3, lambda f: cr3.at[f], blocks(cr3, Y), c3_ss, c3_rs)
+    ex_c4 = along_z(lambda t: cfin, lambda f: ca4.at[f], blocks(cr2, Z), c4_ss, c4_rs)
+
+    r1.wait_recv()
+    gsa[...] = (gs1[right, lower].astype(F32) + gra[...].astype(F32)).astype(BF16)
+    r3.start()
+    l1.wait_recv()
+    gsb[...] = (gs1[left, upper].astype(F32) + grb[...].astype(F32)).astype(BF16)
+    l3.start()
 
     ex_na1.recv()
     came = jnp.concatenate([na1r[t * Z:(t + 1) * Z].reshape(hop, xh) for t in range(X)], axis=1)
@@ -425,36 +480,6 @@
     ex_nb2.start()
     nb2r[me_xz] = nb2s[me_xz]
 
-    def total(ref, n):
-        acc = ref[0].astype(F32)
-        for k in range(1, n):
-            acc = acc + ref[k].astype(F32)
-        return acc
-
-    ex_g1.recv()
-    gs2[...] = total(gr1, X).astype(BF16)
-    ex_g2 = along_z(lambda t: gs2.at[t], lambda f: gr2.at[f], blocks(gr2, Z), g2_ss, g2_rs)
-    ex_g2.start()
-    gr2[z] = gs2[z]
-
-    ex_c1.recv()
-    cs2[...] = total(cr1, X).astype(BF16).reshape(cs2.shape)
-
-    def to_blocks(act):
-        def step(t, carry):
-            @pl.when(t != z)
-            def _():
-                act(t)
-            return carry
-        lax.fori_loop(0, nb, step, 0)
-
-    to_blocks(lambda t: copy(cs2.at[t], cr2.at[z], c2_ss, c2_rs, t, q, x).start())
-    summing = z < nb
-
-    ex_c2 = along_z(None, None, blocks(cr2, Z), c2_ss, c2_rs)
-    ex_c3 = along_y(lambda t: cs3, lambda f: cr3.at[f], blocks(cr3, Y), c3_ss, c3_rs)
-    ex_c4 = along_z(lambda t: cfin, lambda f: ca4.at[f], blocks(cr2, Z), c4_ss, c4_rs)
-
     @pl.when(summing)
     def _():
         cr2[z] = cs2[z]
@@ -463,17 +488,12 @@
         ex_c3.start()
         cr3[y] = cs3[...]
 
-    ex_g2.recv()
-    gs3[...] = total(gr2, Z).astype(BF16).reshape(gs3.shape)
-
-    def g3_copy(yl):
-        return copy(gs3.at[yl], gr3.at[y], g3_ss.at[yl], g3_rs, z, (x * YL + yl) * C + c, x)
-
-    for yl in range(YL):
-        @pl.when(x * YL + yl != y)
-        def _():
-            g3_copy(yl).start()
-    owning = y // YL == x
+    for one in (r2, l2, r3, l3):
+        one.wait_recv()
+    gs2[...] = (gs1[x].astype(F32) + grl[...].astype(F32) + grr[...].astype(F32)).astype(BF16)
+    ex_g2 = along_z(lambda t: gs2.at[t], lambda f: gr2.at[f], blocks(gr2, Z), g2_ss, g2_rs)
+    ex_g2.start()
+    gr2[z] = gs2[z]
 
     @pl.when(summing)
     def _():
@@ -482,10 +502,33 @@
         ex_c4.start()
         ca4[z] = cfin[...]
 
+    ex_g2.recv()
+    gs3[...] = total(gr2, Z).astype(BF16).reshape(gs3.shape)
+
+    def g3_copy(yl):
+        return copy(gs3.at[yl], gr3.at[y], g3_ss.at[yl], g3_rs, z, (x * YL + yl) * C + c, x)
+
+    for yl in range(YL):
+        @pl.when(x * YL + yl != y)
+        def _():
+            g3_copy(yl).start()
+    owning = y // YL == x
+
+    @pl.when(summing)
+    def _():
+        some = ca4.at[pl.ds(0, nb - 1)]
+        copy(some, some, c4_ss, c4_rs, z, q, x).wait_recv()
+
+    @pl.when(jnp.logical_not(summing))
+    def _():
+        copy(ca4, ca4, c4_ss, c4_rs, z, q, x).wait_recv()
+
+    ex_c5 = along_xc(lambda t: ca4, lambda f: ca5.at[f], blocks(ca5, X * C), c5_ss, c5_rs)
+    ex_c5.start()
+    ca5[me_xc] = ca4[...]
+
     ex_na2.recv()
     node_out[:, :xh] = dot(place_a[...], na2r[...].reshape(X * hop, xh)).astype(BF16)
-    ex_nb2.recv()
-    node_out[:, xh:] = dot(place_b[...], nb2r[...].reshape(X * hop, xh)).astype(BF16)
 
     def g4_copy(xx, cc):
         return copy(gs4.at[cc], gr4.at[c], g4_ss.at[xx * C + cc], g4_rs.at[c], z, y * C + cc, xx)
@@ -506,19 +549,13 @@
 
     g4_each(lambda xx, cc: g4_copy(xx, cc).start())
 
-    @pl.when(summing)
-    def _():
-        some = ca4.at[pl.ds(0, nb - 1)]
-        copy(some, some, c4_ss, c4_rs, z, q, x).wait_recv()
-
-    @pl.when(jnp.logical_not(summing))
-    def _():
-        copy(ca4, ca4, c4_ss, c4_rs, z, q, x).wait_recv()
-
-    me_xc = x * C + c
-    ex_c5 = along_xc(lambda t: ca4, lambda f: ca5.at[f], blocks(ca5, X * C), c5_ss, c5_rs)
-    ex_c5.start()
-    ca5[me_xc] = ca4[...]
+    ex_nb2.recv()
+    node_out[:, xh:] = dot(place_b[...], nb2r[...].reshape(X * hop, xh)).astype(BF16)
+
+    ex_c5.recv()
+    for t in range(X):
+        for cc in range(C):
+            class_out[:, cc * HH + t * cw:cc * HH + (t + 1) * cw] = ca5[t * C + cc].reshape(CP, cw)
 
     for cc in range(C):
         @pl.when(jnp.logical_not(owning & (c == cc)))
@@ -526,16 +563,11 @@
             copy(gs4.at[0], gr4.at[cc], g4_ss.at[0], g4_rs.at[cc], z, y * C + cc, y // YL).wait_recv()
         hidden_out[:, cc * DH:(cc + 1) * DH] = gr4[cc]
 
-    ex_c5.recv()
-    for t in range(X):
-        for cc in range(C):
-            class_out[:, cc * HH + t * cw:cc * HH + (t + 1) * cw] = ca5[t * C + cc].reshape(CP, cw)
-
-    for ex in (ex_i1, ex_i2, ex_wx, ex_w2, ex_w3, ex_fa1, ex_fb1, ex_fa2, ex_fb2, ex_na1, ex_nb1, ex_na2, ex_nb2,
-               ex_g1, ex_g2, ex_c1, ex_c5):
+    for ex in (ex_i1, ex_i2, ex_wx, ex_w2, ex_w3, *ex_fa1, *ex_fb1, *ex_fa2, *ex_fb2, ex_na1, ex_nb1, ex_na2, ex_nb2,
+               ex_g2, ex_c1, ex_c5):
         ex.sent()
     w1_each(lambda t: w1_copy(t).wait_send())
-    for one in (w4, ga, g0, c0):
+    for one in (w4, ga, g0, r1, l1, r2, l2, r3, l3):
         one.wait_send()
 
     @pl.when(summing)
@@ -576,34 +608,33 @@
     LW = max(Z * 8, 128)
     dims = (Z, Y, C, X, cap, tile, rows, classes)
     vm, dma = pltpu.VMEM, pltpu.SemaphoreType.DMA
-    xh = HID // X // 2
+    xh, nk = HID // X // 2, DH // 128
     scratch = [
         vm(features.shape, BF16), vm(outer_masks.shape, jnp.int32), vm(inner_masks.shape, jnp.int32),
         vm(class_weight.shape, BF16),
         vm((8, NO), F32), vm((Z, 8, NO), F32), vm((Q, 8, LW), F32), vm((Q, 8, LW), F32),
         vm((X, Q * 8, LW), BF16), vm((rows, X * hop), BF16), vm((rows, X * hop), BF16),
         vm((16, DH), BF16), vm((C, 16, DH), BF16), vm((Z, X, C, 16, D), BF16),
-        vm((Z, cap * Q, DH), BF16), vm((Z, cap * Q, DH), BF16), vm((Q, cap * Z, DH), BF16), vm((Q, cap * Z, DH), BF16),
-        vm((Q, cap * Z, DH), BF16), vm((Q, cap * Z, DH), BF16), vm((Z, cap * Q, DH), BF16), vm((Z, cap * Q, DH), BF16),
+        *[vm((nk, Z, cap * Q, DH // nk), BF16)] * 2, *[vm((nk, Q, cap * Z, DH // nk), BF16)] * 2,
+        *[vm((nk, Q, cap * Z, DH // nk), BF16)] * 2, *[vm((nk, Z, cap * Q, DH // nk), BF16)] * 2,
         vm((cap * NO, cap * NO), BF16), vm((cap * NO, cap * NO), BF16), vm((hop, hop), BF16), vm((hop, hop), BF16),
         vm((2, hop, DH), BF16), vm((hop, DH), BF16), vm((hop, HID), F32), vm((hop, HID), BF16), vm((hop, HID), BF16),
         vm((X * Z, Q * half, xh), BF16), vm((X * Z, Q * half, xh), BF16),
         vm((Q, X, Z * half, xh), BF16), vm((Q, X, Z * half, xh), BF16),
         vm((Q, Z * half, HH), BF16), vm((Q, Z * half, HH), BF16),
         vm((X * Z, Q * half, xh), BF16), vm((X * Z, Q * half, xh), BF16),
-        vm((Z, X, YL * 16, DH), BF16), vm((X, Z, YL * 16, DH), BF16),
+        vm((X, Z, YL * 16, DH), BF16), *[vm((Z // 2, YL * 16, DH), BF16)] * 4, *[vm((Z, YL * 16, DH), BF16)] * 2,
         vm((Z, YL * 16, DH), BF16), vm((Z, YL * 16, DH), BF16),
         vm((YL, 16, DH), BF16), vm((Y, 16, DH), BF16), vm((C, 8, DH), F32), vm((C, 8, DH), F32),
-        vm((CP, HH), F32), vm((CP, HH), BF16), vm((CP, HH), BF16),
-        vm((X, CP, cw), BF16), vm((X, CP, cw), BF16), vm((nb, cb, cw), BF16), vm((Z, cb, cw), BF16),
+        vm((X * C, CP, cw), BF16), vm((X * C, CP, cw), BF16), vm((nb, cb, cw), BF16), vm((Z, cb, cw), BF16),
         vm((cb, cw), BF16), vm((Y, cb, cw), BF16), vm((cb, cw), BF16), vm((nb, cb, cw), BF16),
         vm((X * C, nb, cb, cw), BF16),
         dma((4,)),
         *[dma] * 6,
         dma((Y,)), dma((C,)), *[dma] * 6,
-        *[dma] * 16,
-        *[dma] * 8, dma((YL,)), dma, dma((X * C,)), dma((C,)),
-        *[dma] * 12,
+        *[dma((nk,))] * 8, *[dma] * 8,
+        *[dma] * 4, dma((6,)), dma((6,)), dma, dma, dma((YL,)), dma, dma((X * C,)), dma((C,)),
+        *[dma] * 10,
     ]
     hbm = pl.BlockSpec(memory_space=pl.ANY)
     vmem = pl.BlockSpec(memory_space=pltpu.VMEM)

time: 99.7 us -> 89.3 us (0.90)
  Pallas kernels: 95.7 us -> 84.6 us
    pallas_call x1, Pallas kernels: 95.7 us -> 84.6 us  [on_device(): pl.pallas_call(functools.partial(kernel, dims), out_shape=(jax.ShapeDtype...]
where the time goes in v3:
time: 89.3 us; the launch traced here: 88.4 us
  Pallas kernels  84.6 us (95%)
  other arithmetic  1.91 us (2%)
  local copies, waits for them, and re-layouts  1.27 us (1%)
    pallas_call x1, Pallas kernels, on_device(): pl.pallas_call(functools.partial(kernel, dims), out_shape=(jax.ShapeDtype...  84.6 us
    convert_element_type x1, other arithmetic, on_device(): return (hidden_grad, class_grad[:classes].astype(F32), node_grad)  1.91 us

profile of v3, /device:TPU:1, one launch (start us, length us, event | category | flops | bytes accessed | tf_op | source)
XLA Modules:
  0.0 88.4 jit_solution(12303473390751570377)
XLA Ops:
  0.6 84.6 %shard_map.121 = (f32[8,768]{1,0:T(8,128)}, bf16[160,1024]{1,0:T(8,128)(2,1)}, bf16[256,256]{1,0:T(8,128)(2,1)}) custom-call(bf16[256,768]{1,0:T(8,128)(2,1)} %feat_hbm.1, bf16[8,768]{1,0:T(8,128)(2,1)} %weight_ref.1, bf16[153,1024]{1,0:T(8,128)(2,1)} %cls_hbm.1, s32[4,128]{1,0:T(4,128)} %bitcast.3, s32[2,128]{1,0:T(2,128)} %bitcast.4, s32[2,2]{1,0:T(2,128)} %otile_ref.1, ...), custom_call_target="tpu_custom_call" | custom-call | flops 2000000000 | bytes 3000000 | tf_op jit(solution)/shard_map/pallas_call | solution.py:642
  85.2 0.0 copy-start.1
  85.2 0.0 copy-start
  85.2 1.9 %slice_convert_fusion = f32[153,1024]{1,0:T(8,128)} fusion(bf16[160,1024]{1,0:T(8,128)(2,1)} %get-tuple-element.7), kind=kLoop, calls=%fused_computation | loop fusion | flops 156672 | bytes 940032 | tf_op jit(solution)/shard_map/convert_element_type | solution.py:660
  87.1 0.0 copy-done.1
  87.1 0.6 copy.15
  87.7 0.0 copy-done
  87.7 0.7 copy.16
Async XLA Ops:
  85.2 1.9 %copy-start.1 = (f32[8,768]{1,0:T(8,128)S(1)}, f32[8,768]{1,0:T(8,128)}, u32[]{:S(2)}) copy-start(f32[8,768]{1,0:T(8,128)} %get-tuple-element.12) | copy-start | bytes 73732
  85.2 2.5 %copy-start = (bf16[256,256]{1,0:T(8,128)(2,1)S(1)}, bf16[256,256]{1,0:T(8,128)(2,1)}, u32[]{:S(2)}) copy-start(bf16[256,256]{1,0:T(8,128)(2,1)} %get-tuple-element.14) | copy-start | bytes 393220

commit v4 on v3

--- a/solution.py
+++ b/solution.py
@@ -46,13 +46,13 @@
 
 def kernel(
     dims,
-    feat_hbm, weight_ref, cls_hbm, ids_ref, counts_ref, otile_ref, omask_hbm, itile_ref, imask_hbm, labels_ref,
+    feat_hbm, weight_hbm, cls_hbm, ids_hbm, counts_hbm, otile_ref, omask_hbm, itile_ref, imask_hbm, labels_hbm,
     hidden_out, class_out, node_out,
-    feat, omask, imask, cls,
+    feat, omask, imask, cls, weight_ref, ids_ref, counts_ref, labels_ref,
     i1s, i1r, i2s, i2r, wx, place_a, place_b,
     ws, wr, w_all,
     fa1s, fa1r, fa2s, fa2r, fb1s, fb1r, fb2s, fb2r, move_a, move_b, swap_a, swap_b,
-    agg, agr, pre, pg, pgr,
+    agg, agr, pre, pgt, pgtr, diff,
     na1s, na1r, na2s, na2r, nb1s, nb1r, nb2s, nb2r,
     gs1, gra, grb, gsa, gsb, grl, grr, gs2, gr2, gs3, gr3, gs4, gr4,
     cs1, cr1, cs2, cr2, cs3, cr3, cfin, ca4, ca5,
@@ -142,12 +142,11 @@
     def to_sibling(src, dst, ss, rs):
         return copy(src, dst, ss, rs, z, y * C + sib, x)
 
-    loads = [
-        pltpu.make_async_copy(feat_hbm, feat, local_sem.at[0]),
-        pltpu.make_async_copy(omask_hbm, omask, local_sem.at[1]),
-        pltpu.make_async_copy(imask_hbm, imask, local_sem.at[2]),
-        pltpu.make_async_copy(cls_hbm, cls, local_sem.at[3]),
-    ]
+    staged = (
+        (ids_hbm, ids_ref), (weight_hbm, weight_ref), (feat_hbm, feat), (counts_hbm, counts_ref),
+        (omask_hbm, omask), (imask_hbm, imask), (labels_hbm, labels_ref), (cls_hbm, cls),
+    )
+    loads = [pltpu.make_async_copy(src, dst, local_sem.at[k]) for k, (src, dst) in enumerate(staged)]
     for load in loads:
         load.start()
 
@@ -165,6 +164,8 @@
     each(X, lambda d: greet(z, y * C + sib, lax.bitwise_and(x + d, X - 1)))
 
     i1s[...] = jnp.zeros_like(i1s)
+    for load in loads[:2]:
+        load.wait()
     i1s[0:cap, :] = ids_ref[...].astype(F32)
     w32 = weight_ref[...].astype(F32)
     ws[...] = jnp.concatenate([w32[:, :DH], w32[:, DH:]], axis=0).astype(BF16)
@@ -223,8 +224,7 @@
     )
     ex_w2.start()
 
-    for load in loads[:1]:
-        load.wait()
+    loads[2].wait()
     lane_q = iota((front, Q * 8), 1)
 
     ex_i2.recv()
@@ -241,7 +241,11 @@
     chunks, wide = fa1s.shape[0], fa1s.shape[3]
     r = iota((front, 1), 0)
     pick_a = picked(quo(r, cap * Q) * S8 + quo(rem(r, cap * Q), Q), rem(r, Q))
-    rows_a = dot(pick_a, feat[:, :DH]).astype(BF16)
+
+    def column_blocks(first):
+        return jnp.concatenate([feat[:, b * wide:(b + 1) * wide] for b in range(first, 2 * chunks, 2)], axis=1)
+
+    rows_a = dot(pick_a, column_blocks(0)).astype(BF16)
     ex_fa1, ex_fb1, ex_fa2, ex_fb2 = [], [], [], []
     for k in range(chunks):
         at = slice(k * wide, (k + 1) * wide)
@@ -256,7 +260,7 @@
             lambda t, k=k: fb2s.at[k, t], lambda f, k=k: fb2r.at[k, f], blocks(fb2r.at[k], Z), fb2_ss.at[k], fb2_rs.at[k]))
     ex_fa1[0].start()
     pick_b = picked(rem(r, Z) * S8 + quo(rem(r, cap * Z), Z), quo(r, cap * Z))
-    rows_b = dot(pick_b, feat[:, DH:]).astype(BF16)
+    rows_b = dot(pick_b, column_blocks(1)).astype(BF16)
     for k in range(chunks):
         at = slice(k * wide, (k + 1) * wide)
         fb1s[k] = rows_b[:, at].reshape(fb1s.shape[1:])
@@ -277,7 +281,7 @@
     )
     ex_w3.start()
 
-    for load in loads[1:]:
+    for load in loads[3:]:
         load.wait()
     counts = counts_ref[...].astype(F32)
     counts8 = jnp.concatenate([counts, jnp.zeros((6, NO), F32)], axis=0).astype(BF16)
@@ -318,6 +322,7 @@
     inner32 = jnp.concatenate(tiles, axis=1)
     inner_degree = jnp.maximum(jnp.sum(inner32, axis=1, keepdims=True), 1.0)
     inner = inner32.astype(BF16)
+    inner_twice = jnp.concatenate([inner32.T, inner32.T], axis=1).astype(BF16)
 
     label_row = labels_ref[...]
     label_col = jnp.sum(
@@ -354,28 +359,33 @@
         return flag(iota((rows, n), 0).astype(F32) == ids)
 
     s = iota((1, X * hop), 1)
+    def plane(d):
+        return lax.bitwise_and(x + X - d, jnp.full_like(d, X - 1))
+
     place_a[...] = places(
-        rem(quo(s, half * Z), X), rem(s, half), rem(quo(s, half), Z), quo(s, half * Z * X)
+        plane(quo(s, half * Z * 2 * Q) * 2 + rem(quo(s, half * Z), 2)),
+        rem(s, half), rem(quo(s, half), Z), rem(quo(s, half * Z * 2), Q)
     )
     place_b[...] = places(
-        quo(s, half * Q * Z), rem(s, half), rem(quo(s, half * Q), Z), rem(quo(s, half), Q)
-    )
-
-    for k in range(chunks):
-        at = slice(k * wide, (k + 1) * wide)
+        plane(quo(s, half * Q * Z)), rem(s, half), rem(quo(s, half * Q), Z), rem(quo(s, half), Q)
+    )
+
+    for k in range(chunks):
         ex_fa2[k].recv()
-        agg[0, :, at] = (dot(outer_a, fa2r[k].reshape(front, wide)) / outer_scale).astype(BF16)
-        if k < chunks - 1:
-            ex_fb2[k].recv()
-            agg[1, :, at] = (dot(outer_self, fb2r[k].reshape(front, wide)) / outer_scale).astype(BF16)
-    w4_in.wait_recv()
-    pre[...] = dot(agg[0], w_all[:, :, :, :, :DH].reshape(HID, DH), 1, 1)
-    ex_fb2[-1].recv()
-    agg[1, :, DH - wide:] = (dot(outer_self, fb2r[chunks - 1].reshape(front, wide)) / outer_scale).astype(BF16)
+        part_a = (dot(outer_a, fa2r[k].reshape(front, wide)) / outer_scale).astype(BF16)
+        ex_fb2[k].recv()
+        part_b = (dot(outer_self, fb2r[k].reshape(front, wide)) / outer_scale).astype(BF16)
+        for b, part in ((2 * k, part_a), (2 * k + 1, part_b)):
+            agg[b // chunks, :, (b % chunks) * wide:(b % chunks + 1) * wide] = part
+        if k == 0:
+            w4_in.wait_recv()
+        part = dot(
+            jnp.concatenate([part_a, part_b], axis=1),
+            w_all[:, :, :, :, 2 * k * wide:2 * (k + 1) * wide].reshape(HID, 2 * wide), 1, 1)
+        pre[...] = part if k == 0 else pre[...] + part
     ga = to_sibling(agg.at[sib], agr, ga_ss, ga_rs)
     ga.start()
 
-    pre[...] = pre[...] + dot(agg[1], w_all[:, :, :, :, DH:].reshape(HID, DH), 1, 1)
     hidden = jnp.maximum(pre[...], 0.0).astype(BF16)
     agg_two = (dot(inner, hidden) / inner_degree).astype(BF16)
     logits = dot(agg_two, cls[...], 1, 1)
@@ -395,26 +405,46 @@
     agg_grad = dot(logit_grad, cls[...]) / inner_degree
     high = agg_grad.astype(BF16)
     low = (agg_grad - high.astype(F32)).astype(BF16)
-    hidden_diff = dot(inner, high, 0, 0) + dot(inner, low, 0, 0)
-
-    pg[...] = jnp.where(pre[...] > 0.0, hidden_diff, 0.0).astype(BF16)
-    g0 = to_sibling(pg, pgr, g0_ss, g0_rs)
+    hidden_diff = dot(inner_twice, jnp.concatenate([high, low], axis=0))
+    pgt[...] = jnp.where(pre[...] > 0.0, hidden_diff, 0.0).T.astype(BF16)
+    g0 = to_sibling(pgt, pgtr, g0_ss, g0_rs)
     g0.start()
 
-    diff16 = hidden_diff.astype(BF16)
+    diff[...] = hidden_diff.astype(BF16)
     xw = HID // X
     xh = xw // 2
+    pair = 2 * Z
+
+    def xz_leg(group, src, dst, ss, rs):
+        def step(t, carry):
+            d, zz = 2 * group + t // Z, lax.bitwise_and(z + t, Z - 1)
+            copy(src(d, zz), dst.at[d * Z + z], ss, rs, zz, q, lax.bitwise_and(x + d, X - 1)).start()
+            return carry
+        lax.fori_loop(0 if group else 1, pair, step, 0)
+
+    def wait_blocks(ref, n, ss, rs):
+        some = ref.at[pl.ds(0, n)]
+        return copy(some, some, ss, rs, z, q, lax.bitwise_and(x + 1, X - 1))
+
     for t in range(X):
-        na1s[t * Z:(t + 1) * Z] = diff16[:, t * xw:t * xw + xh].reshape(Z, Q * half, xh)
-    ex_na1 = along_xz(lambda t: na1s.at[t], lambda f: na1r.at[f], blocks(na1r, X * Z), na1_ss, na1_rs)
-    ex_na1.start()
-    me_xz = x * Z + z
-    na1r[me_xz] = na1s[me_xz]
-    second = jnp.concatenate([diff16[:, t * xw + xh:(t + 1) * xw] for t in range(X)], axis=1)
-    nb1s[...] = dot(swap_a[...], second).astype(BF16).reshape(nb1s.shape)
-    ex_nb1 = along_q(lambda t: nb1s.at[t], lambda f: nb1r.at[f], blocks(nb1r, Q), nb1_ss, nb1_rs)
-    ex_nb1.start()
-    nb1r[q] = nb1s[q]
+        na1s[t * Z:(t + 1) * Z] = diff[:, t * xw:t * xw + xh].reshape(Z, Q * half, xh)
+    for d in range(X):
+        cols = pl.ds(pl.multiple_of(lax.bitwise_and(x + d, X - 1) * xw + xh, xh), xh)
+        nb1s[d // 2, :, :, (d % 2) * xh:(d % 2 + 1) * xh] = (
+            dot(swap_a[...], diff[:, cols]).astype(BF16).reshape(Q, Z * half, xh))
+    ex_nb1 = [
+        along_q(lambda t, g=g: nb1s.at[g, t], lambda f, g=g: nb1r.at[g, f], blocks(nb1r.at[g], Q), nb1_ss.at[g], nb1_rs.at[g])
+        for g in range(2)
+    ]
+    ex_na2 = [
+        along_q(lambda t, g=g: na2s.at[g, t], lambda f, g=g: na2r.at[g, f], blocks(na2r.at[g], Q), na2_ss.at[g], na2_rs.at[g])
+        for g in range(2)
+    ]
+    for g in range(2):
+        xz_leg(g, lambda d, zz: na1s.at[lax.bitwise_and(x + d, X - 1) * Z + zz], na1r, na1_ss.at[g], na1_rs.at[g])
+        ex_nb1[g].start()
+        nb1r[g, q] = nb1s[g, q]
+    na1r[z] = na1s[x * Z + z]
 
     def total(ref, n):
         acc = ref[0].astype(F32)
@@ -422,88 +452,97 @@
             acc = acc + ref[k].astype(F32)
         return acc
 
-    gmine = dot(pg[...], agg[c], 0, 0)
+    gmine = dot(pgt[...], agg[c])
     ga.wait_recv()
     g0.wait_recv()
-    gmine = (gmine + dot(pgr[...], agr[...], 0, 0)).astype(BF16).reshape(Z, X, YL * 16, DH)
-    for t in range(X):
-        gs1[t] = gmine[:, t]
+    gmine = (gmine + dot(pgtr[...], agr[...])).astype(BF16).reshape(Z, X, YL * 16, DH)
+    for k in range(chunks):
+        for t in range(X):
+            gs1[k, t] = gmine[:, t, :, k * wide:(k + 1) * wide]
     right, left, across = (lax.bitwise_and(x + d, X - 1) for d in (1, X - 1, 2))
     lower, upper = pl.ds(0, Z // 2), pl.ds(Z // 2, Z // 2)
 
-    def g1(k, src, dst, to):
-        return copy(src, dst, g1_ss.at[k], g1_rs.at[k], z, q, to)
-
-    r1, l1 = g1(0, gs1.at[across, lower], gra, right), g1(1, gs1.at[across, upper], grb, left)
-    r2, l2 = g1(2, gs1.at[right, upper], grl.at[upper], right), g1(3, gs1.at[left, lower], grr.at[lower], left)
-    r3, l3 = g1(4, gsa, grl.at[lower], right), g1(5, gsb, grr.at[upper], left)
-    for one in (r1, l1, r2, l2):
-        one.start()
+    def g1(k, n, src, dst, to):
+        return copy(src, dst, g1_ss.at[k, n], g1_rs.at[k, n], z, q, to)
+
+    ring = [(
+        g1(k, 0, gs1.at[k, across, lower], gra.at[k], right), g1(k, 1, gs1.at[k, across, upper], grb.at[k], left),
+        g1(k, 2, gs1.at[k, right, upper], grl.at[k, upper], right), g1(k, 3, gs1.at[k, left, lower], grr.at[k, lower], left),
+        g1(k, 4, gsa.at[k], grl.at[k, lower], right), g1(k, 5, gsb.at[k], grr.at[k, upper], left),
+    ) for k in range(chunks)]
+    for k in range(chunks):
+        for one in ring[k][:4]:
+            one.start()
 
     ex_c1.recv()
     cs2[...] = total(cr1, X * C).astype(BF16).reshape(cs2.shape)
 
     def to_blocks(act):
         def step(t, carry):
-            @pl.when(t != z)
+            @pl.when(t != y)
             def _():
                 act(t)
             return carry
         lax.fori_loop(0, nb, step, 0)
 
-    to_blocks(lambda t: copy(cs2.at[t], cr2.at[z], c2_ss, c2_rs, t, q, x).start())
-    summing = z < nb
-    ex_c2 = along_z(None, None, blocks(cr2, Z), c2_ss, c2_rs)
-    ex_c3 = along_y(lambda t: cs3, lambda f: cr3.at[f], blocks(cr3, Y), c3_ss, c3_rs)
-    ex_c4 = along_z(lambda t: cfin, lambda f: ca4.at[f], blocks(cr2, Z), c4_ss, c4_rs)
-
-    r1.wait_recv()
-    gsa[...] = (gs1[right, lower].astype(F32) + gra[...].astype(F32)).astype(BF16)
-    r3.start()
-    l1.wait_recv()
-    gsb[...] = (gs1[left, upper].astype(F32) + grb[...].astype(F32)).astype(BF16)
-    l3.start()
-
-    ex_na1.recv()
-    came = jnp.concatenate([na1r[t * Z:(t + 1) * Z].reshape(hop, xh) for t in range(X)], axis=1)
-    came = dot(swap_a[...], came).astype(BF16)
-    for t in range(X):
-        na2s[:, t] = came[:, t * xh:(t + 1) * xh].reshape(Q, Z * half, xh)
-    ex_na2 = along_q(lambda t: na2s.at[t], lambda f: na2r.at[f], blocks(na2r, Q), na2_ss, na2_rs)
-    ex_na2.start()
-    na2r[q] = na2s[q]
-    ex_nb1.recv()
-    came = dot(swap_b[...], nb1r[...].reshape(hop, X * xh)).astype(BF16)
-    for t in range(X):
-        nb2s[t * Z:(t + 1) * Z] = came[:, t * xh:(t + 1) * xh].reshape(Z, Q * half, xh)
-    ex_nb2 = along_xz(lambda t: nb2s.at[t], lambda f: nb2r.at[f], blocks(nb2r, X * Z), nb2_ss, nb2_rs)
-    ex_nb2.start()
-    nb2r[me_xz] = nb2s[me_xz]
+    to_blocks(lambda t: copy(cs2.at[t], cr2.at[y], c2_ss, c2_rs, z, t * C + c, x).start())
+    summing = y < nb
+    ex_c2 = along_y(None, None, blocks(cr2, Y), c2_ss, c2_rs)
+    ex_c3 = along_z(lambda t: cs3, lambda f: cr3.at[f], blocks(cr3, Z), c3_ss, c3_rs)
+    ex_c4 = along_y(lambda t: cfin, lambda f: ca4.at[f], blocks(cr2, Y), c4_ss, c4_rs)
+
+    for k in range(chunks):
+        r1, l1, r2, l2, r3, l3 = ring[k]
+        r1.wait_recv()
+        gsa[k] = (gs1[k, right, lower].astype(F32) + gra[k].astype(F32)).astype(BF16)
+        r3.start()
+        l1.wait_recv()
+        gsb[k] = (gs1[k, left, upper].astype(F32) + grb[k].astype(F32)).astype(BF16)
+        l3.start()
+
+    for g in range(2):
+        wait_blocks(na1r, pair if g else pair - 1, na1_ss.at[g], na1_rs.at[g]).wait_recv()
+        came = jnp.concatenate([na1r[d * Z:(d + 1) * Z].reshape(hop, xh) for d in (2 * g, 2 * g + 1)], axis=1)
+        came = dot(swap_a[...], came).astype(BF16)
+        for t in range(2):
+            na2s[g, :, t] = came[:, t * xh:(t + 1) * xh].reshape(Q, Z * half, xh)
+        ex_na2[g].start()
+        na2r[g, q] = na2s[g, q]
+        ex_nb1[g].recv()
+        came = dot(swap_b[...], nb1r[g].reshape(hop, 2 * xh)).astype(BF16)
+        for t in range(2):
+            nb2s[(2 * g + t) * Z:(2 * g + t + 1) * Z] = came[:, t * xh:(t + 1) * xh].reshape(Z, Q * half, xh)
+        xz_leg(g, lambda d, zz: nb2s.at[d * Z + zz], nb2r, nb2_ss, nb2_rs)
+    nb2r[z] = nb2s[z]
 
     @pl.when(summing)
     def _():
-        cr2[z] = cs2[z]
+        cr2[y] = cs2[y]
         ex_c2.recv()
-        cs3[...] = total(cr2, Z).astype(BF16)
+        cs3[...] = total(cr2, Y).astype(BF16)
         ex_c3.start()
-        cr3[y] = cs3[...]
-
-    for one in (r2, l2, r3, l3):
-        one.wait_recv()
-    gs2[...] = (gs1[x].astype(F32) + grl[...].astype(F32) + grr[...].astype(F32)).astype(BF16)
-    ex_g2 = along_z(lambda t: gs2.at[t], lambda f: gr2.at[f], blocks(gr2, Z), g2_ss, g2_rs)
-    ex_g2.start()
-    gr2[z] = gs2[z]
+        cr3[z] = cs3[...]
+
+    ex_g2 = []
+    for k in range(chunks):
+        for one in ring[k][2:]:
+            one.wait_recv()
+        gs2[k] = (gs1[k, x].astype(F32) + grl[k].astype(F32) + grr[k].astype(F32)).astype(BF16)
+        ex_g2.append(along_z(
+            lambda t, k=k: gs2.at[k, t], lambda f, k=k: gr2.at[k, f], blocks(gr2.at[k], Z), g2_ss.at[k], g2_rs.at[k]))
+        ex_g2[k].start()
+        gr2[k, z] = gs2[k, z]
 
     @pl.when(summing)
     def _():
         ex_c3.recv()
-        cfin[...] = total(cr3, Y).astype(BF16)
+        cfin[...] = total(cr3, Z).astype(BF16)
         ex_c4.start()
-        ca4[z] = cfin[...]
-
-    ex_g2.recv()
-    gs3[...] = total(gr2, Z).astype(BF16).reshape(gs3.shape)
+        ca4[y] = cfin[...]
+
+    for k in range(chunks):
+        ex_g2[k].recv()
+        gs3[:, :, k * wide:(k + 1) * wide] = total(gr2.at[k], Z).astype(BF16).reshape(YL, 16, wide)
 
     def g3_copy(yl):
         return copy(gs3.at[yl], gr3.at[y], g3_ss.at[yl], g3_rs, z, (x * YL + yl) * C + c, x)
@@ -527,7 +566,8 @@
     ex_c5.start()
     ca5[me_xc] = ca4[...]
 
-    ex_na2.recv()
+    for g in range(2):
+        ex_na2[g].recv()
     node_out[:, :xh] = dot(place_a[...], na2r[...].reshape(X * hop, xh)).astype(BF16)
 
     def g4_copy(xx, cc):
@@ -549,13 +589,11 @@
 
     g4_each(lambda xx, cc: g4_copy(xx, cc).start())
 
-    ex_nb2.recv()
+    wait_blocks(nb2r, 2 * pair - 1, nb2_ss, nb2_rs).wait_recv()
     node_out[:, xh:] = dot(place_b[...], nb2r[...].reshape(X * hop, xh)).astype(BF16)
 
     ex_c5.recv()
-    for t in range(X):
-        for cc in range(C):
-            class_out[:, cc * HH + t * cw:cc * HH + (t + 1) * cw] = ca5[t * C + cc].reshape(CP, cw)
+    class_out[...] = ca5[...].reshape(class_out.shape)
 
     for cc in range(C):
         @pl.when(jnp.logical_not(owning & (c == cc)))
@@ -563,12 +601,14 @@
             copy(gs4.at[0], gr4.at[cc], g4_ss.at[0], g4_rs.at[cc], z, y * C + cc, y // YL).wait_recv()
         hidden_out[:, cc * DH:(cc + 1) * DH] = gr4[cc]
 
-    for ex in (ex_i1, ex_i2, ex_wx, ex_w2, ex_w3, *ex_fa1, *ex_fb1, *ex_fa2, *ex_fb2, ex_na1, ex_nb1, ex_na2, ex_nb2,
-               ex_g2, ex_c1, ex_c5):
+    for ex in (ex_i1, ex_i2, ex_wx, ex_w2, ex_w3, *ex_fa1, *ex_fb1, *ex_fa2, *ex_fb2, *ex_nb1, *ex_na2, *ex_g2, ex_c1, ex_c5):
         ex.sent()
     w1_each(lambda t: w1_copy(t).wait_send())
-    for one in (w4, ga, g0, r1, l1, r2, l2, r3, l3):
+    for one in (w4, ga, g0, *[leg for legs in ring for leg in legs]):
         one.wait_send()
+    for g in range(2):
+        wait_blocks(na1r, pair if g else pair - 1, na1_ss.at[g], na1_rs.at[g]).wait_send()
+    wait_blocks(nb2r, 2 * pair - 1, nb2_ss, nb2_rs).wait_send()
 
     @pl.when(summing)
     def _():
@@ -586,6 +626,28 @@
         def _():
             g3_copy(yl).wait_send()
     g4_each(lambda xx, cc: g4_copy(xx, cc).wait_send())
+
+
+def finish(class_dims, hidden_in, class_in, node_in, hidden_out, class_out, node_out, parts, spread, sem):
+    X, C, classes = class_dims
+    passed = [
+        pltpu.make_async_copy(class_in, parts, sem.at[0]),
+        pltpu.make_async_copy(hidden_in, hidden_out, sem.at[1]),
+        pltpu.make_async_copy(node_in, node_out, sem.at[2]),
+    ]
+    for one in passed:
+        one.start()
+    passed[0].wait()
+    cw = parts.shape[2]
+    for t in range(X):
+        for c in range(C):
+            at = (c * X + t) * cw
+            spread[:, at:at + cw] = parts[t * C + c].astype(F32)[:classes]
+    last = pltpu.make_async_copy(spread, class_out, sem.at[3])
+    last.start()
+    for one in passed[1:]:
+        one.wait()
+    last.wait()
 
 
 def on_device(
@@ -611,29 +673,30 @@
     xh, nk = HID // X // 2, DH // 128
     scratch = [
         vm(features.shape, BF16), vm(outer_masks.shape, jnp.int32), vm(inner_masks.shape, jnp.int32),
-        vm(class_weight.shape, BF16),
+        vm(class_weight.shape, BF16), vm(hidden_weight.shape, BF16),
+        vm((cap, NO), jnp.int32), vm((2, NO), jnp.int32), vm((1, labels.shape[0]), jnp.int32),
         vm((8, NO), F32), vm((Z, 8, NO), F32), vm((Q, 8, LW), F32), vm((Q, 8, LW), F32),
         vm((X, Q * 8, LW), BF16), vm((rows, X * hop), BF16), vm((rows, X * hop), BF16),
         vm((16, DH), BF16), vm((C, 16, DH), BF16), vm((Z, X, C, 16, D), BF16),
         *[vm((nk, Z, cap * Q, DH // nk), BF16)] * 2, *[vm((nk, Q, cap * Z, DH // nk), BF16)] * 2,
         *[vm((nk, Q, cap * Z, DH // nk), BF16)] * 2, *[vm((nk, Z, cap * Q, DH // nk), BF16)] * 2,
         vm((cap * NO, cap * NO), BF16), vm((cap * NO, cap * NO), BF16), vm((hop, hop), BF16), vm((hop, hop), BF16),
-        vm((2, hop, DH), BF16), vm((hop, DH), BF16), vm((hop, HID), F32), vm((hop, HID), BF16), vm((hop, HID), BF16),
+        vm((2, hop, DH), BF16), vm((hop, DH), BF16), vm((hop, HID), F32), vm((HID, hop), BF16), vm((HID, hop), BF16),
+        vm((hop, HID), BF16),
         vm((X * Z, Q * half, xh), BF16), vm((X * Z, Q * half, xh), BF16),
-        vm((Q, X, Z * half, xh), BF16), vm((Q, X, Z * half, xh), BF16),
-        vm((Q, Z * half, HH), BF16), vm((Q, Z * half, HH), BF16),
+        *[vm((2, Q, 2, Z * half, xh), BF16)] * 2, *[vm((2, Q, Z * half, 2 * xh), BF16)] * 2,
         vm((X * Z, Q * half, xh), BF16), vm((X * Z, Q * half, xh), BF16),
-        vm((X, Z, YL * 16, DH), BF16), *[vm((Z // 2, YL * 16, DH), BF16)] * 4, *[vm((Z, YL * 16, DH), BF16)] * 2,
-        vm((Z, YL * 16, DH), BF16), vm((Z, YL * 16, DH), BF16),
+        vm((nk, X, Z, YL * 16, DH // nk), BF16), *[vm((nk, Z // 2, YL * 16, DH // nk), BF16)] * 4,
+        *[vm((nk, Z, YL * 16, DH // nk), BF16)] * 4,
         vm((YL, 16, DH), BF16), vm((Y, 16, DH), BF16), vm((C, 8, DH), F32), vm((C, 8, DH), F32),
-        vm((X * C, CP, cw), BF16), vm((X * C, CP, cw), BF16), vm((nb, cb, cw), BF16), vm((Z, cb, cw), BF16),
-        vm((cb, cw), BF16), vm((Y, cb, cw), BF16), vm((cb, cw), BF16), vm((nb, cb, cw), BF16),
+        vm((X * C, CP, cw), BF16), vm((X * C, CP, cw), BF16), vm((nb, cb, cw), BF16), vm((Y, cb, cw), BF16),
+        vm((cb, cw), BF16), vm((Z, cb, cw), BF16), vm((cb, cw), BF16), vm((nb, cb, cw), BF16),
         vm((X * C, nb, cb, cw), BF16),
-        dma((4,)),
+        dma((8,)),
         *[dma] * 6,
         dma((Y,)), dma((C,)), *[dma] * 6,
-        *[dma((nk,))] * 8, *[dma] * 8,
-        *[dma] * 4, dma((6,)), dma((6,)), dma, dma, dma((YL,)), dma, dma((X * C,)), dma((C,)),
+        *[dma((nk,))] * 8, *[dma((2,))] * 6, dma, dma,
+        *[dma] * 4, dma((nk, 6)), dma((nk, 6)), dma((nk,)), dma((nk,)), dma((YL,)), dma, dma((X * C,)), dma((C,)),
         *[dma] * 10,
     ]
     hbm = pl.BlockSpec(memory_space=pl.ANY)
@@ -643,10 +706,10 @@
         functools.partial(kernel, dims),
         out_shape=(
             jax.ShapeDtypeStruct(hidden_weight.shape, F32),
-            jax.ShapeDtypeStruct((CP, HID), BF16),
+            jax.ShapeDtypeStruct((X * C, CP, cw), BF16),
             jax.ShapeDtypeStruct((rows, HID // X), BF16),
         ),
-        in_specs=[hbm, vmem, hbm, vmem, vmem, smem, hbm, smem, hbm, vmem],
+        in_specs=[hbm, hbm, hbm, hbm, hbm, smem, hbm, smem, hbm, hbm],
         out_specs=(vmem, vmem, vmem),
         scratch_shapes=scratch,
         compiler_params=pltpu.CompilerParams(
@@ -657,7 +720,18 @@
         features, hidden_weight, class_weight, request_ids.T, request_counts.T,
         outer_tiles, outer_masks, inner_tiles, inner_masks, labels.reshape(1, -1),
     )
-    return hidden_grad, class_grad[:classes].astype(F32), node_grad
+    return pl.pallas_call(
+        functools.partial(finish, (X, C, classes)),
+        out_shape=(
+            jax.ShapeDtypeStruct(hidden_grad.shape, F32),
+            jax.ShapeDtypeStruct(class_weight.shape, F32),
+            jax.ShapeDtypeStruct(node_grad.shape, BF16),
+        ),
+        in_specs=[hbm] * 3,
+        out_specs=(hbm,) * 3,
+        scratch_shapes=[vm((X * C, CP, cw), BF16), vm(class_weight.shape, F32), dma((4,))],
+        cost_estimate=pl.CostEstimate(flops=0, bytes_accessed=1_300_000, transcendentals=0),
+    )(hidden_grad, class_grad, node_grad)
 
 
 def solution(mesh):

time: 89.3 us -> 94.3 us (1.056)
  Pallas kernels: 84.6 us -> 93.5 us
  other arithmetic: 1.91 us -> 0 us
  local copies, waits for them, and re-layouts: 1.27 us -> 0 us
    pallas_call x0 -> x1, Pallas kernels: none -> 5.86 us  [on_device(): pl.pallas_call(functools.partial(finish, (X, C, classes)), out_shape=(jax...]
    pallas_call x1, Pallas kernels: 84.6 us -> 87.7 us  [on_device(): pl.pallas_call(functools.partial(kernel, dims), out_shape=(jax.ShapeDtype...]
    convert_element_type x1 -> x0, other arithmetic: 1.91 us -> none  [on_device(): return (hidden_grad, class_grad[:classes].astype(F32), node_grad)]
    unnamed x6 -> x0, local copies, waits for them, and re-layouts: 1.27 us -> none
where the time goes in v4:
time: 94.3 us; the launch traced here: 94.2 us
  Pallas kernels  93.5 us (99%)
    pallas_call x1, Pallas kernels, on_device(): pl.pallas_call(functools.partial(kernel, dims), out_shape=(jax.ShapeDtype...  87.7 us
    pallas_call x1, Pallas kernels, on_device(): pl.pallas_call(functools.partial(finish, (X, C, classes)), out_shape=(jax...  5.86 us

profile of v4, /device:TPU:1, one launch (start us, length us, event | category | flops | bytes accessed | tf_op | source)
XLA Modules:
  0.0 94.2 jit_solution(16441912109611123380)
XLA Ops:
  0.6 87.7 %shard_map.121 = (f32[8,768]{1,0:T(8,128)}, bf16[8,160,128]{2,1,0:T(8,128)(2,1)}, bf16[256,256]{1,0:T(8,128)(2,1)}) custom-call(bf16[256,768]{1,0:T(8,128)(2,1)} %feat_hbm.1, bf16[8,768]{1,0:T(8,128)(2,1)} %weight_hbm.1, bf16[153,1024]{1,0:T(8,128)(2,1)} %cls_hbm.1, s32[4,128]{1,0:T(4,128)} %bitcast.3, s32[2,128]{1,0:T(2,128)} %bitcast.4, s32[2,2]{1,0:T(2,128)} %otile_ref.1, ...), custom_call_target="tpu_custom_call" | custom-call | flops 2000000000 | bytes 3000000 | tf_op jit(solution)/shard_map/pallas_call | solution.py:705
  88.3 5.9 %shard_map.122 = (f32[8,768]{1,0:T(8,128)}, f32[153,1024]{1,0:T(8,128)}, bf16[256,256]{1,0:T(8,128)(2,1)}) custom-call(f32[8,768]{1,0:T(8,128)} %get-tuple-element.6.hidden_in, bf16[8,160,128]{2,1,0:T(8,128)(2,1)} %get-tuple-element.7.class_in, bf16[256,256]{1,0:T(8,128)(2,1)} %get-tuple-element.8.node_in), custom_call_target="tpu_custom_call" | custom-call | bytes 1300000 | tf_op jit(solution)/shard_map/pallas_call | solution.py:723

commit v5 on v4

--- a/solution.py
+++ b/solution.py
@@ -97,7 +97,7 @@
         def step(i, carry):
             body(i)
             return carry
-        lax.fori_loop(1, n, step, 0)
+        lax.fori_loop(1, n, step, 0, unroll=True)
 
     class Exchange:
         def __init__(self, n, me, at, src, dst, bulk, ss, rs):
@@ -187,7 +187,7 @@
             def _():
                 act(t)
             return carry
-        lax.fori_loop(0, Y, step, 0)
+        lax.fori_loop(0, Y, step, 0, unroll=True)
 
     w1_each(lambda t: w1_copy(t).start())
     y_mine = x * C + c
@@ -363,8 +363,7 @@
         return lax.bitwise_and(x + X - d, jnp.full_like(d, X - 1))
 
     place_a[...] = places(
-        plane(quo(s, half * Z * 2 * Q) * 2 + rem(quo(s, half * Z), 2)),
-        rem(s, half), rem(quo(s, half), Z), rem(quo(s, half * Z * 2), Q)
+        plane(rem(quo(s, half * Z), X)), rem(s, half), rem(quo(s, half), Z), quo(s, half * Z * X)
     )
     place_b[...] = places(
         plane(quo(s, half * Q * Z)), rem(s, half), rem(quo(s, half * Q), Z), rem(quo(s, half), Q)
@@ -413,14 +412,12 @@
     diff[...] = hidden_diff.astype(BF16)
     xw = HID // X
     xh = xw // 2
-    pair = 2 * Z
-
-    def xz_leg(group, src, dst, ss, rs):
-        def step(t, carry):
-            d, zz = 2 * group + t // Z, lax.bitwise_and(z + t, Z - 1)
+
+    def xz_leg(src, dst, ss, rs):
+        def send(t):
+            d, zz = t // Z, lax.bitwise_and(z + t, Z - 1)
             copy(src(d, zz), dst.at[d * Z + z], ss, rs, zz, q, lax.bitwise_and(x + d, X - 1)).start()
-            return carry
-        lax.fori_loop(0 if group else 1, pair, step, 0)
+        each(X * Z, send)
 
     def wait_blocks(ref, n, ss, rs):
         some = ref.at[pl.ds(0, n)]
@@ -428,23 +425,16 @@
 
     for t in range(X):
         na1s[t * Z:(t + 1) * Z] = diff[:, t * xw:t * xw + xh].reshape(Z, Q * half, xh)
-    for d in range(X):
-        cols = pl.ds(pl.multiple_of(lax.bitwise_and(x + d, X - 1) * xw + xh, xh), xh)
-        nb1s[d // 2, :, :, (d % 2) * xh:(d % 2 + 1) * xh] = (
-            dot(swap_a[...], diff[:, cols]).astype(BF16).reshape(Q, Z * half, xh))
-    ex_nb1 = [
-        along_q(lambda t, g=g: nb1s.at[g, t], lambda f, g=g: nb1r.at[g, f], blocks(nb1r.at[g], Q), nb1_ss.at[g], nb1_rs.at[g])
-        for g in range(2)
-    ]
-    ex_na2 = [
-        along_q(lambda t, g=g: na2s.at[g, t], lambda f, g=g: na2r.at[g, f], blocks(na2r.at[g], Q), na2_ss.at[g], na2_rs.at[g])
-        for g in range(2)
-    ]
-    for g in range(2):
-        xz_leg(g, lambda d, zz: na1s.at[lax.bitwise_and(x + d, X - 1) * Z + zz], na1r, na1_ss.at[g], na1_rs.at[g])
-        ex_nb1[g].start()
-        nb1r[g, q] = nb1s[g, q]
+    xz_leg(lambda d, zz: na1s.at[lax.bitwise_and(x + d, X - 1) * Z + zz], na1r, na1_ss, na1_rs)
+    second = jnp.concatenate([
+        diff[:, pl.ds(pl.multiple_of(lax.bitwise_and(x + d, X - 1) * xw + xh, xh), xh)] for d in range(X)
+    ], axis=1)
+    nb1s[...] = dot(swap_a[...], second).astype(BF16).reshape(nb1s.shape)
+    ex_nb1 = along_q(lambda t: nb1s.at[t], lambda f: nb1r.at[f], blocks(nb1r, Q), nb1_ss, nb1_rs)
+    ex_nb1.start()
+    ex_na2 = along_q(lambda t: na2s.at[t], lambda f: na2r.at[f], blocks(na2r, Q), na2_ss, na2_rs)
     na1r[z] = na1s[x * Z + z]
+    nb1r[q] = nb1s[q]
 
     def total(ref, n):
         acc = ref[0].astype(F32)
@@ -456,9 +446,10 @@
     ga.wait_recv()
     g0.wait_recv()
     gmine = (gmine + dot(pgtr[...], agr[...])).astype(BF16).reshape(Z, X, YL * 16, DH)
-    for k in range(chunks):
+    parts, span = gs1.shape[0], gs1.shape[4]
+    for k in range(parts):
         for t in range(X):
-            gs1[k, t] = gmine[:, t, :, k * wide:(k + 1) * wide]
+            gs1[k, t] = gmine[:, t, :, k * span:(k + 1) * span]
     right, left, across = (lax.bitwise_and(x + d, X - 1) for d in (1, X - 1, 2))
     lower, upper = pl.ds(0, Z // 2), pl.ds(Z // 2, Z // 2)
 
@@ -469,8 +460,8 @@
         g1(k, 0, gs1.at[k, across, lower], gra.at[k], right), g1(k, 1, gs1.at[k, across, upper], grb.at[k], left),
         g1(k, 2, gs1.at[k, right, upper], grl.at[k, upper], right), g1(k, 3, gs1.at[k, left, lower], grr.at[k, lower], left),
         g1(k, 4, gsa.at[k], grl.at[k, lower], right), g1(k, 5, gsb.at[k], grr.at[k, upper], left),
-    ) for k in range(chunks)]
-    for k in range(chunks):
+    ) for k in range(parts)]
+    for k in range(parts):
         for one in ring[k][:4]:
             one.start()
 
@@ -483,7 +474,7 @@
             def _():
                 act(t)
             return carry
-        lax.fori_loop(0, nb, step, 0)
+        lax.fori_loop(0, nb, step, 0, unroll=True)
 
     to_blocks(lambda t: copy(cs2.at[t], cr2.at[y], c2_ss, c2_rs, z, t * C + c, x).start())
     summing = y < nb
@@ -491,7 +482,7 @@
     ex_c3 = along_z(lambda t: cs3, lambda f: cr3.at[f], blocks(cr3, Z), c3_ss, c3_rs)
     ex_c4 = along_y(lambda t: cfin, lambda f: ca4.at[f], blocks(cr2, Y), c4_ss, c4_rs)
 
-    for k in range(chunks):
+    for k in range(parts):
         r1, l1, r2, l2, r3, l3 = ring[k]
         r1.wait_recv()
         gsa[k] = (gs1[k, right, lower].astype(F32) + gra[k].astype(F32)).astype(BF16)
@@ -500,19 +491,18 @@
         gsb[k] = (gs1[k, left, upper].astype(F32) + grb[k].astype(F32)).astype(BF16)
         l3.start()
 
-    for g in range(2):
-        wait_blocks(na1r, pair if g else pair - 1, na1_ss.at[g], na1_rs.at[g]).wait_recv()
-        came = jnp.concatenate([na1r[d * Z:(d + 1) * Z].reshape(hop, xh) for d in (2 * g, 2 * g + 1)], axis=1)
-        came = dot(swap_a[...], came).astype(BF16)
-        for t in range(2):
-            na2s[g, :, t] = came[:, t * xh:(t + 1) * xh].reshape(Q, Z * half, xh)
-        ex_na2[g].start()
-        na2r[g, q] = na2s[g, q]
-        ex_nb1[g].recv()
-        came = dot(swap_b[...], nb1r[g].reshape(hop, 2 * xh)).astype(BF16)
-        for t in range(2):
-            nb2s[(2 * g + t) * Z:(2 * g + t + 1) * Z] = came[:, t * xh:(t + 1) * xh].reshape(Z, Q * half, xh)
-        xz_leg(g, lambda d, zz: nb2s.at[d * Z + zz], nb2r, nb2_ss, nb2_rs)
+    wait_blocks(na1r, X * Z - 1, na1_ss, na1_rs).wait_recv()
+    came = jnp.concatenate([na1r[d * Z:(d + 1) * Z].reshape(hop, xh) for d in range(X)], axis=1)
+    came = dot(swap_a[...], came).astype(BF16)
+    for d in range(X):
+        na2s[:, d] = came[:, d * xh:(d + 1) * xh].reshape(Q, Z * half, xh)
+    ex_na2.start()
+    na2r[q] = na2s[q]
+    ex_nb1.recv()
+    came = dot(swap_b[...], nb1r[...].reshape(hop, X * xh)).astype(BF16)
+    for d in range(X):
+        nb2s[d * Z:(d + 1) * Z] = came[:, d * xh:(d + 1) * xh].reshape(Z, Q * half, xh)
+    xz_leg(lambda d, zz: nb2s.at[d * Z + zz], nb2r, nb2_ss, nb2_rs)
     nb2r[z] = nb2s[z]
 
     @pl.when(summing)
@@ -524,7 +514,7 @@
         cr3[z] = cs3[...]
 
     ex_g2 = []
-    for k in range(chunks):
+    for k in range(parts):
         for one in ring[k][2:]:
             one.wait_recv()
         gs2[k] = (gs1[k, x].astype(F32) + grl[k].astype(F32) + grr[k].astype(F32)).astype(BF16)
@@ -540,9 +530,9 @@
         ex_c4.start()
         ca4[y] = cfin[...]
 
-    for k in range(chunks):
+    for k in range(parts):
         ex_g2[k].recv()
-        gs3[:, :, k * wide:(k + 1) * wide] = total(gr2.at[k], Z).astype(BF16).reshape(YL, 16, wide)
+        gs3[:, :, k * span:(k + 1) * span] = total(gr2.at[k], Z).astype(BF16).reshape(YL, 16, span)
 
     def g3_copy(yl):
         return copy(gs3.at[yl], gr3.at[y], g3_ss.at[yl], g3_rs, z, (x * YL + yl) * C + c, x)
@@ -566,8 +556,7 @@
     ex_c5.start()
     ca5[me_xc] = ca4[...]
 
-    for g in range(2):
-        ex_na2[g].recv()
+    ex_na2.recv()
     node_out[:, :xh] = dot(place_a[...], na2r[...].reshape(X * hop, xh)).astype(BF16)
 
     def g4_copy(xx, cc):
@@ -589,11 +578,14 @@
 
     g4_each(lambda xx, cc: g4_copy(xx, cc).start())
 
-    wait_blocks(nb2r, 2 * pair - 1, nb2_ss, nb2_rs).wait_recv()
+    wait_blocks(nb2r, X * Z - 1, nb2_ss, nb2_rs).wait_recv()
     node_out[:, xh:] = dot(place_b[...], nb2r[...].reshape(X * hop, xh)).astype(BF16)
 
     ex_c5.recv()
-    class_out[...] = ca5[...].reshape(class_out.shape)
+    for t in range(X):
+        for cc in range(C):
+            at = cc * HH + t * cw
+            class_out[:, at:at + cw] = ca5[t * C + cc].reshape(CP, cw).astype(F32)[:classes]
 
     for cc in range(C):
         @pl.when(jnp.logical_not(owning & (c == cc)))
@@ -601,14 +593,13 @@
             copy(gs4.at[0], gr4.at[cc], g4_ss.at[0], g4_rs.at[cc], z, y * C + cc, y // YL).wait_recv()
         hidden_out[:, cc * DH:(cc + 1) * DH] = gr4[cc]
 
-    for ex in (ex_i1, ex_i2, ex_wx, ex_w2, ex_w3, *ex_fa1, *ex_fb1, *ex_fa2, *ex_fb2, *ex_nb1, *ex_na2, *ex_g2, ex_c1, ex_c5):
+    for ex in (ex_i1, ex_i2, ex_wx, ex_w2, ex_w3, *ex_fa1, *ex_fb1, *ex_fa2, *ex_fb2, ex_nb1, ex_na2, *ex_g2, ex_c1, ex_c5):
         ex.sent()
     w1_each(lambda t: w1_copy(t).wait_send())
     for one in (w4, ga, g0, *[leg for legs in ring for leg in legs]):
         one.wait_send()
-    for g in range(2):
-        wait_blocks(na1r, pair if g else pair - 1, na1_ss.at[g], na1_rs.at[g]).wait_send()
-    wait_blocks(nb2r, 2 * pair - 1, nb2_ss, nb2_rs).wait_send()
+    wait_blocks(na1r, X * Z - 1, na1_ss, na1_rs).wait_send()
+    wait_blocks(nb2r, X * Z - 1, nb2_ss, nb2_rs).wait_send()
 
     @pl.when(summing)
     def _():
@@ -626,28 +617,6 @@
         def _():
             g3_copy(yl).wait_send()
     g4_each(lambda xx, cc: g4_copy(xx, cc).wait_send())
-
-
-def finish(class_dims, hidden_in, class_in, node_in, hidden_out, class_out, node_out, parts, spread, sem):
-    X, C, classes = class_dims
-    passed = [
-        pltpu.make_async_copy(class_in, parts, sem.at[0]),
-        pltpu.make_async_copy(hidden_in, hidden_out, sem.at[1]),
-        pltpu.make_async_copy(node_in, node_out, sem.at[2]),
-    ]
-    for one in passed:
-        one.start()
-    passed[0].wait()
-    cw = parts.shape[2]
-    for t in range(X):
-        for c in range(C):
-            at = (c * X + t) * cw
-            spread[:, at:at + cw] = parts[t * C + c].astype(F32)[:classes]
-    last = pltpu.make_async_copy(spread, class_out, sem.at[3])
-    last.start()
-    for one in passed[1:]:
-        one.wait()
-    last.wait()
 
 
 def on_device(
@@ -670,7 +639,7 @@
     LW = max(Z * 8, 128)
     dims = (Z, Y, C, X, cap, tile, rows, classes)
     vm, dma = pltpu.VMEM, pltpu.SemaphoreType.DMA
-    xh, nk = HID // X // 2, DH // 128
+    xh, nk, gk = HID // X // 2, DH // 128, 1
     scratch = [
         vm(features.shape, BF16), vm(outer_masks.shape, jnp.int32), vm(inner_masks.shape, jnp.int32),
         vm(class_weight.shape, BF16), vm(hidden_weight.shape, BF16),
@@ -684,10 +653,10 @@
         vm((2, hop, DH), BF16), vm((hop, DH), BF16), vm((hop, HID), F32), vm((HID, hop), BF16), vm((HID, hop), BF16),
         vm((hop, HID), BF16),
         vm((X * Z, Q * half, xh), BF16), vm((X * Z, Q * half, xh), BF16),
-        *[vm((2, Q, 2, Z * half, xh), BF16)] * 2, *[vm((2, Q, Z * half, 2 * xh), BF16)] * 2,
+        *[vm((Q, X, Z * half, xh), BF16)] * 2, *[vm((Q, Z * half, HH), BF16)] * 2,
         vm((X * Z, Q * half, xh), BF16), vm((X * Z, Q * half, xh), BF16),
-        vm((nk, X, Z, YL * 16, DH // nk), BF16), *[vm((nk, Z // 2, YL * 16, DH // nk), BF16)] * 4,
-        *[vm((nk, Z, YL * 16, DH // nk), BF16)] * 4,
+        vm((gk, X, Z, YL * 16, DH // gk), BF16), *[vm((gk, Z // 2, YL * 16, DH // gk), BF16)] * 4,
+        *[vm((gk, Z, YL * 16, DH // gk), BF16)] * 4,
         vm((YL, 16, DH), BF16), vm((Y, 16, DH), BF16), vm((C, 8, DH), F32), vm((C, 8, DH), F32),
         vm((X * C, CP, cw), BF16), vm((X * C, CP, cw), BF16), vm((nb, cb, cw), BF16), vm((Y, cb, cw), BF16),
         vm((cb, cw), BF16), vm((Z, cb, cw), BF16), vm((cb, cw), BF16), vm((nb, cb, cw), BF16),
@@ -695,18 +664,18 @@
         dma((8,)),
         *[dma] * 6,
         dma((Y,)), dma((C,)), *[dma] * 6,
-        *[dma((nk,))] * 8, *[dma((2,))] * 6, dma, dma,
-        *[dma] * 4, dma((nk, 6)), dma((nk, 6)), dma((nk,)), dma((nk,)), dma((YL,)), dma, dma((X * C,)), dma((C,)),
+        *[dma((nk,))] * 8, *[dma] * 8,
+        *[dma] * 4, dma((gk, 6)), dma((gk, 6)), dma((gk,)), dma((gk,)), dma((YL,)), dma, dma((X * C,)), dma((C,)),
         *[dma] * 10,
     ]
     hbm = pl.BlockSpec(memory_space=pl.ANY)
     vmem = pl.BlockSpec(memory_space=pltpu.VMEM)
     smem = pl.BlockSpec(memory_space=pltpu.SMEM)
-    hidden_grad, class_grad, node_grad = pl.pallas_call(
+    return pl.pallas_call(
         functools.partial(kernel, dims),
         out_shape=(
             jax.ShapeDtypeStruct(hidden_weight.shape, F32),
-            jax.ShapeDtypeStruct((X * C, CP, cw), BF16),
+            jax.ShapeDtypeStruct(class_weight.shape, F32),
             jax.ShapeDtypeStruct((rows, HID // X), BF16),
         ),
         in_specs=[hbm, hbm, hbm, hbm, hbm, smem, hbm, smem, hbm, hbm],
@@ -720,18 +689,6 @@
         features, hidden_weight, class_weight, request_ids.T, request_counts.T,
         outer_tiles, outer_masks, inner_tiles, inner_masks, labels.reshape(1, -1),
     )
-    return pl.pallas_call(
-        functools.partial(finish, (X, C, classes)),
-        out_shape=(
-            jax.ShapeDtypeStruct(hidden_grad.shape, F32),
-            jax.ShapeDtypeStruct(class_weight.shape, F32),
-            jax.ShapeDtypeStruct(node_grad.shape, BF16),
-        ),
-        in_specs=[hbm] * 3,
-        out_specs=(hbm,) * 3,
-        scratch_shapes=[vm((X * C, CP, cw), BF16), vm(class_weight.shape, F32), dma((4,))],
-        cost_estimate=pl.CostEstimate(flops=0, bytes_accessed=1_300_000, transcendentals=0),
-    )(hidden_grad, class_grad, node_grad)
 
 
 def solution(mesh):

time: 94.3 us -> 89.6 us (0.950)
  Pallas kernels: 93.5 us -> 84.6 us
  local copies, waits for them, and re-layouts: 0 us -> 4.03 us
    pallas_call x1 -> x0, Pallas kernels: 5.86 us -> none  [on_device(): pl.pallas_call(functools.partial(finish, (X, C, classes)), out_shape=(jax...]
    unnamed x0 -> x5, local copies, waits for them, and re-layouts: none -> 4.03 us
    pallas_call x1, Pallas kernels: 87.7 us -> 84.6 us  [on_device(): pl.pallas_call(functools.partial(kernel, dims), out_shape=(jax.ShapeDtype...]
where the time goes in v5:
time: 89.6 us; the launch traced here: 89.3 us
  Pallas kernels  84.6 us (94%)
  local copies, waits for them, and re-layouts  4.03 us (4%)
    pallas_call x1, Pallas kernels, on_device(): pl.pallas_call(functools.partial(kernel, dims), out_shape=(jax.ShapeDtype...  84.6 us
    unnamed x5, local copies, waits for them, and re-layouts  4.03 us

profile of v5, /device:TPU:1, one launch (start us, length us, event | category | flops | bytes accessed | tf_op | source)
XLA Modules:
  0.0 89.3 jit_solution(2407587437237812018)
XLA Ops:
  0.6 84.6 %shard_map.121 = (f32[8,768]{1,0:T(8,128)}, f32[153,1024]{1,0:T(8,128)}, bf16[256,256]{1,0:T(8,128)(2,1)}) custom-call(bf16[256,768]{1,0:T(8,128)(2,1)} %feat_hbm.1, bf16[8,768]{1,0:T(8,128)(2,1)} %weight_hbm.1, bf16[153,1024]{1,0:T(8,128)(2,1)} %cls_hbm.1, s32[4,128]{1,0:T(4,128)} %bitcast.3, s32[2,128]{1,0:T(2,128)} %bitcast.4, s32[2,2]{1,0:T(2,128)} %otile_ref.1, ...), custom_call_target="tpu_custom_call" | custom-call | flops 2000000000 | bytes 3000000 | tf_op jit(solution)/shard_map/pallas_call | solution.py:674
  85.3 1.3 %copy.16 = f32[8,768]{1,0:T(8,128)} copy(f32[8,768]{1,0:T(8,128)} %get-tuple-element.6) | data formatting | bytes 49152
  86.6 0.0 copy-start
  86.6 2.0 %copy.17 = f32[153,1024]{1,0:T(8,128)} copy(f32[153,1024]{1,0:T(8,128)} %get-tuple-element.7) | data formatting | bytes 1253376
  88.7 0.0 copy-done
  88.7 0.7 copy.18
Async XLA Ops:
  86.6 2.0 %copy-start = (bf16[256,256]{1,0:T(8,128)(2,1)S(1)}, bf16[256,256]{1,0:T(8,128)(2,1)}, u32[]{:S(2)}) copy-start(bf16[256,256]{1,0:T(8,128)(2,1)} %get-tuple-element.8) | copy-start | bytes 393220

commit v6 on v5

--- a/solution.py
+++ b/solution.py
@@ -55,14 +55,14 @@
     agg, agr, pre, pgt, pgtr, diff,
     na1s, na1r, na2s, na2r, nb1s, nb1r, nb2s, nb2r,
     gs1, gra, grb, gsa, gsb, grl, grr, gs2, gr2, gs3, gr3, gs4, gr4,
-    cs1, cr1, cs2, cr2, cs3, cr3, cfin, ca4, ca5,
+    cmine, cs0, cr0, cs1, cr1, cs2, cr2, cs3, cr3, cfin, ca4, ca5, ca6,
     local_sem,
     i1_ss, i1_rs, i2_ss, i2_rs, wx_ss, wx_rs,
     w1_ss, w1_rs, w2_ss, w2_rs, w3_ss, w3_rs, w4_ss, w4_rs,
     fa1_ss, fa1_rs, fa2_ss, fa2_rs, fb1_ss, fb1_rs, fb2_ss, fb2_rs,
     na1_ss, na1_rs, na2_ss, na2_rs, nb1_ss, nb1_rs, nb2_ss, nb2_rs,
     ga_ss, ga_rs, g0_ss, g0_rs, g1_ss, g1_rs, g2_ss, g2_rs, g3_ss, g3_rs, g4_ss, g4_rs,
-    c1_ss, c1_rs, c2_ss, c2_rs, c3_ss, c3_rs, c4_ss, c4_rs, c5_ss, c5_rs,
+    c0_ss, c0_rs, c1_ss, c1_rs, c2_ss, c2_rs, c3_ss, c3_rs, c4_ss, c4_rs, c5_ss, c5_rs, c6_ss, c6_rs,
 ):
     Z, Y, C, X, cap, tile, rows, classes = dims
     Q = Y * C
@@ -97,7 +97,7 @@
         def step(i, carry):
             body(i)
             return carry
-        lax.fori_loop(1, n, step, 0, unroll=True)
+        lax.fori_loop(1, n, step, 0)
 
     class Exchange:
         def __init__(self, n, me, at, src, dst, bulk, ss, rs):
@@ -130,12 +130,6 @@
     def along_x(*rest):
         return Exchange(X, x, lambda t: (z, q, t), *rest)
 
-    def along_xz(*rest):
-        return Exchange(X * Z, x * Z + z, lambda t: (lax.bitwise_and(t, Z - 1), q, t // Z), *rest)
-
-    def along_xc(*rest):
-        return Exchange(X * C, x * C + c, lambda t: (z, y * C + lax.bitwise_and(t, C - 1), t // C), *rest)
-
     def blocks(ref, n):
         return ref.at[pl.ds(0, n - 1)]
 
@@ -155,13 +149,9 @@
     def greet(zz, qq, xx):
         pl.semaphore_signal(barrier, inc=1, device_id=(zz * Q + qq, xx), device_id_type=MESH)
 
-    def greet_xz(d):
-        t = lax.bitwise_and(x * Z + z + d, X * Z - 1)
-        greet(lax.bitwise_and(t, Z - 1), q, t // Z)
-
+    each(Z, lambda d: greet(lax.bitwise_and(z + d, Z - 1), q, x))
     each(Q, lambda d: greet(z, lax.bitwise_and(q + d, Q - 1), x))
-    each(X * Z, greet_xz)
-    each(X, lambda d: greet(z, y * C + sib, lax.bitwise_and(x + d, X - 1)))
+    each(X, lambda d: greet(z, q, lax.bitwise_and(x + d, X - 1)))
 
     i1s[...] = jnp.zeros_like(i1s)
     for load in loads[:2]:
@@ -170,7 +160,7 @@
     w32 = weight_ref[...].astype(F32)
     ws[...] = jnp.concatenate([w32[:, :DH], w32[:, DH:]], axis=0).astype(BF16)
 
-    pl.semaphore_wait(barrier, (Q - 1) + (X * Z - 1) + (X - 1))
+    pl.semaphore_wait(barrier, (Z - 1) + (Q - 1) + (X - 1))
 
     ex_i1 = along_z(lambda t: i1s, lambda f: i1r.at[f], blocks(i1r, Z), i1_ss, i1_rs)
     ex_i1.start()
@@ -187,7 +177,7 @@
             def _():
                 act(t)
             return carry
-        lax.fori_loop(0, Y, step, 0, unroll=True)
+        lax.fori_loop(0, Y, step, 0)
 
     w1_each(lambda t: w1_copy(t).start())
     y_mine = x * C + c
@@ -363,7 +353,7 @@
         return lax.bitwise_and(x + X - d, jnp.full_like(d, X - 1))
 
     place_a[...] = places(
-        plane(rem(quo(s, half * Z), X)), rem(s, half), rem(quo(s, half), Z), quo(s, half * Z * X)
+        plane(quo(s, half * Z * Q)), rem(s, half), rem(quo(s, half), Z), rem(quo(s, half * Z), Q)
     )
     place_b[...] = places(
         plane(quo(s, half * Q * Z)), rem(s, half), rem(quo(s, half * Q), Z), rem(quo(s, half), Q)
@@ -391,16 +381,6 @@
     exponent = jnp.exp(logits - jnp.max(logits, axis=1, keepdims=True))
     softmax = exponent / jnp.sum(exponent, axis=1, keepdims=True)
     logit_grad = ((softmax - one_hot) / seeds).astype(BF16)
-    widen = flag(iota((classes, CP), 0) == iota((classes, CP), 1))
-    class_rows = dot(dot(logit_grad, widen).astype(BF16), agg_two, 0, 0).astype(BF16)
-    for t in range(X):
-        for cc in range(C):
-            cs1[t * C + cc] = class_rows[:, cc * HH + t * cw:cc * HH + (t + 1) * cw]
-    me_xc = x * C + c
-    ex_c1 = along_xc(lambda t: cs1.at[t], lambda f: cr1.at[f], blocks(cr1, X * C), c1_ss, c1_rs)
-    ex_c1.start()
-    cr1[me_xc] = cs1[me_xc]
-
     agg_grad = dot(logit_grad, cls[...]) / inner_degree
     high = agg_grad.astype(BF16)
     low = (agg_grad - high.astype(F32)).astype(BF16)
@@ -412,29 +392,34 @@
     diff[...] = hidden_diff.astype(BF16)
     xw = HID // X
     xh = xw // 2
-
-    def xz_leg(src, dst, ss, rs):
-        def send(t):
-            d, zz = t // Z, lax.bitwise_and(z + t, Z - 1)
-            copy(src(d, zz), dst.at[d * Z + z], ss, rs, zz, q, lax.bitwise_and(x + d, X - 1)).start()
-        each(X * Z, send)
-
-    def wait_blocks(ref, n, ss, rs):
-        some = ref.at[pl.ds(0, n)]
-        return copy(some, some, ss, rs, z, q, lax.bitwise_and(x + 1, X - 1))
-
     for t in range(X):
-        na1s[t * Z:(t + 1) * Z] = diff[:, t * xw:t * xw + xh].reshape(Z, Q * half, xh)
-    xz_leg(lambda d, zz: na1s.at[lax.bitwise_and(x + d, X - 1) * Z + zz], na1r, na1_ss, na1_rs)
-    second = jnp.concatenate([
-        diff[:, pl.ds(pl.multiple_of(lax.bitwise_and(x + d, X - 1) * xw + xh, xh), xh)] for d in range(X)
-    ], axis=1)
+        na1s[:, :, t * xh:(t + 1) * xh] = diff[:, t * xw:t * xw + xh].reshape(Z, Q * half, xh)
+    ex_na1 = along_z(lambda t: na1s.at[t], lambda f: na1r.at[f], blocks(na1r, Z), na1_ss, na1_rs)
+    ex_na1.start()
+    na1r[z] = na1s[z]
+    second = jnp.concatenate([diff[:, t * xw + xh:(t + 1) * xw] for t in range(X)], axis=1)
     nb1s[...] = dot(swap_a[...], second).astype(BF16).reshape(nb1s.shape)
     ex_nb1 = along_q(lambda t: nb1s.at[t], lambda f: nb1r.at[f], blocks(nb1r, Q), nb1_ss, nb1_rs)
     ex_nb1.start()
-    ex_na2 = along_q(lambda t: na2s.at[t], lambda f: na2r.at[f], blocks(na2r, Q), na2_ss, na2_rs)
-    na1r[z] = na1s[x * Z + z]
     nb1r[q] = nb1s[q]
+
+    def planes_leg(n, me, at, src, dst, ss, rs):
+        def send(t):
+            d, to = t // n, lax.bitwise_and(me + t, n - 1)
+            xx = lax.bitwise_and(x + d, X - 1)
+            copy(src.at[xx * n + to], dst.at[d * n + me], ss, rs, *at(to), xx).start()
+        each(X * n, send)
+
+    def planes_all(ref, ss, rs):
+        some = blocks(ref, ref.shape[0])
+        return copy(some, some, ss, rs, z, q, lax.bitwise_and(x + 1, X - 1))
+
+    widen = flag(iota((classes, CP), 0) == iota((classes, CP), 1))
+    class_rows = dot(dot(logit_grad, widen).astype(BF16), agg_two, 0, 0)
+    cs0[...] = jnp.where(c == 0, class_rows[:, HH:], class_rows[:, :HH]).astype(BF16)
+    c0 = to_sibling(cs0, cr0, c0_ss, c0_rs)
+    c0.start()
+    cmine[...] = jnp.where(c == 0, class_rows[:, :HH], class_rows[:, HH:])
 
     def total(ref, n):
         acc = ref[0].astype(F32)
@@ -465,8 +450,13 @@
         for one in ring[k][:4]:
             one.start()
 
-    ex_c1.recv()
-    cs2[...] = total(cr1, X * C).astype(BF16).reshape(cs2.shape)
+    c0.wait_recv()
+    cmine[...] = cmine[...] + cr0[...].astype(F32)
+    for t in range(X):
+        cs1[t] = cmine[:, t * cw:(t + 1) * cw].astype(BF16)
+    ex_c1 = along_x(lambda t: cs1.at[t], lambda f: cr1.at[f], blocks(cr1, X), c1_ss, c1_rs)
+    ex_c1.start()
+    cr1[x] = cs1[x]
 
     def to_blocks(act):
         def step(t, carry):
@@ -474,9 +464,8 @@
             def _():
                 act(t)
             return carry
-        lax.fori_loop(0, nb, step, 0, unroll=True)
-
-    to_blocks(lambda t: copy(cs2.at[t], cr2.at[y], c2_ss, c2_rs, z, t * C + c, x).start())
+        lax.fori_loop(0, nb, step, 0)
+
     summing = y < nb
     ex_c2 = along_y(None, None, blocks(cr2, Y), c2_ss, c2_rs)
     ex_c3 = along_z(lambda t: cs3, lambda f: cr3.at[f], blocks(cr3, Z), c3_ss, c3_rs)
@@ -491,19 +480,23 @@
         gsb[k] = (gs1[k, left, upper].astype(F32) + grb[k].astype(F32)).astype(BF16)
         l3.start()
 
-    wait_blocks(na1r, X * Z - 1, na1_ss, na1_rs).wait_recv()
-    came = jnp.concatenate([na1r[d * Z:(d + 1) * Z].reshape(hop, xh) for d in range(X)], axis=1)
-    came = dot(swap_a[...], came).astype(BF16)
-    for d in range(X):
-        na2s[:, d] = came[:, d * xh:(d + 1) * xh].reshape(Q, Z * half, xh)
-    ex_na2.start()
-    na2r[q] = na2s[q]
+    ex_na1.recv()
+    came = dot(swap_a[...], na1r[...].reshape(hop, X * xh)).astype(BF16)
+    for t in range(X):
+        na2s[t * Q:(t + 1) * Q] = came[:, t * xh:(t + 1) * xh].reshape(Q, Z * half, xh)
+    planes_leg(Q, q, lambda t: (z, t), na2s, na2r, na2_ss, na2_rs)
+    na2r[q] = na2s[x * Q + q]
+
+    ex_c1.recv()
+    cs2[...] = total(cr1, X).astype(BF16).reshape(cs2.shape)
+    to_blocks(lambda t: copy(cs2.at[t], cr2.at[y], c2_ss, c2_rs, z, t * C + c, x).start())
+
     ex_nb1.recv()
     came = dot(swap_b[...], nb1r[...].reshape(hop, X * xh)).astype(BF16)
-    for d in range(X):
-        nb2s[d * Z:(d + 1) * Z] = came[:, d * xh:(d + 1) * xh].reshape(Z, Q * half, xh)
-    xz_leg(lambda d, zz: nb2s.at[d * Z + zz], nb2r, nb2_ss, nb2_rs)
-    nb2r[z] = nb2s[z]
+    for t in range(X):
+        nb2s[t * Z:(t + 1) * Z] = came[:, t * xh:(t + 1) * xh].reshape(Z, Q * half, xh)
+    planes_leg(Z, z, lambda t: (t, q), nb2s, nb2r, nb2_ss, nb2_rs)
+    nb2r[z] = nb2s[x * Z + z]
 
     @pl.when(summing)
     def _():
@@ -552,11 +545,11 @@
     def _():
         copy(ca4, ca4, c4_ss, c4_rs, z, q, x).wait_recv()
 
-    ex_c5 = along_xc(lambda t: ca4, lambda f: ca5.at[f], blocks(ca5, X * C), c5_ss, c5_rs)
+    ex_c5 = along_x(lambda t: ca4, lambda f: ca5.at[f], blocks(ca5, X), c5_ss, c5_rs)
     ex_c5.start()
-    ca5[me_xc] = ca4[...]
-
-    ex_na2.recv()
+    ca5[x] = ca4[...]
+
+    planes_all(na2r, na2_ss, na2_rs).wait_recv()
     node_out[:, :xh] = dot(place_a[...], na2r[...].reshape(X * hop, xh)).astype(BF16)
 
     def g4_copy(xx, cc):
@@ -578,14 +571,12 @@
 
     g4_each(lambda xx, cc: g4_copy(xx, cc).start())
 
-    wait_blocks(nb2r, X * Z - 1, nb2_ss, nb2_rs).wait_recv()
+    ex_c5.recv()
+    c6 = to_sibling(ca5, ca6, c6_ss, c6_rs)
+    c6.start()
+
+    planes_all(nb2r, nb2_ss, nb2_rs).wait_recv()
     node_out[:, xh:] = dot(place_b[...], nb2r[...].reshape(X * hop, xh)).astype(BF16)
-
-    ex_c5.recv()
-    for t in range(X):
-        for cc in range(C):
-            at = cc * HH + t * cw
-            class_out[:, at:at + cw] = ca5[t * C + cc].reshape(CP, cw).astype(F32)[:classes]
 
     for cc in range(C):
         @pl.when(jnp.logical_not(owning & (c == cc)))
@@ -593,13 +584,19 @@
             copy(gs4.at[0], gr4.at[cc], g4_ss.at[0], g4_rs.at[cc], z, y * C + cc, y // YL).wait_recv()
         hidden_out[:, cc * DH:(cc + 1) * DH] = gr4[cc]
 
-    for ex in (ex_i1, ex_i2, ex_wx, ex_w2, ex_w3, *ex_fa1, *ex_fb1, *ex_fa2, *ex_fb2, ex_nb1, ex_na2, *ex_g2, ex_c1, ex_c5):
+    c6.wait_recv()
+    for t in range(X):
+        ours, theirs = ca5[t].reshape(CP, cw), ca6[t].reshape(CP, cw)
+        for cc in range(C):
+            class_out[:, cc * HH + t * cw:cc * HH + (t + 1) * cw] = jnp.where(c == cc, ours, theirs)
+
+    for ex in (ex_i1, ex_i2, ex_wx, ex_w2, ex_w3, *ex_fa1, *ex_fb1, *ex_fa2, *ex_fb2, ex_na1, ex_nb1, *ex_g2, ex_c1, ex_c5):
         ex.sent()
     w1_each(lambda t: w1_copy(t).wait_send())
-    for one in (w4, ga, g0, *[leg for legs in ring for leg in legs]):
+    for one in (w4, ga, g0, c0, c6, *[leg for legs in ring for leg in legs]):
         one.wait_send()
-    wait_blocks(na1r, X * Z - 1, na1_ss, na1_rs).wait_send()
-    wait_blocks(nb2r, X * Z - 1, nb2_ss, nb2_rs).wait_send()
+    planes_all(na2r, na2_ss, na2_rs).wait_send()
+    planes_all(nb2r, nb2_ss, nb2_rs).wait_send()
 
     @pl.when(summing)
     def _():
@@ -652,30 +649,30 @@
         vm((cap * NO, cap * NO), BF16), vm((cap * NO, cap * NO), BF16), vm((hop, hop), BF16), vm((hop, hop), BF16),
         vm((2, hop, DH), BF16), vm((hop, DH), BF16), vm((hop, HID), F32), vm((HID, hop), BF16), vm((HID, hop), BF16),
         vm((hop, HID), BF16),
-        vm((X * Z, Q * half, xh), BF16), vm((X * Z, Q * half, xh), BF16),
-        *[vm((Q, X, Z * half, xh), BF16)] * 2, *[vm((Q, Z * half, HH), BF16)] * 2,
+        *[vm((Z, Q * half, HH), BF16)] * 2, *[vm((X * Q, Z * half, xh), BF16)] * 2, *[vm((Q, Z * half, HH), BF16)] * 2,
         vm((X * Z, Q * half, xh), BF16), vm((X * Z, Q * half, xh), BF16),
         vm((gk, X, Z, YL * 16, DH // gk), BF16), *[vm((gk, Z // 2, YL * 16, DH // gk), BF16)] * 4,
         *[vm((gk, Z, YL * 16, DH // gk), BF16)] * 4,
         vm((YL, 16, DH), BF16), vm((Y, 16, DH), BF16), vm((C, 8, DH), F32), vm((C, 8, DH), F32),
-        vm((X * C, CP, cw), BF16), vm((X * C, CP, cw), BF16), vm((nb, cb, cw), BF16), vm((Y, cb, cw), BF16),
+        vm((CP, HH), F32), vm((CP, HH), BF16), vm((CP, HH), BF16),
+        vm((X, CP, cw), BF16), vm((X, CP, cw), BF16), vm((nb, cb, cw), BF16), vm((Y, cb, cw), BF16),
         vm((cb, cw), BF16), vm((Z, cb, cw), BF16), vm((cb, cw), BF16), vm((nb, cb, cw), BF16),
-        vm((X * C, nb, cb, cw), BF16),
+        vm((X, nb, cb, cw), BF16), vm((X, nb, cb, cw), BF16),
         dma((8,)),
         *[dma] * 6,
         dma((Y,)), dma((C,)), *[dma] * 6,
         *[dma((nk,))] * 8, *[dma] * 8,
         *[dma] * 4, dma((gk, 6)), dma((gk, 6)), dma((gk,)), dma((gk,)), dma((YL,)), dma, dma((X * C,)), dma((C,)),
-        *[dma] * 10,
+        *[dma] * 14,
     ]
     hbm = pl.BlockSpec(memory_space=pl.ANY)
     vmem = pl.BlockSpec(memory_space=pltpu.VMEM)
     smem = pl.BlockSpec(memory_space=pltpu.SMEM)
-    return pl.pallas_call(
+    hidden_grad, class_grad, node_grad = pl.pallas_call(
         functools.partial(kernel, dims),
         out_shape=(
             jax.ShapeDtypeStruct(hidden_weight.shape, F32),
-            jax.ShapeDtypeStruct(class_weight.shape, F32),
+            jax.ShapeDtypeStruct((CP, HID), BF16),
             jax.ShapeDtypeStruct((rows, HID // X), BF16),
         ),
         in_specs=[hbm, hbm, hbm, hbm, hbm, smem, hbm, smem, hbm, hbm],
@@ -689,6 +686,7 @@
         features, hidden_weight, class_weight, request_ids.T, request_counts.T,
         outer_tiles, outer_masks, inner_tiles, inner_masks, labels.reshape(1, -1),
     )
+    return hidden_grad, class_grad[:classes].astype(F32), node_grad
 
 
 def solution(mesh):

time: 89.6 us -> 91.3 us (1.019)
  local copies, waits for them, and re-layouts: 4.03 us -> 1.27 us
  Pallas kernels: 84.6 us -> 87.3 us
  other arithmetic: 0 us -> 1.91 us
    unnamed x5 -> x6, local copies, waits for them, and re-layouts: 4.03 us -> 1.27 us
    pallas_call x1, Pallas kernels: 84.6 us -> 87.3 us  [on_device(): pl.pallas_call(functools.partial(kernel, dims), out_shape=(jax.ShapeDtype...]
    convert_element_type x0 -> x1, other arithmetic: none -> 1.91 us  [on_device(): return (hidden_grad, class_grad[:classes].astype(F32), node_grad)]
where the time goes in v6:
time: 91.3 us; the launch traced here: 91.1 us
  Pallas kernels  87.3 us (96%)
  other arithmetic  1.91 us (2%)
  local copies, waits for them, and re-layouts  1.27 us (1%)
    pallas_call x1, Pallas kernels, on_device(): pl.pallas_call(functools.partial(kernel, dims), out_shape=(jax.ShapeDtype...  87.3 us
    convert_element_type x1, other arithmetic, on_device(): return (hidden_grad, class_grad[:classes].astype(F32), node_grad)  1.91 us

profile of v6, /device:TPU:1, one launch (start us, length us, event | category | flops | bytes accessed | tf_op | source)
XLA Modules:
  0.0 91.1 jit_solution(6098543624904568697)
XLA Ops:
  0.6 87.3 %shard_map.121 = (f32[8,768]{1,0:T(8,128)}, bf16[160,1024]{1,0:T(8,128)(2,1)}, bf16[256,256]{1,0:T(8,128)(2,1)}) custom-call(bf16[256,768]{1,0:T(8,128)(2,1)} %feat_hbm.1, bf16[8,768]{1,0:T(8,128)(2,1)} %weight_hbm.1, bf16[153,1024]{1,0:T(8,128)(2,1)} %cls_hbm.1, s32[4,128]{1,0:T(4,128)} %bitcast.3, s32[2,128]{1,0:T(2,128)} %bitcast.4, s32[2,2]{1,0:T(2,128)} %otile_ref.1, ...), custom_call_target="tpu_custom_call" | custom-call | flops 2000000000 | bytes 3000000 | tf_op jit(solution)/shard_map/pallas_call | solution.py:671
  87.9 0.0 copy-start.1
  88.0 0.0 copy-start
  88.0 1.9 %slice_convert_fusion = f32[153,1024]{1,0:T(8,128)} fusion(bf16[160,1024]{1,0:T(8,128)(2,1)} %get-tuple-element.7), kind=kLoop, calls=%fused_computation | loop fusion | flops 156672 | bytes 940032 | tf_op jit(solution)/shard_map/convert_element_type | solution.py:689
  89.9 0.0 copy-done.1
  89.9 0.6 copy.15
  90.5 0.0 copy-done
  90.5 0.7 copy.16
Async XLA Ops:
  87.9 1.9 %copy-start.1 = (f32[8,768]{1,0:T(8,128)S(1)}, f32[8,768]{1,0:T(8,128)}, u32[]{:S(2)}) copy-start(f32[8,768]{1,0:T(8,128)} %get-tuple-element.12) | copy-start | bytes 73732
  88.0 2.5 %copy-start = (bf16[256,256]{1,0:T(8,128)(2,1)S(1)}, bf16[256,256]{1,0:T(8,128)(2,1)}, u32[]{:S(2)}) copy-start(bf16[256,256]{1,0:T(8,128)(2,1)} %get-tuple-element.14) | copy-start | bytes 393220

commit v7 on v5

--- a/solution.py
+++ b/solution.py
@@ -97,7 +97,7 @@
         def step(i, carry):
             body(i)
             return carry
-        lax.fori_loop(1, n, step, 0, unroll=True)
+        lax.fori_loop(1, n, step, 0)
 
     class Exchange:
         def __init__(self, n, me, at, src, dst, bulk, ss, rs):
@@ -155,13 +155,9 @@
     def greet(zz, qq, xx):
         pl.semaphore_signal(barrier, inc=1, device_id=(zz * Q + qq, xx), device_id_type=MESH)
 
-    def greet_xz(d):
-        t = lax.bitwise_and(x * Z + z + d, X * Z - 1)
-        greet(lax.bitwise_and(t, Z - 1), q, t // Z)
-
+    each(Z, lambda d: greet(lax.bitwise_and(z + d, Z - 1), q, x))
     each(Q, lambda d: greet(z, lax.bitwise_and(q + d, Q - 1), x))
-    each(X * Z, greet_xz)
-    each(X, lambda d: greet(z, y * C + sib, lax.bitwise_and(x + d, X - 1)))
+    each(X, lambda d: greet(z, q, lax.bitwise_and(x + d, X - 1)))
 
     i1s[...] = jnp.zeros_like(i1s)
     for load in loads[:2]:
@@ -170,7 +166,7 @@
     w32 = weight_ref[...].astype(F32)
     ws[...] = jnp.concatenate([w32[:, :DH], w32[:, DH:]], axis=0).astype(BF16)
 
-    pl.semaphore_wait(barrier, (Q - 1) + (X * Z - 1) + (X - 1))
+    pl.semaphore_wait(barrier, (Z - 1) + (Q - 1) + (X - 1))
 
     ex_i1 = along_z(lambda t: i1s, lambda f: i1r.at[f], blocks(i1r, Z), i1_ss, i1_rs)
     ex_i1.start()
@@ -187,7 +183,7 @@
             def _():
                 act(t)
             return carry
-        lax.fori_loop(0, Y, step, 0, unroll=True)
+        lax.fori_loop(0, Y, step, 0)
 
     w1_each(lambda t: w1_copy(t).start())
     y_mine = x * C + c
@@ -408,8 +404,37 @@
     pgt[...] = jnp.where(pre[...] > 0.0, hidden_diff, 0.0).T.astype(BF16)
     g0 = to_sibling(pgt, pgtr, g0_ss, g0_rs)
     g0.start()
-
     diff[...] = hidden_diff.astype(BF16)
+
+    def total(ref, n):
+        acc = ref[0].astype(F32)
+        for k in range(1, n):
+            acc = acc + ref[k].astype(F32)
+        return acc
+
+    gmine = dot(pgt[...], agg[c])
+    ga.wait_recv()
+    g0.wait_recv()
+    gmine = (gmine + dot(pgtr[...], agr[...])).astype(BF16).reshape(Z, X, YL * 16, DH)
+    parts, span = gs1.shape[0], gs1.shape[4]
+    for k in range(parts):
+        for t in range(X):
+            gs1[k, t] = gmine[:, t, :, k * span:(k + 1) * span]
+    right, left, across = (lax.bitwise_and(x + d, X - 1) for d in (1, X - 1, 2))
+    lower, upper = pl.ds(0, Z // 2), pl.ds(Z // 2, Z // 2)
+
+    def g1(k, n, src, dst, to):
+        return copy(src, dst, g1_ss.at[k, n], g1_rs.at[k, n], z, q, to)
+
+    ring = [(
+        g1(k, 0, gs1.at[k, across, lower], gra.at[k], right), g1(k, 1, gs1.at[k, across, upper], grb.at[k], left),
+        g1(k, 2, gs1.at[k, right, upper], grl.at[k, upper], right), g1(k, 3, gs1.at[k, left, lower], grr.at[k, lower], left),
+        g1(k, 4, gsa.at[k], grl.at[k, lower], right), g1(k, 5, gsb.at[k], grr.at[k, upper], left),
+    ) for k in range(parts)]
+    for k in range(parts):
+        for one in ring[k][:4]:
+            one.start()
+
     xw = HID // X
     xh = xw // 2
 
@@ -436,35 +461,6 @@
     na1r[z] = na1s[x * Z + z]
     nb1r[q] = nb1s[q]
 
-    def total(ref, n):
-        acc = ref[0].astype(F32)
-        for k in range(1, n):
-            acc = acc + ref[k].astype(F32)
-        return acc
-
-    gmine = dot(pgt[...], agg[c])
-    ga.wait_recv()
-    g0.wait_recv()
-    gmine = (gmine + dot(pgtr[...], agr[...])).astype(BF16).reshape(Z, X, YL * 16, DH)
-    parts, span = gs1.shape[0], gs1.shape[4]
-    for k in range(parts):
-        for t in range(X):
-            gs1[k, t] = gmine[:, t, :, k * span:(k + 1) * span]
-    right, left, across = (lax.bitwise_and(x + d, X - 1) for d in (1, X - 1, 2))
-    lower, upper = pl.ds(0, Z // 2), pl.ds(Z // 2, Z // 2)
-
-    def g1(k, n, src, dst, to):
-        return copy(src, dst, g1_ss.at[k, n], g1_rs.at[k, n], z, q, to)
-
-    ring = [(
-        g1(k, 0, gs1.at[k, across, lower], gra.at[k], right), g1(k, 1, gs1.at[k, across, upper], grb.at[k], left),
-        g1(k, 2, gs1.at[k, right, upper], grl.at[k, upper], right), g1(k, 3, gs1.at[k, left, lower], grr.at[k, lower], left),
-        g1(k, 4, gsa.at[k], grl.at[k, lower], right), g1(k, 5, gsb.at[k], grr.at[k, upper], left),
-    ) for k in range(parts)]
-    for k in range(parts):
-        for one in ring[k][:4]:
-            one.start()
-
     ex_c1.recv()
     cs2[...] = total(cr1, X * C).astype(BF16).reshape(cs2.shape)
 
@@ -474,7 +470,7 @@
             def _():
                 act(t)
             return carry
-        lax.fori_loop(0, nb, step, 0, unroll=True)
+        lax.fori_loop(0, nb, step, 0)
 
     to_blocks(lambda t: copy(cs2.at[t], cr2.at[y], c2_ss, c2_rs, z, t * C + c, x).start())
     summing = y < nb
@@ -490,20 +486,6 @@
         l1.wait_recv()
         gsb[k] = (gs1[k, left, upper].astype(F32) + grb[k].astype(F32)).astype(BF16)
         l3.start()
-
-    wait_blocks(na1r, X * Z - 1, na1_ss, na1_rs).wait_recv()
-    came = jnp.concatenate([na1r[d * Z:(d + 1) * Z].reshape(hop, xh) for d in range(X)], axis=1)
-    came = dot(swap_a[...], came).astype(BF16)
-    for d in range(X):
-        na2s[:, d] = came[:, d * xh:(d + 1) * xh].reshape(Q, Z * half, xh)
-    ex_na2.start()
-    na2r[q] = na2s[q]
-    ex_nb1.recv()
-    came = dot(swap_b[...], nb1r[...].reshape(hop, X * xh)).astype(BF16)
-    for d in range(X):
-        nb2s[d * Z:(d + 1) * Z] = came[:, d * xh:(d + 1) * xh].reshape(Z, Q * half, xh)
-    xz_leg(lambda d, zz: nb2s.at[d * Z + zz], nb2r, nb2_ss, nb2_rs)
-    nb2r[z] = nb2s[z]
 
     @pl.when(summing)
     def _():
@@ -523,6 +505,13 @@
         ex_g2[k].start()
         gr2[k, z] = gs2[k, z]
 
+    wait_blocks(na1r, X * Z - 1, na1_ss, na1_rs).wait_recv()
+    came = jnp.concatenate([na1r[d * Z:(d + 1) * Z].reshape(hop, xh) for d in range(X)], axis=1)
+    came = dot(swap_a[...], came).astype(BF16)
+    for d in range(X):
+        na2s[:, d] = came[:, d * xh:(d + 1) * xh].reshape(Q, Z * half, xh)
+    ex_na2.start()
+    na2r[q] = na2s[q]
     @pl.when(summing)
     def _():
         ex_c3.recv()
@@ -530,6 +519,26 @@
         ex_c4.start()
         ca4[y] = cfin[...]
 
+    ex_nb1.recv()
+    came = dot(swap_b[...], nb1r[...].reshape(hop, X * xh)).astype(BF16)
+    for d in range(X):
+        nb2s[d * Z:(d + 1) * Z] = came[:, d * xh:(d + 1) * xh].reshape(Z, Q * half, xh)
+    xz_leg(lambda d, zz: nb2s.at[d * Z + zz], nb2r, nb2_ss, nb2_rs)
+    nb2r[z] = nb2s[z]
+
+    @pl.when(summing)
+    def _():
+        some = ca4.at[pl.ds(0, nb - 1)]
+        copy(some, some, c4_ss, c4_rs, z, q, x).wait_recv()
+
+    @pl.when(jnp.logical_not(summing))
+    def _():
+        copy(ca4, ca4, c4_ss, c4_rs, z, q, x).wait_recv()
+
+    ex_c5 = along_xc(lambda t: ca4, lambda f: ca5.at[f], blocks(ca5, X * C), c5_ss, c5_rs)
+    ex_c5.start()
+    ca5[me_xc] = ca4[...]
+
     for k in range(parts):
         ex_g2[k].recv()
         gs3[:, :, k * span:(k + 1) * span] = total(gr2.at[k], Z).astype(BF16).reshape(YL, 16, span)
@@ -542,19 +551,6 @@
         def _():
             g3_copy(yl).start()
     owning = y // YL == x
-
-    @pl.when(summing)
-    def _():
-        some = ca4.at[pl.ds(0, nb - 1)]
-        copy(some, some, c4_ss, c4_rs, z, q, x).wait_recv()
-
-    @pl.when(jnp.logical_not(summing))
-    def _():
-        copy(ca4, ca4, c4_ss, c4_rs, z, q, x).wait_recv()
-
-    ex_c5 = along_xc(lambda t: ca4, lambda f: ca5.at[f], blocks(ca5, X * C), c5_ss, c5_rs)
-    ex_c5.start()
-    ca5[me_xc] = ca4[...]
 
     ex_na2.recv()
     node_out[:, :xh] = dot(place_a[...], na2r[...].reshape(X * hop, xh)).astype(BF16)
@@ -584,8 +580,7 @@
     ex_c5.recv()
     for t in range(X):
         for cc in range(C):
-            at = cc * HH + t * cw
-            class_out[:, at:at + cw] = ca5[t * C + cc].reshape(CP, cw).astype(F32)[:classes]
+            class_out[:, cc * HH + t * cw:cc * HH + (t + 1) * cw] = ca5[t * C + cc].reshape(CP, cw)
 
     for cc in range(C):
         @pl.when(jnp.logical_not(owning & (c == cc)))
@@ -671,11 +666,11 @@
     hbm = pl.BlockSpec(memory_space=pl.ANY)
     vmem = pl.BlockSpec(memory_space=pltpu.VMEM)
     smem = pl.BlockSpec(memory_space=pltpu.SMEM)
-    return pl.pallas_call(
+    hidden_grad, class_grad, node_grad = pl.pallas_call(
         functools.partial(kernel, dims),
         out_shape=(
             jax.ShapeDtypeStruct(hidden_weight.shape, F32),
-            jax.ShapeDtypeStruct(class_weight.shape, F32),
+            jax.ShapeDtypeStruct((CP, HID), BF16),
             jax.ShapeDtypeStruct((rows, HID // X), BF16),
         ),
         in_specs=[hbm, hbm, hbm, hbm, hbm, smem, hbm, smem, hbm, hbm],
@@ -689,6 +684,7 @@
         features, hidden_weight, class_weight, request_ids.T, request_counts.T,
         outer_tiles, outer_masks, inner_tiles, inner_masks, labels.reshape(1, -1),
     )
+    return hidden_grad, class_grad[:classes].astype(F32), node_grad
 
 
 def solution(mesh):

time: 89.6 us -> 86.9 us (0.970)
  local copies, waits for them, and re-layouts: 4.03 us -> 1.27 us
  Pallas kernels: 84.6 us -> 82.3 us
  other arithmetic: 0 us -> 1.91 us
    unnamed x5 -> x6, local copies, waits for them, and re-layouts: 4.03 us -> 1.27 us
    pallas_call x1, Pallas kernels: 84.6 us -> 82.3 us  [on_device(): pl.pallas_call(functools.partial(kernel, dims), out_shape=(jax.ShapeDtype...]
    convert_element_type x0 -> x1, other arithmetic: none -> 1.91 us  [on_device(): return (hidden_grad, class_grad[:classes].astype(F32), node_grad)]
where the time goes in v7:
time: 86.9 us; the launch traced here: 86.2 us
  Pallas kernels  82.3 us (95%)
  other arithmetic  1.91 us (2%)
  local copies, waits for them, and re-layouts  1.27 us (1%)
    pallas_call x1, Pallas kernels, on_device(): pl.pallas_call(functools.partial(kernel, dims), out_shape=(jax.ShapeDtype...  82.3 us
    convert_element_type x1, other arithmetic, on_device(): return (hidden_grad, class_grad[:classes].astype(F32), node_grad)  1.91 us

profile of v7, /device:TPU:1, one launch (start us, length us, event | category | flops | bytes accessed | tf_op | source)
XLA Modules:
  0.0 86.2 jit_solution(17040161301448250079)
XLA Ops:
  0.6 82.3 %shard_map.121 = (f32[8,768]{1,0:T(8,128)}, bf16[160,1024]{1,0:T(8,128)(2,1)}, bf16[256,256]{1,0:T(8,128)(2,1)}) custom-call(bf16[256,768]{1,0:T(8,128)(2,1)} %feat_hbm.1, bf16[8,768]{1,0:T(8,128)(2,1)} %weight_hbm.1, bf16[153,1024]{1,0:T(8,128)(2,1)} %cls_hbm.1, s32[4,128]{1,0:T(4,128)} %bitcast.3, s32[2,128]{1,0:T(2,128)} %bitcast.4, s32[2,2]{1,0:T(2,128)} %otile_ref.1, ...), custom_call_target="tpu_custom_call" | custom-call | flops 2000000000 | bytes 3000000 | tf_op jit(solution)/shard_map/pallas_call | solution.py:669
  83.0 0.0 copy-start.1
  83.0 0.0 copy-start
  83.0 1.9 %slice_convert_fusion = f32[153,1024]{1,0:T(8,128)} fusion(bf16[160,1024]{1,0:T(8,128)(2,1)} %get-tuple-element.7), kind=kLoop, calls=%fused_computation | loop fusion | flops 156672 | bytes 940032 | tf_op jit(solution)/shard_map/convert_element_type | solution.py:687
  84.9 0.0 copy-done.1
  84.9 0.6 copy.15
  85.5 0.0 copy-done
  85.5 0.7 copy.16
Async XLA Ops:
  83.0 1.9 %copy-start.1 = (f32[8,768]{1,0:T(8,128)S(1)}, f32[8,768]{1,0:T(8,128)}, u32[]{:S(2)}) copy-start(f32[8,768]{1,0:T(8,128)} %get-tuple-element.12) | copy-start | bytes 73732
  83.0 2.5 %copy-start = (bf16[256,256]{1,0:T(8,128)(2,1)S(1)}, bf16[256,256]{1,0:T(8,128)(2,1)}, u32[]{:S(2)}) copy-start(bf16[256,256]{1,0:T(8,128)(2,1)} %get-tuple-element.14) | copy-start | bytes 393220

commit v8 on v7

--- a/solution.py
+++ b/solution.py
@@ -51,7 +51,8 @@
     feat, omask, imask, cls, weight_ref, ids_ref, counts_ref, labels_ref,
     i1s, i1r, i2s, i2r, wx, place_a, place_b,
     ws, wr, w_all,
-    fa1s, fa1r, fa2s, fa2r, fb1s, fb1r, fb2s, fb2r, move_a, move_b, swap_a, swap_b,
+    fa1s_0, fa1s_1, fa1r_0, fa1r_1, fb1s_0, fb1s_1, fb1r_0, fb1r_1,
+    fa2s_0, fa2s_1, fa2r_0, fa2r_1, fb2s_0, fb2s_1, fb2r_0, fb2r_1, move_a, move_b, swap_a, swap_b,
     agg, agr, pre, pgt, pgtr, diff,
     na1s, na1r, na2s, na2r, nb1s, nb1r, nb2s, nb2r,
     gs1, gra, grb, gsa, gsb, grl, grr, gs2, gr2, gs3, gr3, gs4, gr4,
@@ -234,39 +235,43 @@
         ids = jnp.sum(jnp.where(lane_q == q_of * 8, spread, 0.0), axis=1, keepdims=True)
         return flag(ids == iota((front, rows), 1).astype(F32))
 
-    chunks, wide = fa1s.shape[0], fa1s.shape[3]
+    wide, nk = 128, DH // 128
+    spans = ((0, nk - 1), (nk - 1, nk))
+    fa1s, fa1r, fb1s, fb1r = (fa1s_0, fa1s_1), (fa1r_0, fa1r_1), (fb1s_0, fb1s_1), (fb1r_0, fb1r_1)
+    fa2s, fa2r, fb2s, fb2r = (fa2s_0, fa2s_1), (fa2r_0, fa2r_1), (fb2s_0, fb2s_1), (fb2r_0, fb2r_1)
+    chunks = len(spans)
     r = iota((front, 1), 0)
     pick_a = picked(quo(r, cap * Q) * S8 + quo(rem(r, cap * Q), Q), rem(r, Q))
 
     def column_blocks(first):
-        return jnp.concatenate([feat[:, b * wide:(b + 1) * wide] for b in range(first, 2 * chunks, 2)], axis=1)
+        return jnp.concatenate([feat[:, b * wide:(b + 1) * wide] for b in range(first, 2 * nk, 2)], axis=1)
 
     rows_a = dot(pick_a, column_blocks(0)).astype(BF16)
     ex_fa1, ex_fb1, ex_fa2, ex_fb2 = [], [], [], []
     for k in range(chunks):
-        at = slice(k * wide, (k + 1) * wide)
-        fa1s[k] = rows_a[:, at].reshape(fa1s.shape[1:])
+        at = slice(spans[k][0] * wide, spans[k][1] * wide)
+        fa1s[k][...] = rows_a[:, at].reshape(fa1s[k].shape)
         ex_fa1.append(along_z(
-            lambda t, k=k: fa1s.at[k, t], lambda f, k=k: fa1r.at[k, f], blocks(fa1r.at[k], Z), fa1_ss.at[k], fa1_rs.at[k]))
+            lambda t, k=k: fa1s[k].at[t], lambda f, k=k: fa1r[k].at[f], blocks(fa1r[k], Z), fa1_ss.at[k], fa1_rs.at[k]))
         ex_fb1.append(along_q(
-            lambda t, k=k: fb1s.at[k, t], lambda f, k=k: fb1r.at[k, f], blocks(fb1r.at[k], Q), fb1_ss.at[k], fb1_rs.at[k]))
+            lambda t, k=k: fb1s[k].at[t], lambda f, k=k: fb1r[k].at[f], blocks(fb1r[k], Q), fb1_ss.at[k], fb1_rs.at[k]))
         ex_fa2.append(along_q(
-            lambda t, k=k: fa2s.at[k, t], lambda f, k=k: fa2r.at[k, f], blocks(fa2r.at[k], Q), fa2_ss.at[k], fa2_rs.at[k]))
+            lambda t, k=k: fa2s[k].at[t], lambda f, k=k: fa2r[k].at[f], blocks(fa2r[k], Q), fa2_ss.at[k], fa2_rs.at[k]))
         ex_fb2.append(along_z(
-            lambda t, k=k: fb2s.at[k, t], lambda f, k=k: fb2r.at[k, f], blocks(fb2r.at[k], Z), fb2_ss.at[k], fb2_rs.at[k]))
+            lambda t, k=k: fb2s[k].at[t], lambda f, k=k: fb2r[k].at[f], blocks(fb2r[k], Z), fb2_ss.at[k], fb2_rs.at[k]))
     ex_fa1[0].start()
     pick_b = picked(rem(r, Z) * S8 + quo(rem(r, cap * Z), Z), quo(r, cap * Z))
     rows_b = dot(pick_b, column_blocks(1)).astype(BF16)
     for k in range(chunks):
-        at = slice(k * wide, (k + 1) * wide)
-        fb1s[k] = rows_b[:, at].reshape(fb1s.shape[1:])
+        at = slice(spans[k][0] * wide, spans[k][1] * wide)
+        fb1s[k][...] = rows_b[:, at].reshape(fb1s[k].shape)
     ex_fb1[0].start()
     for k in range(1, chunks):
         ex_fa1[k].start()
         ex_fb1[k].start()
     for k in range(chunks):
-        fa1r[k, z] = fa1s[k, z]
-        fb1r[k, q] = fb1s[k, q]
+        fa1r[k][z] = fa1s[k][z]
+        fb1r[k][q] = fb1s[k][q]
     ex_wx.start()
     move_a[...] = regroup(Z * cap, Q, 1)
     move_b[...] = regroup(Q * cap, Z, 1)
@@ -328,13 +333,13 @@
 
     for k in range(chunks):
         ex_fa1[k].recv()
-        fa2s[k] = dot(move_a[...], fa1r[k].reshape(front, wide)).astype(BF16).reshape(fa2s.shape[1:])
+        fa2s[k][...] = dot(move_a[...], fa1r[k][...].reshape(front, -1)).astype(BF16).reshape(fa2s[k].shape)
         ex_fa2[k].start()
-        fa2r[k, q] = fa2s[k, q]
+        fa2r[k][q] = fa2s[k][q]
         ex_fb1[k].recv()
-        fb2s[k] = dot(move_b[...], fb1r[k].reshape(front, wide)).astype(BF16).reshape(fb2s.shape[1:])
+        fb2s[k][...] = dot(move_b[...], fb1r[k][...].reshape(front, -1)).astype(BF16).reshape(fb2s[k].shape)
         ex_fb2[k].start()
-        fb2r[k, z] = fb2s[k, z]
+        fb2r[k][z] = fb2s[k][z]
 
     ex_w3.recv()
     w4 = to_sibling(w_all.at[:, :, c], w_all.at[:, :, c], w4_ss, w4_rs)
@@ -367,16 +372,20 @@
 
     for k in range(chunks):
         ex_fa2[k].recv()
-        part_a = (dot(outer_a, fa2r[k].reshape(front, wide)) / outer_scale).astype(BF16)
+        part_a = (dot(outer_a, fa2r[k][...].reshape(front, -1)) / outer_scale).astype(BF16)
         ex_fb2[k].recv()
-        part_b = (dot(outer_self, fb2r[k].reshape(front, wide)) / outer_scale).astype(BF16)
-        for b, part in ((2 * k, part_a), (2 * k + 1, part_b)):
-            agg[b // chunks, :, (b % chunks) * wide:(b % chunks + 1) * wide] = part
+        part_b = (dot(outer_self, fb2r[k][...].reshape(front, -1)) / outer_scale).astype(BF16)
+        first, last = spans[k]
+        columns = []
+        for i in range(last - first):
+            for b, part in ((2 * (first + i), part_a), (2 * (first + i) + 1, part_b)):
+                columns.append(part[:, i * wide:(i + 1) * wide])
+                agg[b // nk, :, (b % nk) * wide:(b % nk + 1) * wide] = columns[-1]
         if k == 0:
             w4_in.wait_recv()
         part = dot(
-            jnp.concatenate([part_a, part_b], axis=1),
-            w_all[:, :, :, :, 2 * k * wide:2 * (k + 1) * wide].reshape(HID, 2 * wide), 1, 1)
+            jnp.concatenate(columns, axis=1),
+            w_all[:, :, :, :, 2 * first * wide:2 * last * wide].reshape(HID, -1), 1, 1)
         pre[...] = part if k == 0 else pre[...] + part
     ga = to_sibling(agg.at[sib], agr, ga_ss, ga_rs)
     ga.start()
@@ -387,6 +396,21 @@
     exponent = jnp.exp(logits - jnp.max(logits, axis=1, keepdims=True))
     softmax = exponent / jnp.sum(exponent, axis=1, keepdims=True)
     logit_grad = ((softmax - one_hot) / seeds).astype(BF16)
+    agg_grad = dot(logit_grad, cls[...]) / inner_degree
+    high = agg_grad.astype(BF16)
+    low = (agg_grad - high.astype(F32)).astype(BF16)
+    hidden_diff = dot(inner_twice, jnp.concatenate([high, low], axis=0))
+    pgt[...] = jnp.where(pre[...] > 0.0, hidden_diff, 0.0).T.astype(BF16)
+    g0 = to_sibling(pgt, pgtr, g0_ss, g0_rs)
+    g0.start()
+    diff[...] = hidden_diff.astype(BF16)
+
+    def total(ref, n):
+        acc = ref[0].astype(F32)
+        for k in range(1, n):
+            acc = acc + ref[k].astype(F32)
+        return acc
+
     widen = flag(iota((classes, CP), 0) == iota((classes, CP), 1))
     class_rows = dot(dot(logit_grad, widen).astype(BF16), agg_two, 0, 0).astype(BF16)
     for t in range(X):
@@ -396,21 +420,6 @@
     ex_c1 = along_xc(lambda t: cs1.at[t], lambda f: cr1.at[f], blocks(cr1, X * C), c1_ss, c1_rs)
     ex_c1.start()
     cr1[me_xc] = cs1[me_xc]
-
-    agg_grad = dot(logit_grad, cls[...]) / inner_degree
-    high = agg_grad.astype(BF16)
-    low = (agg_grad - high.astype(F32)).astype(BF16)
-    hidden_diff = dot(inner_twice, jnp.concatenate([high, low], axis=0))
-    pgt[...] = jnp.where(pre[...] > 0.0, hidden_diff, 0.0).T.astype(BF16)
-    g0 = to_sibling(pgt, pgtr, g0_ss, g0_rs)
-    g0.start()
-    diff[...] = hidden_diff.astype(BF16)
-
-    def total(ref, n):
-        acc = ref[0].astype(F32)
-        for k in range(1, n):
-            acc = acc + ref[k].astype(F32)
-        return acc
 
     gmine = dot(pgt[...], agg[c])
     ga.wait_recv()
@@ -635,6 +644,8 @@
     dims = (Z, Y, C, X, cap, tile, rows, classes)
     vm, dma = pltpu.VMEM, pltpu.SemaphoreType.DMA
     xh, nk, gk = HID // X // 2, DH // 128, 1
+    by_z = [vm((Z, cap * Q, n * 128), BF16) for n in (nk - 1, 1)]
+    by_q = [vm((Q, cap * Z, n * 128), BF16) for n in (nk - 1, 1)]
     scratch = [
         vm(features.shape, BF16), vm(outer_masks.shape, jnp.int32), vm(inner_masks.shape, jnp.int32),
         vm(class_weight.shape, BF16), vm(hidden_weight.shape, BF16),
@@ -642,8 +653,7 @@
         vm((8, NO), F32), vm((Z, 8, NO), F32), vm((Q, 8, LW), F32), vm((Q, 8, LW), F32),
         vm((X, Q * 8, LW), BF16), vm((rows, X * hop), BF16), vm((rows, X * hop), BF16),
         vm((16, DH), BF16), vm((C, 16, DH), BF16), vm((Z, X, C, 16, D), BF16),
-        *[vm((nk, Z, cap * Q, DH // nk), BF16)] * 2, *[vm((nk, Q, cap * Z, DH // nk), BF16)] * 2,
-        *[vm((nk, Q, cap * Z, DH // nk), BF16)] * 2, *[vm((nk, Z, cap * Q, DH // nk), BF16)] * 2,
+        *by_z, *by_z, *by_q, *by_q, *by_q, *by_q, *by_z, *by_z,
         vm((cap * NO, cap * NO), BF16), vm((cap * NO, cap * NO), BF16), vm((hop, hop), BF16), vm((hop, hop), BF16),
         vm((2, hop, DH), BF16), vm((hop, DH), BF16), vm((hop, HID), F32), vm((HID, hop), BF16), vm((HID, hop), BF16),
         vm((hop, HID), BF16),
@@ -659,7 +669,7 @@
         dma((8,)),
         *[dma] * 6,
         dma((Y,)), dma((C,)), *[dma] * 6,
-        *[dma((nk,))] * 8, *[dma] * 8,
+        *[dma((2,))] * 8, *[dma] * 8,
         *[dma] * 4, dma((gk, 6)), dma((gk, 6)), dma((gk,)), dma((gk,)), dma((YL,)), dma, dma((X * C,)), dma((C,)),
         *[dma] * 10,
     ]

time: 86.9 us -> 88 us (1.013)
  Pallas kernels: 82.3 us -> 83.6 us
    pallas_call x1, Pallas kernels: 82.3 us -> 83.6 us  [on_device(): pl.pallas_call(functools.partial(kernel, dims), out_shape=(jax.ShapeDtype...]
where the time goes in v8:
time: 88 us; the launch traced here: 87.5 us
  Pallas kernels  83.6 us (95%)
  other arithmetic  1.91 us (2%)
  local copies, waits for them, and re-layouts  1.27 us (1%)
    pallas_call x1, Pallas kernels, on_device(): pl.pallas_call(functools.partial(kernel, dims), out_shape=(jax.ShapeDtype...  83.6 us
    convert_element_type x1, other arithmetic, on_device(): return (hidden_grad, class_grad[:classes].astype(F32), node_grad)  1.91 us

profile of v8, /device:TPU:1, one launch (start us, length us, event | category | flops | bytes accessed | tf_op | source)
XLA Modules:
  0.0 87.5 jit_solution(14144249332570253862)
XLA Ops:
  0.6 83.6 %shard_map.121 = (f32[8,768]{1,0:T(8,128)}, bf16[160,1024]{1,0:T(8,128)(2,1)}, bf16[256,256]{1,0:T(8,128)(2,1)}) custom-call(bf16[256,768]{1,0:T(8,128)(2,1)} %feat_hbm.1, bf16[8,768]{1,0:T(8,128)(2,1)} %weight_hbm.1, bf16[153,1024]{1,0:T(8,128)(2,1)} %cls_hbm.1, s32[4,128]{1,0:T(4,128)} %bitcast.3, s32[2,128]{1,0:T(2,128)} %bitcast.4, s32[2,2]{1,0:T(2,128)} %otile_ref.1, ...), custom_call_target="tpu_custom_call" | custom-call | flops 2000000000 | bytes 3000000 | tf_op jit(solution)/shard_map/pallas_call | solution.py:679
  84.2 0.0 copy-start.1
  84.3 0.0 copy-start
  84.3 1.9 %slice_convert_fusion = f32[153,1024]{1,0:T(8,128)} fusion(bf16[160,1024]{1,0:T(8,128)(2,1)} %get-tuple-element.7), kind=kLoop, calls=%fused_computation | loop fusion | flops 156672 | bytes 940032 | tf_op jit(solution)/shard_map/convert_element_type | solution.py:697
  86.2 0.0 copy-done.1
  86.2 0.6 copy.15
  86.8 0.0 copy-done
  86.8 0.7 copy.16
Async XLA Ops:
  84.2 1.9 %copy-start.1 = (f32[8,768]{1,0:T(8,128)S(1)}, f32[8,768]{1,0:T(8,128)}, u32[]{:S(2)}) copy-start(f32[8,768]{1,0:T(8,128)} %get-tuple-element.12) | copy-start | bytes 73732
  84.3 2.5 %copy-start = (bf16[256,256]{1,0:T(8,128)(2,1)S(1)}, bf16[256,256]{1,0:T(8,128)(2,1)}, u32[]{:S(2)}) copy-start(bf16[256,256]{1,0:T(8,128)(2,1)} %get-tuple-element.14) | copy-start | bytes 393220

commit v9 on v8

--- a/solution.py
+++ b/solution.py
@@ -56,14 +56,14 @@
     agg, agr, pre, pgt, pgtr, diff,
     na1s, na1r, na2s, na2r, nb1s, nb1r, nb2s, nb2r,
     gs1, gra, grb, gsa, gsb, grl, grr, gs2, gr2, gs3, gr3, gs4, gr4,
-    cs1, cr1, cs2, cr2, cs3, cr3, cfin, ca4, ca5,
+    cmine, cs0, cr0, cs1, cr1, cs2, cr2, cs3, cr3, cfin, ca4, ca5, ca6,
     local_sem,
     i1_ss, i1_rs, i2_ss, i2_rs, wx_ss, wx_rs,
     w1_ss, w1_rs, w2_ss, w2_rs, w3_ss, w3_rs, w4_ss, w4_rs,
     fa1_ss, fa1_rs, fa2_ss, fa2_rs, fb1_ss, fb1_rs, fb2_ss, fb2_rs,
     na1_ss, na1_rs, na2_ss, na2_rs, nb1_ss, nb1_rs, nb2_ss, nb2_rs,
     ga_ss, ga_rs, g0_ss, g0_rs, g1_ss, g1_rs, g2_ss, g2_rs, g3_ss, g3_rs, g4_ss, g4_rs,
-    c1_ss, c1_rs, c2_ss, c2_rs, c3_ss, c3_rs, c4_ss, c4_rs, c5_ss, c5_rs,
+    c0_ss, c0_rs, c1_ss, c1_rs, c2_ss, c2_rs, c3_ss, c3_rs, c4_ss, c4_rs, c5_ss, c5_rs, c6_ss, c6_rs,
 ):
     Z, Y, C, X, cap, tile, rows, classes = dims
     Q = Y * C
@@ -216,10 +216,21 @@
         w_all[z, x, c, :, cols] = jnp.concatenate(
             [wr[c0, hcol * 8:(hcol + 1) * 8, :].astype(F32) for c0 in range(C)], axis=0
         ).astype(BF16)
-    ex_w2 = along_z(
-        lambda t: w_all.at[z, x, c], lambda f: w_all.at[f, x, c], w_all.at[pl.ds(0, Z - 1), x, c], w2_ss, w2_rs
-    )
-    ex_w2.start()
+    def w2(k, way):
+        block = w_all.at[lax.bitwise_and(z + (Z - k if way == 0 else k), Z - 1), x, c]
+        to = lax.bitwise_and(z + (1 if way == 0 else Z - 1), Z - 1)
+        return copy(block, block, w2_ss.at[k, way], w2_rs.at[k, way], to, q, x)
+
+    def w2_steps(k):
+        return [w2(k, way) for way, steps in ((0, Z // 2), (1, Z // 2 - 1)) if 0 <= k < steps]
+
+    def w2_go(k):
+        for one in w2_steps(k - 1):
+            one.wait_recv()
+        for one in w2_steps(k):
+            one.start()
+
+    w2_go(0)
 
     loads[2].wait()
     lane_q = iota((front, Q * 8), 1)
@@ -260,6 +271,7 @@
         ex_fb2.append(along_z(
             lambda t, k=k: fb2s[k].at[t], lambda f, k=k: fb2r[k].at[f], blocks(fb2r[k], Z), fb2_ss.at[k], fb2_rs.at[k]))
     ex_fa1[0].start()
+    w2_go(1)
     pick_b = picked(rem(r, Z) * S8 + quo(rem(r, cap * Z), Z), quo(r, cap * Z))
     rows_b = dot(pick_b, column_blocks(1)).astype(BF16)
     for k in range(chunks):
@@ -276,11 +288,7 @@
     move_a[...] = regroup(Z * cap, Q, 1)
     move_b[...] = regroup(Q * cap, Z, 1)
 
-    ex_w2.recv()
-    ex_w3 = along_x(
-        lambda t: w_all.at[:, x, c], lambda f: w_all.at[:, f, c], w_all.at[:, pl.ds(0, X - 1), c], w3_ss, w3_rs
-    )
-    ex_w3.start()
+    w2_go(2)
 
     for load in loads[3:]:
         load.wait()
@@ -331,6 +339,10 @@
     )
     one_hot = flag(label_col == iota((seeds, classes), 1), F32)
 
+    w2_go(3)
+    ex_w3 = along_x(
+        lambda t: w_all.at[:, x, c], lambda f: w_all.at[:, f, c], w_all.at[:, pl.ds(0, X - 1), c], w3_ss, w3_rs
+    )
     for k in range(chunks):
         ex_fa1[k].recv()
         fa2s[k][...] = dot(move_a[...], fa1r[k][...].reshape(front, -1)).astype(BF16).reshape(fa2s[k].shape)
@@ -340,11 +352,9 @@
         fb2s[k][...] = dot(move_b[...], fb1r[k][...].reshape(front, -1)).astype(BF16).reshape(fb2s[k].shape)
         ex_fb2[k].start()
         fb2r[k][z] = fb2s[k][z]
-
-    ex_w3.recv()
-    w4 = to_sibling(w_all.at[:, :, c], w_all.at[:, :, c], w4_ss, w4_rs)
-    w4_in = to_sibling(w_all.at[:, :, sib], w_all.at[:, :, sib], w4_ss, w4_rs)
-    w4.start()
+        if k == 0:
+            w2_go(Z // 2)
+            ex_w3.start()
 
     swap_a[...] = regroup(Z, Q, half)
     swap_b[...] = regroup(Q, Z, half)
@@ -369,6 +379,11 @@
     place_b[...] = places(
         plane(quo(s, half * Q * Z)), rem(s, half), rem(quo(s, half * Q), Z), rem(quo(s, half), Q)
     )
+
+    ex_w3.recv()
+    w4 = to_sibling(w_all.at[:, :, c], w_all.at[:, :, c], w4_ss, w4_rs)
+    w4_in = to_sibling(w_all.at[:, :, sib], w_all.at[:, :, sib], w4_ss, w4_rs)
+    w4.start()
 
     for k in range(chunks):
         ex_fa2[k].recv()
@@ -412,14 +427,11 @@
         return acc
 
     widen = flag(iota((classes, CP), 0) == iota((classes, CP), 1))
-    class_rows = dot(dot(logit_grad, widen).astype(BF16), agg_two, 0, 0).astype(BF16)
-    for t in range(X):
-        for cc in range(C):
-            cs1[t * C + cc] = class_rows[:, cc * HH + t * cw:cc * HH + (t + 1) * cw]
-    me_xc = x * C + c
-    ex_c1 = along_xc(lambda t: cs1.at[t], lambda f: cr1.at[f], blocks(cr1, X * C), c1_ss, c1_rs)
-    ex_c1.start()
-    cr1[me_xc] = cs1[me_xc]
+    class_rows = dot(dot(logit_grad, widen).astype(BF16), agg_two, 0, 0)
+    cs0[...] = jnp.where(c == 0, class_rows[:, HH:], class_rows[:, :HH]).astype(BF16)
+    c0 = to_sibling(cs0, cr0, c0_ss, c0_rs)
+    c0.start()
+    cmine[...] = jnp.where(c == 0, class_rows[:, :HH], class_rows[:, HH:])
 
     gmine = dot(pgt[...], agg[c])
     ga.wait_recv()
@@ -443,6 +455,14 @@
     for k in range(parts):
         for one in ring[k][:4]:
             one.start()
+
+    c0.wait_recv()
+    cmine[...] = cmine[...] + cr0[...].astype(F32)
+    for t in range(X):
+        cs1[t] = cmine[:, t * cw:(t + 1) * cw].astype(BF16)
+    ex_c1 = along_x(lambda t: cs1.at[t], lambda f: cr1.at[f], blocks(cr1, X), c1_ss, c1_rs)
+    ex_c1.start()
+    cr1[x] = cs1[x]
 
     xw = HID // X
     xh = xw // 2
@@ -471,7 +491,7 @@
     nb1r[q] = nb1s[q]
 
     ex_c1.recv()
-    cs2[...] = total(cr1, X * C).astype(BF16).reshape(cs2.shape)
+    cs2[...] = total(cr1, X).astype(BF16).reshape(cs2.shape)
 
     def to_blocks(act):
         def step(t, carry):
@@ -544,9 +564,9 @@
     def _():
         copy(ca4, ca4, c4_ss, c4_rs, z, q, x).wait_recv()
 
-    ex_c5 = along_xc(lambda t: ca4, lambda f: ca5.at[f], blocks(ca5, X * C), c5_ss, c5_rs)
+    ex_c5 = along_x(lambda t: ca4, lambda f: ca5.at[f], blocks(ca5, X), c5_ss, c5_rs)
     ex_c5.start()
-    ca5[me_xc] = ca4[...]
+    ca5[x] = ca4[...]
 
     for k in range(parts):
         ex_g2[k].recv()
@@ -583,13 +603,12 @@
 
     g4_each(lambda xx, cc: g4_copy(xx, cc).start())
 
+    ex_c5.recv()
+    c6 = to_sibling(ca5, ca6, c6_ss, c6_rs)
+    c6.start()
+
     wait_blocks(nb2r, X * Z - 1, nb2_ss, nb2_rs).wait_recv()
     node_out[:, xh:] = dot(place_b[...], nb2r[...].reshape(X * hop, xh)).astype(BF16)
-
-    ex_c5.recv()
-    for t in range(X):
-        for cc in range(C):
-            class_out[:, cc * HH + t * cw:cc * HH + (t + 1) * cw] = ca5[t * C + cc].reshape(CP, cw)
 
     for cc in range(C):
         @pl.when(jnp.logical_not(owning & (c == cc)))
@@ -597,10 +616,16 @@
             copy(gs4.at[0], gr4.at[cc], g4_ss.at[0], g4_rs.at[cc], z, y * C + cc, y // YL).wait_recv()
         hidden_out[:, cc * DH:(cc + 1) * DH] = gr4[cc]
 
-    for ex in (ex_i1, ex_i2, ex_wx, ex_w2, ex_w3, *ex_fa1, *ex_fb1, *ex_fa2, *ex_fb2, ex_nb1, ex_na2, *ex_g2, ex_c1, ex_c5):
+    c6.wait_recv()
+    for t in range(X):
+        ours, theirs = ca5[t].reshape(CP, cw), ca6[t].reshape(CP, cw)
+        for cc in range(C):
+            class_out[:, cc * HH + t * cw:cc * HH + (t + 1) * cw] = jnp.where(c == cc, ours, theirs)
+
+    for ex in (ex_i1, ex_i2, ex_wx, ex_w3, *ex_fa1, *ex_fb1, *ex_fa2, *ex_fb2, ex_nb1, ex_na2, *ex_g2, ex_c1, ex_c5):
         ex.sent()
     w1_each(lambda t: w1_copy(t).wait_send())
-    for one in (w4, ga, g0, *[leg for legs in ring for leg in legs]):
+    for one in (w4, ga, g0, c0, c6, *[step for k in range(Z // 2) for step in w2_steps(k)], *[leg for legs in ring for leg in legs]):
         one.wait_send()
     wait_blocks(na1r, X * Z - 1, na1_ss, na1_rs).wait_send()
     wait_blocks(nb2r, X * Z - 1, nb2_ss, nb2_rs).wait_send()
@@ -663,15 +688,16 @@
         vm((gk, X, Z, YL * 16, DH // gk), BF16), *[vm((gk, Z // 2, YL * 16, DH // gk), BF16)] * 4,
         *[vm((gk, Z, YL * 16, DH // gk), BF16)] * 4,
         vm((YL, 16, DH), BF16), vm((Y, 16, DH), BF16), vm((C, 8, DH), F32), vm((C, 8, DH), F32),
-        vm((X * C, CP, cw), BF16), vm((X * C, CP, cw), BF16), vm((nb, cb, cw), BF16), vm((Y, cb, cw), BF16),
+        vm((CP, HH), F32), vm((CP, HH), BF16), vm((CP, HH), BF16),
+        vm((X, CP, cw), BF16), vm((X, CP, cw), BF16), vm((nb, cb, cw), BF16), vm((Y, cb, cw), BF16),
         vm((cb, cw), BF16), vm((Z, cb, cw), BF16), vm((cb, cw), BF16), vm((nb, cb, cw), BF16),
-        vm((X * C, nb, cb, cw), BF16),
+        vm((X, nb, cb, cw), BF16), vm((X, nb, cb, cw), BF16),
         dma((8,)),
         *[dma] * 6,
-        dma((Y,)), dma((C,)), *[dma] * 6,
+        dma((Y,)), dma((C,)), dma((Z // 2, 2)), dma((Z // 2, 2)), *[dma] * 4,
         *[dma((2,))] * 8, *[dma] * 8,
         *[dma] * 4, dma((gk, 6)), dma((gk, 6)), dma((gk,)), dma((gk,)), dma((YL,)), dma, dma((X * C,)), dma((C,)),
-        *[dma] * 10,
+        *[dma] * 14,
     ]
     hbm = pl.BlockSpec(memory_space=pl.ANY)
     vmem = pl.BlockSpec(memory_space=pltpu.VMEM)

time: 88 us -> 95.4 us (1.084)
  Pallas kernels: 83.6 us -> 91.1 us
    pallas_call x1, Pallas kernels: 83.6 us -> 91.1 us  [on_device(): pl.pallas_call(functools.partial(kernel, dims), out_shape=(jax.ShapeDtype...]
where the time goes in v9:
time: 95.4 us; the launch traced here: 94.9 us
  Pallas kernels  91.1 us (95%)
  other arithmetic  1.91 us (2%)
  local copies, waits for them, and re-layouts  1.27 us (1%)
    pallas_call x1, Pallas kernels, on_device(): pl.pallas_call(functools.partial(kernel, dims), out_shape=(jax.ShapeDtype...  91.1 us
    convert_element_type x1, other arithmetic, on_device(): return (hidden_grad, class_grad[:classes].astype(F32), node_grad)  1.91 us

profile of v9, /device:TPU:1, one launch (start us, length us, event | category | flops | bytes accessed | tf_op | source)
XLA Modules:
  0.0 94.9 jit_solution(14899249411438944880)
XLA Ops:
  0.6 91.1 %shard_map.121 = (f32[8,768]{1,0:T(8,128)}, bf16[160,1024]{1,0:T(8,128)(2,1)}, bf16[256,256]{1,0:T(8,128)(2,1)}) custom-call(bf16[256,768]{1,0:T(8,128)(2,1)} %feat_hbm.1, bf16[8,768]{1,0:T(8,128)(2,1)} %weight_hbm.1, bf16[153,1024]{1,0:T(8,128)(2,1)} %cls_hbm.1, s32[4,128]{1,0:T(4,128)} %bitcast.3, s32[2,128]{1,0:T(2,128)} %bitcast.4, s32[2,2]{1,0:T(2,128)} %otile_ref.1, ...), custom_call_target="tpu_custom_call" | custom-call | flops 2000000000 | bytes 3000000 | tf_op jit(solution)/shard_map/pallas_call | solution.py:705
  91.7 0.0 copy-start.1
  91.7 0.0 copy-start
  91.7 1.9 %slice_convert_fusion = f32[153,1024]{1,0:T(8,128)} fusion(bf16[160,1024]{1,0:T(8,128)(2,1)} %get-tuple-element.7), kind=kLoop, calls=%fused_computation | loop fusion | flops 156672 | bytes 940032 | tf_op jit(solution)/shard_map/convert_element_type | solution.py:723
  93.7 0.0 copy-done.1
  93.7 0.6 copy.15
  94.3 0.0 copy-done
  94.3 0.7 copy.16
Async XLA Ops:
  91.7 1.9 %copy-start.1 = (f32[8,768]{1,0:T(8,128)S(1)}, f32[8,768]{1,0:T(8,128)}, u32[]{:S(2)}) copy-start(f32[8,768]{1,0:T(8,128)} %get-tuple-element.12) | copy-start | bytes 73732
  91.7 2.5 %copy-start = (bf16[256,256]{1,0:T(8,128)(2,1)S(1)}, bf16[256,256]{1,0:T(8,128)(2,1)}, u32[]{:S(2)}) copy-start(bf16[256,256]{1,0:T(8,128)(2,1)} %get-tuple-element.14) | copy-start | bytes 393220
